TPU v7x, 32 devices: a whole 2x2x4 slice. The times are simulated.
32 devices in a mesh: dom: 8 (over y, x, core), pair: 4 (over z).
Axes of the slice: x: 2, y: 2, z: 4, core: 2. Of those that a mesh axis runs over, the one named last changes fastest.
Arguments:
- occupied: bfloat16 [12, 32, 256, 128], P(None, 'dom'), may hold values from -6 to 6
- virtual: bfloat16 [12, 32, 256, 128], P(None, 'dom'), may hold values from -6 to 6
- pair_ids: int32 [16, 2], P('pair'), may hold values from 0 to 11
Outputs:
- potentials: bfloat16 [16, 32, 256, 128], P('pair', 'dom')
- panel: float32 [16, 16], P('dom', 'pair')
Inputs may be any that keep to these rules, and one draw needn't show every extreme that they name: `pair_ids`: each row holds an occupied orbital's index and a virtual orbital's index.
All inputs are finite; a program needn't handle non-finite values.
Results may differ from a plain program's by a relative error of at most 0.001.
Values may be sent and summed in bfloat16 or wider, within the bound.
No kernel may reach another device: no remote copies, remote signals or barrier semaphores. Data moves between devices by JAX's collectives and lax.ppermute only.
A program may use at most 128 MiB of HBM per device.

v0:
```python
import math

import jax
import jax.numpy as jnp
from jax import lax
from jax.sharding import PartitionSpec as P

relax_step = 0.8 / 6.0
highest = lax.Precision.HIGHEST


def padded_2(block, sides, width):
    for axis, dim in sides:
        count = lax.axis_size(axis)
        forward = [(i, i + 1) for i in range(count - 1)]
        backward = [(target, source) for source, target in forward]
        low = lax.ppermute(
            lax.slice_in_dim(block, block.shape[dim] - width, None, axis=dim), axis, forward
        )
        high = lax.ppermute(lax.slice_in_dim(block, 0, width, axis=dim), axis, backward)
        block = jnp.concatenate([low, block, high], axis=dim)
    return block


def apply_operator(padded):
    middle = padded[:, 1:-1]
    zero_y = jnp.zeros_like(middle[:, :, :1])
    zero_z = jnp.zeros_like(middle[:, :, :, :1])
    beside = padded[:, 2:] + padded[:, :-2]
    beside = (
        beside
        + jnp.concatenate([middle[:, :, 1:], zero_y], 2)
        + jnp.concatenate([zero_y, middle[:, :, :-1]], 2)
    )
    beside = (
        beside
        + jnp.concatenate([middle[:, :, :, 1:], zero_z], 3)
        + jnp.concatenate([zero_z, middle[:, :, :, :-1]], 3)
    )
    return 6.0 * middle - beside


def rim_of(field):
    return padded_2(field, (("dom", 1),), 1)


def sweep_single(field, source):
    return field + relax_step * (source - apply_operator(rim_of(field)))


def presmooth(source):
    field = sweep_single(relax_step * source, source)
    residual = source - apply_operator(rim_of(field))
    return (field, residual, source)


def postsmooth(field, source):
    return sweep_single(sweep_single(field, source), source)


def restrict(field):
    count, sx, sy, sz = field.shape
    half_z = field[:, :, :, 0::2] + field[:, :, :, 1::2]
    folded = half_z.reshape(count, sx // 2, 2, sy // 2, sz)
    half_y = folded[:, :, :, :, : sz // 2] + folded[:, :, :, :, sz // 2 :]
    return 0.5 * (half_y[:, :, 0] + half_y[:, :, 1])


def prolong(field):
    count, sx, sy, sz = field.shape
    columns = jnp.arange(2 * sz, dtype=jnp.int32) // 2
    spread_table = (jnp.arange(sz, dtype=jnp.int32)[:, None] == columns[None, :]).astype(
        jnp.float32
    )
    wide_z = jnp.dot(field.reshape(count * sx * sy, sz), spread_table, precision=highest)
    wide_z = wide_z.reshape(count, sx, sy, 2 * sz)
    wide_y = jnp.concatenate([wide_z, wide_z], 3).reshape(count, sx, 2 * sy, 2 * sz)
    spread = jnp.broadcast_to(wide_y[:, :, None], (count, sx, 2, 2 * sy, 2 * sz))
    return spread.reshape(count, 2 * sx, 2 * sy, 2 * sz)


def sine_table(length):
    steps = jnp.arange(length, dtype=jnp.float32) + 1.0
    return math.sqrt(2.0 / (length + 1)) * jnp.sin(
        math.pi * steps[:, None] * steps[None, :] / (length + 1)
    )


def mode_diagonal(length_y, length_z):
    lam_y = 2.0 - 2.0 * jnp.cos(
        math.pi * (jnp.arange(length_y, dtype=jnp.float32) + 1.0) / (length_y + 1)
    )
    lam_z = 2.0 - 2.0 * jnp.cos(
        math.pi * (jnp.arange(length_z, dtype=jnp.float32) + 1.0) / (length_z + 1)
    )
    return (2.0 + lam_y[:, None] + lam_z[None, :]).reshape(length_y * length_z)


def solve_lines(right_side, diagonal):
    systems = jnp.transpose(right_side, (2, 1, 0))
    count = systems.shape[1]
    main = jnp.broadcast_to(diagonal[:, None], systems.shape[:2])
    position = jnp.arange(count, dtype=jnp.int32)
    lower = jnp.broadcast_to(jnp.where(position == 0, 0.0, -1.0).astype(jnp.float32), main.shape)
    upper = jnp.broadcast_to(
        jnp.where(position == count - 1, 0.0, -1.0).astype(jnp.float32), main.shape
    )
    solved = lax.linalg.tridiagonal_solve(lower, main, upper, systems)
    return jnp.transpose(solved, (2, 1, 0))


def coarse_solve(source):
    count, slab_rows, sy, sz = source.shape
    table_y = sine_table(sy)
    table_z = sine_table(sz)
    diagonal = mode_diagonal(sy, sz)
    spectral = jnp.einsum("pxyz,ky,lz->pxkl", source, table_y, table_z, precision=highest)
    spectral = spectral.reshape(count, slab_rows, sy * sz)
    gathered = lax.all_gather(spectral, "dom", axis=1, tiled=True)
    solved_all = solve_lines(gathered, diagonal)
    solved = lax.dynamic_slice_in_dim(solved_all, lax.axis_index("dom") * slab_rows, slab_rows, 1)
    solved = solved.reshape(count, slab_rows, sy, sz)
    return jnp.einsum("pxkl,ky,lz->pxyz", solved, table_y, table_z, precision=highest)


def vcycle(source):
    fine, fine_residual, fine_context = presmooth(source)
    middle_source = restrict(fine_residual)
    middle, middle_residual, middle_context = presmooth(middle_source)
    coarse = coarse_solve(restrict(middle_residual))
    middle = postsmooth(middle + prolong(coarse), middle_source)
    return postsmooth(fine + prolong(middle), source)


def pick_rows(indices, table):
    matches = (indices[:, None] == jnp.arange(table.shape[0], dtype=jnp.int32)[None, :]).astype(
        jnp.bfloat16
    )
    return jnp.dot(matches, table, preferred_element_type=jnp.float32)


def densities_of(pair_rows, occ_flat, vir_flat):
    return pick_rows(pair_rows[:, 0], occ_flat) * pick_rows(pair_rows[:, 1], vir_flat)


def shards(occupied, virtual, pair_ids):
    orbitals, slab_rows, cross_y, cross_z = occupied.shape
    slab_cells = slab_rows * cross_y * cross_z
    occ_flat = occupied.reshape(orbitals, slab_cells)
    vir_flat = virtual.reshape(orbitals, slab_cells)
    own_pairs = pair_ids.shape[0]
    density = densities_of(pair_ids, occ_flat, vir_flat)
    field = vcycle(density.reshape(own_pairs, slab_rows, cross_y, cross_z))
    potentials = field.astype(jnp.bfloat16)
    pot_flat = potentials.reshape(own_pairs, slab_cells)
    partial_value = lax.dot_general(
        lax.all_gather(density.astype(jnp.bfloat16), "pair", axis=0, tiled=True),
        pot_flat,
        (((1,), (1,)), ((), ())),
        preferred_element_type=jnp.float32,
    )
    summed = lax.psum_scatter(partial_value, "dom", scatter_dimension=0, tiled=True)
    panel = summed / float(slab_cells * lax.axis_size("dom"))
    return (potentials, panel)


def solution(mesh):
    placed = (P(None, "dom", None, None), P(None, "dom", None, None), P("pair", None))
    return jax.shard_map(
        shards,
        mesh=mesh,
        in_specs=placed,
        out_specs=(P("pair", "dom", None, None), P("dom", "pair")),
        check_vma=False,
    )
```

profile of v0, /device:TPU:0, one launch (start us, length us, event | category | flops | bytes accessed | tf_op | source)
XLA Modules:
  0.0 307.2 jit_solution(11963998840334858303)
XLA Ops:
  8.0 2.4 pad.102
  10.3 2.7 copy.27
  13.5 2.7 copy.28
  17.0 1.1 convolution_multiply_fusion
  18.5 1.1 copy-done.1
  19.6 1.2 fusion.153
  20.8 1.3 collective-permute-start
  22.0 3.1 collective-permute-start.1
  25.1 1.3 convert_bitcast_fusion
  26.5 2.3 fusion.151
  30.4 3.2 %broadcast_divide_fusion.4 = (f32[2048]{0:T(1024)S(1)}, f32[2048]{0:T(1024)S(1)}) fusion(f32[]{:T(128)} %bitcast.22, f32[2048]{0:T(1024)S(1)} %add.768, f32[]{:T(128)} %bitcast.15, f32[]{:T(128)} %bitcast.18, f32[]{:T(128)} %bitcast.19, f32[]{:T(128)} %bitcast.21), kind=kLoop, calls=%fused_computation.200 | loop fusion | flops 14336 | bytes 24596 | tf_op jit(solution)/shard_map/vmap()/eval_jaxpr/div | solution.py:108
  33.6 3.2 %broadcast_divide_fusion.2 = (f32[2048]{0:T(1024)S(1)}, f32[2048]{0:T(1024)S(1)}, f32[2048]{0:T(1024)S(1)}) fusion(f32[]{:T(128)} %bitcast.28, f32[2048]{0:T(1024)S(1)} %add.768, f32[]{:T(128)} %bitcast.25, f32[]{:T(128)} %bitcast.27, f32[2048]{0:T(1024)S(1)} %get-tuple-element.9, f32[]{:T(128)} %bitcast.22, f32[]{:T(128)} %bitcast.24), kind=kLoop, calls=%fused_computation.198 | loop fusion | flops 14336 | bytes 40980 | tf_op jit(solution)/shard_map/vmap()/eval_jaxpr/div | solution.py:108
  36.9 6.4 %multiply_subtract_fusion.6 = (f32[2048]{0:T(1024)S(1)}, f32[2048]{0:T(1024)S(1)}, f32[2048]{0:T(1024)S(1)}, f32[2048]{0:T(1024)S(1)}, f32[2048]{0:T(1024)S(1)}, /*index=5*/f32[2048]{0:T(1024)S(1)}, f32[2048]{0:T(1024)S(1)}) fusion(f32[2048]{0:T(1024)S(1)} %add.768, f32[]{:T(128)} %bitcast.36, f32[]{:T(128)} %bitcast.34, f32[]{:T(128)} %bitcast.31, ...), kind=kLoop, calls=%fused_computation.181 | loop fusion | flops 28672 | bytes 81960 | tf_op jit(solution)/shard_map/vmap()/eval_jaxpr/sub | solution.py:108
  48.7 3.6 %fusion.34 = f32[4,4,256,128]{3,2,1,0:T(8,128)S(1)} fusion(f32[4,4,256,128]{3,2,1,0:T(8,128)} %copy-done, f32[4,4,256,128]{3,2,1,0:T(8,128)S(1)} %bitcast.187, f32[4,1,256,128]{3,2,1,0:T(8,128)S(1)} %collective-permute-done.1, f32[4,1,256,128]{3,2,1,0:T(8,128)S(1)} %collective-permute-done, f32[4,4,256,127]{3,2,1,0:T(8,128)S(1)} %get-tuple-element.39, ...), kind=kLoop, calls=%fused_computation.42 | loop fusion | flops 6291456 | bytes 15679488 | tf_op jit(solution)/shard_map/add | solution.py:48
  52.4 1.3 collective-permute-start.2
  53.7 5.3 %collective-permute-start.3 = (f32[4,1,256,128]{3,2,1,0:T(8,128)S(1)}, f32[4,1,256,128]{3,2,1,0:T(8,128)S(1)}, u32[]{:S(2)}, u32[]{:S(2)}) collective-permute-start(f32[4,1,256,128]{3,2,1,0:T(8,128)S(1)} %get-tuple-element.35), channel_id=1, source_target_pairs={{0,4},{4,8},{8,12},{12,16},{16,20},{20,24},{24,28},{1,5},{5,9},{9,... | collective-permute-start | bytes 1572872 | tf_op jit(solution)/shard_map/ppermute | solution.py:17
  60.3 3.0 fusion.25
  63.3 36.9 %slice.394 = f32[4,4,256,64]{3,2,1,0:T(8,128)} slice(f32[4,4,256,128]{3,2,1,0:T(8,128)} %fusion.25), slice={[0:4:1], [0:4:1], [0:256:1], [0:128:2]} | slice | bytes 2097152 | tf_op jit(solution)/shard_map/slice | solution.py:63
  100.2 37.4 %slice.395 = f32[4,4,256,64]{3,2,1,0:T(8,128)} slice(f32[4,4,256,128]{3,2,1,0:T(8,128)} %fusion.25), slice={[0:4:1], [0:4:1], [0:256:1], [1:128:2]} | slice | bytes 2097152 | tf_op jit(solution)/shard_map/slice | solution.py:63
  137.6 3.9 %add.744 = f32[4,4,256,64]{3,2,1,0:T(8,128)} add(f32[4,4,256,64]{3,2,1,0:T(8,128)} %slice.394, f32[4,4,256,64]{3,2,1,0:T(8,128)} %slice.395) | non-fusion elementwise | flops 262144 | bytes 3145728 | tf_op jit(solution)/shard_map/add | solution.py:63
  141.5 1.8 reshape.1289
  143.9 1.3 collective-permute-start.4
  145.2 9.1 %collective-permute-start.5 = (f32[4,1,128,64]{3,2,1,0:T(8,128)S(1)}, f32[4,1,128,64]{3,2,1,0:T(8,128)S(1)}, u32[]{:S(2)}, u32[]{:S(2)}) collective-permute-start(f32[4,1,128,64]{3,2,1,0:T(8,128)S(1)} %get-tuple-element.65), channel_id=1, source_target_pairs={{0,4},{4,8},{8,12},{12,16},{16,20},{20,24},{24,28},{1,5},{5,9},{9,... | collective-permute-start | bytes 393224 | tf_op jit(solution)/shard_map/ppermute | solution.py:17
  155.9 1.3 collective-permute-start.6
  157.2 7.0 %collective-permute-start.7 = (f32[4,1,128,64]{3,2,1,0:T(8,128)S(1)}, f32[4,1,128,64]{3,2,1,0:T(8,128)S(1)}, u32[]{:S(2)}, u32[]{:S(2)}) collective-permute-start(f32[4,1,128,64]{3,2,1,0:T(8,128)S(1)} %get-tuple-element.59), channel_id=1, source_target_pairs={{0,4},{4,8},{8,12},{12,16},{16,20},{20,24},{24,28},{1,5},{5,9},{9,... | collective-permute-start | bytes 393224 | tf_op jit(solution)/shard_map/ppermute | solution.py:17
  165.4 1.2 fusion.66
  166.6 6.0 %slice.416 = f32[4,2,128,32]{3,2,1,0:T(8,128)} slice(f32[4,2,128,64]{3,2,1,0:T(8,128)} %fusion.66), slice={[0:4:1], [0:2:1], [0:128:1], [0:64:2]} | slice | bytes 262144 | tf_op jit(solution)/shard_map/slice | solution.py:63
  172.6 6.2 %slice.417 = f32[4,2,128,32]{3,2,1,0:T(8,128)} slice(f32[4,2,128,64]{3,2,1,0:T(8,128)} %fusion.66), slice={[0:4:1], [0:2:1], [0:128:1], [1:64:2]} | slice | bytes 262144 | tf_op jit(solution)/shard_map/slice | solution.py:63
  178.8 2.0 add.759
  180.9 1.2 reshape.1290
  183.3 23.6 %all_gather.6 = f32[4,8,2048]{2,0,1:T(4,128)S(1)} all-gather(f32[4,1,2048]{2,0,1:T(4,128)S(1)} %reshape.1291), channel_id=1, replica_groups=mesh['dom'=8,'pair'=4] {'dom'}, dimensions={1}, use_global_device_ids=true | all-gather | bytes 294912 | tf_op jit(solution)/shard_map/all_gather | solution.py:119
  206.9 4.7 %subtract_dynamic-update-slice_fusion = (f32[7,2048,4]{1,2,0:T(4,128)S(1)}, f32[1,2048,4]{1,2,0:T(4,128)S(1)}, f32[1,2048,4]{1,2,0:T(4,128)S(1)}, f32[1,2048,4]{...) fusion(f32[2048]{0:T(1024)S(1)} %get-tuple-element.67, f32[2048]{0:T(1024)S(1)} %get-tuple-element.8, ...), kind=kLoop, calls=%fused_computation.140 | loop fusion | flops 278527 | bytes 573468
  211.6 4.7 %multiply_subtract_fusion.5 = f32[2048,1,4]{0,2,1:T(4,128)S(1)} fusion(f32[7,2048,4]{1,2,0:T(4,128)S(1)} %slice_bitcast_fusion, f32[2048,8,4]{0,2,1:T(4,128)S(1)} %bitcast.201, f32[2048]{0:T(1024)S(1)} %get-tuple-element.13, f32[]{:T(128)} %bitcast.36, f32[2048]{0:T(1024)S(1)} %broadcast_divide_fusion, f32[2048]{0:T(1024)S(1)} %get-tuple-element.14, ...), kind=kLoop, calls=%fused_computation.152 | loop fusion | flops 294912 | bytes 417820 | tf_op jit(solution)/shard_map/vmap()/eval_jaxpr/sub | solution.py:108
  219.4 1.3 collective-permute-start.8
  220.7 3.0 collective-permute-start.9
  225.4 1.3 collective-permute-start.10
  226.7 6.3 %collective-permute-start.11 = (f32[4,1,128,64]{3,2,1,0:T(8,128)S(1)}, f32[4,1,128,64]{3,2,1,0:T(8,128)S(1)}, u32[]{:S(2)}, u32[]{:S(2)}) collective-permute-start(f32[4,1,128,64]{3,2,1,0:T(8,128)S(1)} %get-tuple-element.47), channel_id=1, source_target_pairs={{0,4},{4,8},{8,12},{12,16},{16,20},{20,24},{24,28},{1,5},{5,9},{9,... | collective-permute-start | bytes 393224 | tf_op jit(solution)/shard_map/ppermute | solution.py:17
  235.0 1.3 copy.22
  236.3 1.3 broadcast_in_dim.22
  238.1 1.3 collective-permute-start.12
  239.4 7.2 %collective-permute-start.13 = (f32[4,1,256,128]{3,2,1,0:T(8,128)S(1)}, f32[4,1,256,128]{3,2,1,0:T(8,128)S(1)}, u32[]{:S(2)}, u32[]{:S(2)}) collective-permute-start(f32[4,1,256,128]{3,2,1,0:T(8,128)S(1)} %get-tuple-element.29), channel_id=1, source_target_pairs={{0,4},{4,8},{8,12},{12,16},{16,20},{20,24},{24,28},{1,5},{5,9},{9,... | collective-permute-start | bytes 1572872 | tf_op jit(solution)/shard_map/ppermute | solution.py:17
  248.7 1.7 fusion.18
  250.5 1.3 collective-permute-start.14
  251.8 9.1 %collective-permute-start.15 = (f32[4,1,256,128]{3,2,1,0:T(8,128)S(1)}, f32[4,1,256,128]{3,2,1,0:T(8,128)S(1)}, u32[]{:S(2)}, u32[]{:S(2)}) collective-permute-start(f32[4,1,256,128]{3,2,1,0:T(8,128)S(1)} %get-tuple-element.23), channel_id=1, source_target_pairs={{0,4},{4,8},{8,12},{12,16},{16,20},{20,24},{24,28},{1,5},{5,9},{9,... | collective-permute-start | bytes 1572872 | tf_op jit(solution)/shard_map/ppermute | solution.py:17
  262.4 1.8 fusion.9
  264.3 4.5 %reshape.1298 = bf16[16,131072]{1,0:T(8,128)(2,1)} reshape(bf16[4,4,131072]{2,1,0:T(4,128)(2,1)} %all-gather.3.cloned.1.call-done) | data formatting | bytes 8388608
  268.8 4.4 %fusion.35 = f32[16,4]{1,0:T(8,128)S(1)} fusion(bf16[16,131072]{1,0:T(8,128)(2,1)} %reshape.1298, bf16[1,4,1024,128]{3,2,1,0:T(8,128)(2,1)S(1)} %bitcast.202), kind=kOutput, calls=%fused_computation.47 | convolution fusion | flops 16777216 | bytes 5243136 | tf_op jit(solution)/shard_map/dot_general | solution.py:156
  273.2 26.6 %all-reduce.32 = f32[16,4]{1,0:T(8,128)S(1)} all-reduce(f32[16,4]{1,0:T(8,128)S(1)} %fusion.35), channel_id=2, replica_groups=mesh['dom'=8,'pair'=4] {'dom'}, use_global_device_ids=true, to_apply=%region_0.1.clone | all-reduce | flops 64 | bytes 512
  (110 shorter events, 25.9 us)
Async XLA Ops:
  7.2 257.1 %all-gather.3.cloned.1.call-start = ((), (), s32[]{:S(2)}) async-start(), calls=%async_computation | async-start | bytes 5242880 | tf_op jit(solution)/shard_map/all_gather | solution.py:157
  10.3 2.7 copy-start.6
  18.2 1.3 copy-start.1
  19.6 26.2 %copy-start = (f32[4,4,256,128]{3,2,1,0:T(8,128)}, f32[4,4,256,128]{3,2,1,0:T(8,128)S(1)}, u32[]{:S(2)}) copy-start(f32[4,4,256,128]{3,2,1,0:T(8,128)S(1)} %broadcast_multiply_fusion) | copy-start | bytes 6291460
  20.8 25.8 %collective-permute-start = (f32[4,1,256,128]{3,2,1,0:T(8,128)}, f32[4,1,256,128]{3,2,1,0:T(8,128)S(1)}, u32[]{:S(2)}, u32[]{:S(2)}) collective-permute-start(f32[4,1,256,128]{3,2,1,0:T(8,128)} %get-tuple-element.40), channel_id=1, source_target_pairs={{4,0},{8,4},{12,8},{16,12},{20,16},{24,20},{28,24},{5,1},{9,5},{13... | collective-permute-start | bytes 1572872 | tf_op jit(solution)/shard_map/ppermute | solution.py:20
  22.0 24.6 %collective-permute-start.1 = (f32[4,1,256,128]{3,2,1,0:T(8,128)}, f32[4,1,256,128]{3,2,1,0:T(8,128)S(1)}, u32[]{:S(2)}, u32[]{:S(2)}) collective-permute-start(f32[4,1,256,128]{3,2,1,0:T(8,128)} %get-tuple-element.41), channel_id=1, source_target_pairs={{0,4},{4,8},{8,12},{12,16},{16,20},{20,24},{24,28},{1,5},{5,9},{9,... | collective-permute-start | bytes 1572872 | tf_op jit(solution)/shard_map/ppermute | solution.py:17
  26.5 18.1 %copy-start.8 = (u32[32]{0:T(128)S(1)}, u32[32]{0:T(128)}, u32[]{:S(2)}) copy-start(u32[32]{0:T(128)} %constant.165) | copy-start | bytes 388
  45.8 1.6 copy-start.2
  45.8 2.2 copy-start.4
  45.8 2.9 copy-start.5
  52.4 7.8 %collective-permute-start.2 = (f32[4,1,256,128]{3,2,1,0:T(8,128)S(1)}, f32[4,1,256,128]{3,2,1,0:T(8,128)S(1)}, u32[]{:S(2)}, u32[]{:S(2)}) collective-permute-start(f32[4,1,256,128]{3,2,1,0:T(8,128)S(1)} %get-tuple-element.34), channel_id=1, source_target_pairs={{4,0},{8,4},{12,8},{16,12},{20,16},{24,20},{28,24},{5,1},{9,5},{13... | collective-permute-start | bytes 1572872 | tf_op jit(solution)/shard_map/ppermute | solution.py:20
  53.7 6.6 %collective-permute-start.3 = (f32[4,1,256,128]{3,2,1,0:T(8,128)S(1)}, f32[4,1,256,128]{3,2,1,0:T(8,128)S(1)}, u32[]{:S(2)}, u32[]{:S(2)}) collective-permute-start(f32[4,1,256,128]{3,2,1,0:T(8,128)S(1)} %get-tuple-element.35), channel_id=1, source_target_pairs={{0,4},{4,8},{8,12},{12,16},{16,20},{20,24},{24,28},{1,5},{5,9},{9,... | collective-permute-start | bytes 1572872 | tf_op jit(solution)/shard_map/ppermute | solution.py:17
  143.9 10.6 %collective-permute-start.4 = (f32[4,1,128,64]{3,2,1,0:T(8,128)S(1)}, f32[4,1,128,64]{3,2,1,0:T(8,128)S(1)}, u32[]{:S(2)}, u32[]{:S(2)}) collective-permute-start(f32[4,1,128,64]{3,2,1,0:T(8,128)S(1)} %get-tuple-element.64), channel_id=1, source_target_pairs={{4,0},{8,4},{12,8},{16,12},{20,16},{24,20},{28,24},{5,1},{9,5},{13... | collective-permute-start | bytes 393224 | tf_op jit(solution)/shard_map/ppermute | solution.py:20
  145.2 10.2 %collective-permute-start.5 = (f32[4,1,128,64]{3,2,1,0:T(8,128)S(1)}, f32[4,1,128,64]{3,2,1,0:T(8,128)S(1)}, u32[]{:S(2)}, u32[]{:S(2)}) collective-permute-start(f32[4,1,128,64]{3,2,1,0:T(8,128)S(1)} %get-tuple-element.65), channel_id=1, source_target_pairs={{0,4},{4,8},{8,12},{12,16},{16,20},{20,24},{24,28},{1,5},{5,9},{9,... | collective-permute-start | bytes 393224 | tf_op jit(solution)/shard_map/ppermute | solution.py:17
  155.9 8.5 %collective-permute-start.6 = (f32[4,1,128,64]{3,2,1,0:T(8,128)S(1)}, f32[4,1,128,64]{3,2,1,0:T(8,128)S(1)}, u32[]{:S(2)}, u32[]{:S(2)}) collective-permute-start(f32[4,1,128,64]{3,2,1,0:T(8,128)S(1)} %get-tuple-element.58), channel_id=1, source_target_pairs={{4,0},{8,4},{12,8},{16,12},{20,16},{24,20},{28,24},{5,1},{9,5},{13... | collective-permute-start | bytes 393224 | tf_op jit(solution)/shard_map/ppermute | solution.py:20
  157.2 8.1 %collective-permute-start.7 = (f32[4,1,128,64]{3,2,1,0:T(8,128)S(1)}, f32[4,1,128,64]{3,2,1,0:T(8,128)S(1)}, u32[]{:S(2)}, u32[]{:S(2)}) collective-permute-start(f32[4,1,128,64]{3,2,1,0:T(8,128)S(1)} %get-tuple-element.59), channel_id=1, source_target_pairs={{0,4},{4,8},{8,12},{12,16},{16,20},{20,24},{24,28},{1,5},{5,9},{9,... | collective-permute-start | bytes 393224 | tf_op jit(solution)/shard_map/ppermute | solution.py:17
  219.4 4.6 %collective-permute-start.8 = (f32[4,1,128,64]{3,2,1,0:T(8,128)S(1)}, f32[4,1,128,64]{3,2,1,0:T(8,128)S(1)}, u32[]{:S(2)}, u32[]{:S(2)}) collective-permute-start(f32[4,1,128,64]{3,2,1,0:T(8,128)S(1)} %get-tuple-element.52), channel_id=1, source_target_pairs={{4,0},{8,4},{12,8},{16,12},{20,16},{24,20},{28,24},{5,1},{9,5},{13... | collective-permute-start | bytes 393224 | tf_op jit(solution)/shard_map/ppermute | solution.py:20
  220.7 4.2 %collective-permute-start.9 = (f32[4,1,128,64]{3,2,1,0:T(8,128)S(1)}, f32[4,1,128,64]{3,2,1,0:T(8,128)S(1)}, u32[]{:S(2)}, u32[]{:S(2)}) collective-permute-start(f32[4,1,128,64]{3,2,1,0:T(8,128)S(1)} %get-tuple-element.53), channel_id=1, source_target_pairs={{0,4},{4,8},{8,12},{12,16},{16,20},{20,24},{24,28},{1,5},{5,9},{9,... | collective-permute-start | bytes 393224 | tf_op jit(solution)/shard_map/ppermute | solution.py:17
  225.4 7.9 %collective-permute-start.10 = (f32[4,1,128,64]{3,2,1,0:T(8,128)S(1)}, f32[4,1,128,64]{3,2,1,0:T(8,128)S(1)}, u32[]{:S(2)}, u32[]{:S(2)}) collective-permute-start(f32[4,1,128,64]{3,2,1,0:T(8,128)S(1)} %get-tuple-element.46), channel_id=1, source_target_pairs={{4,0},{8,4},{12,8},{16,12},{20,16},{24,20},{28,24},{5,1},{9,5},{13... | collective-permute-start | bytes 393224 | tf_op jit(solution)/shard_map/ppermute | solution.py:20
  226.7 7.4 %collective-permute-start.11 = (f32[4,1,128,64]{3,2,1,0:T(8,128)S(1)}, f32[4,1,128,64]{3,2,1,0:T(8,128)S(1)}, u32[]{:S(2)}, u32[]{:S(2)}) collective-permute-start(f32[4,1,128,64]{3,2,1,0:T(8,128)S(1)} %get-tuple-element.47), channel_id=1, source_target_pairs={{0,4},{4,8},{8,12},{12,16},{16,20},{20,24},{24,28},{1,5},{5,9},{9,... | collective-permute-start | bytes 393224 | tf_op jit(solution)/shard_map/ppermute | solution.py:17
  238.1 9.7 %collective-permute-start.12 = (f32[4,1,256,128]{3,2,1,0:T(8,128)S(1)}, f32[4,1,256,128]{3,2,1,0:T(8,128)S(1)}, u32[]{:S(2)}, u32[]{:S(2)}) collective-permute-start(f32[4,1,256,128]{3,2,1,0:T(8,128)S(1)} %get-tuple-element.28), channel_id=1, source_target_pairs={{4,0},{8,4},{12,8},{16,12},{20,16},{24,20},{28,24},{5,1},{9,5},{13... | collective-permute-start | bytes 1572872 | tf_op jit(solution)/shard_map/ppermute | solution.py:20
  239.4 8.7 %collective-permute-start.13 = (f32[4,1,256,128]{3,2,1,0:T(8,128)S(1)}, f32[4,1,256,128]{3,2,1,0:T(8,128)S(1)}, u32[]{:S(2)}, u32[]{:S(2)}) collective-permute-start(f32[4,1,256,128]{3,2,1,0:T(8,128)S(1)} %get-tuple-element.29), channel_id=1, source_target_pairs={{0,4},{4,8},{8,12},{12,16},{16,20},{20,24},{24,28},{1,5},{5,9},{9,... | collective-permute-start | bytes 1572872 | tf_op jit(solution)/shard_map/ppermute | solution.py:17
  247.1 1.6 copy-start.3
  250.5 11.6 %collective-permute-start.14 = (f32[4,1,256,128]{3,2,1,0:T(8,128)S(1)}, f32[4,1,256,128]{3,2,1,0:T(8,128)S(1)}, u32[]{:S(2)}, u32[]{:S(2)}) collective-permute-start(f32[4,1,256,128]{3,2,1,0:T(8,128)S(1)} %get-tuple-element.22), channel_id=1, source_target_pairs={{4,0},{8,4},{12,8},{16,12},{20,16},{24,20},{28,24},{5,1},{9,5},{13... | collective-permute-start | bytes 1572872 | tf_op jit(solution)/shard_map/ppermute | solution.py:20
  251.8 10.6 %collective-permute-start.15 = (f32[4,1,256,128]{3,2,1,0:T(8,128)S(1)}, f32[4,1,256,128]{3,2,1,0:T(8,128)S(1)}, u32[]{:S(2)}, u32[]{:S(2)}) collective-permute-start(f32[4,1,256,128]{3,2,1,0:T(8,128)S(1)} %get-tuple-element.23), channel_id=1, source_target_pairs={{0,4},{4,8},{8,12},{12,16},{16,20},{20,24},{24,28},{1,5},{5,9},{9,... | collective-permute-start | bytes 1572872 | tf_op jit(solution)/shard_map/ppermute | solution.py:17
  264.2 4.5 %copy-start.7 = (bf16[4,4,256,128]{3,2,1,0:T(8,128)(2,1)}, bf16[4,4,256,128]{3,2,1,0:T(8,128)(2,1)S(1)}, u32[]{:S(2)}) copy-start(bf16[4,4,256,128]{3,2,1,0:T(8,128)(2,1)S(1)} %fusion.9) | copy-start | bytes 3145732
Sparse Core Ops, SparseCore 0:
  26.6 84.0 all-gather.2
where the time goes:
time: 308 us; the launch traced here: 307 us
  local copies, waits for them, and re-layouts  121 us (39%)
  starting transfers between devices  60.4 us (20%)
  blocking collectives  50.1 us (16%)
  other arithmetic  46.6 us (15%)
  between operations  15.5 us (5%)
  matrix products  8.89 us (3%)
  waiting for transfers between devices  4.24 us (1%)
    slice x4, local copies, waits for them, and re-layouts, restrict(): half_z = field[:, :, :, 0::2] + field[:, :, :, 1::2]  86.5 us
    ppermute x8, starting transfers between devices, padded_2(): lax.ppermute(lax.slice_in_dim(block, block.shape[dim] - width, None, axis...  50 us
    unnamed x1, blocking collectives  26.6 us
    all_gather x1, blocking collectives, coarse_solve(): gathered = lax.all_gather(spectral, 'dom', axis=1, tiled=True)  23.6 us
    unnamed x27, local copies, waits for them, and re-layouts  17.2 us
    sub x2, other arithmetic, solve_lines(): solved = lax.linalg.tridiagonal_solve(lower, main, upper, systems)  11.1 us
    ppermute x8, starting transfers between devices, padded_2(): lax.ppermute(lax.slice_in_dim(block, 0, width, axis=dim), axis, backward)  10.3 us
    div x4, other arithmetic, solve_lines(): solved = lax.linalg.tridiagonal_solve(lower, main, upper, systems)  7.63 us
  transfers between devices with their start and end apart: 17, of which 7 were waited for; matrix products, arithmetic and copies ran while one was open for 49% of the time, Pallas kernels for 0%

commit v1 on v0

v1 whole, which is shorter than its diff:
```python
import functools
import math

import jax
import jax.numpy as jnp
import numpy as np
from jax import lax
from jax.experimental import pallas as pl
from jax.experimental.pallas import tpu as pltpu
from jax.sharding import PartitionSpec as P

W = 0.8 / 6.0
C = 0.2
PAD = 8
F32 = jnp.float32
BF16 = jnp.bfloat16


def dot(a, b, contract=((1,), (0,)), precision=None):
    return lax.dot_general(a, b, (contract, ((), ())), precision=precision, preferred_element_type=F32)


def high_low(x):
    high = x.astype(BF16)
    return high, (x - high.astype(F32)).astype(BF16)


def zero_rims(ref):
    zeros = jnp.zeros((ref.shape[0], PAD, ref.shape[2]), F32)
    ref[:, :PAD] = zeros
    ref[:, ref.shape[1] - PAD :] = zeros


def read(ref, layer, row, rows):
    return ref[layer, PAD + row : PAD + row + rows, :]


def around(ref, layer, row, rows, centre, blocks=1):
    lane = lax.broadcasted_iota(jnp.int32, centre.shape, 1)
    width = centre.shape[1] // blocks
    first = lane % width == 0 if blocks > 1 else lane == 0
    last = lane % width == width - 1 if blocks > 1 else lane == width - 1
    total = read(ref, layer, row - 1, rows) + read(ref, layer, row + 1, rows)
    total = total + jnp.where(first, 0.0, pltpu.roll(centre, 1, 1))
    return total + jnp.where(last, 0.0, pltpu.roll(centre, centre.shape[1] - 1, 1))


def source_kernel(ids, place, occ, vir, fold, shares, first, second, v0_out, field, once, sums):
    slab, rows_y, _ = occ.shape[1:]
    step = 64
    in_left = jnp.where(place[0] == 0, 0.0, 1.0)
    in_right = jnp.where(place[1] == 0, 0.0, 1.0)
    even = place[2] == 0
    zero_rims(field)
    zero_rims(once)
    for layer in range(slab):
        field[layer, PAD : PAD + rows_y] = occ[0, layer].astype(F32) * vir[0, layer].astype(F32)

    def pack_out(edge, index, row, value):
        rows = slice(row, row + step)
        value = value.astype(BF16)

        @pl.when(even == (edge == 1))
        def _():
            first[0, index, rows] = value

        @pl.when(even != (edge == 1))
        def _():
            second[0, index, rows] = value

    for row in range(0, rows_y, step):
        for layer in range(slab):
            centre = read(field, layer, row, step)
            total = around(field, layer, row, step, centre)
            if layer > 0:
                total = total + read(field, layer - 1, row, step)
            if layer < slab - 1:
                total = total + read(field, layer + 1, row, step)
            value = C * centre + W * total
            once[layer + 1, PAD + row : PAD + row + step] = value
            v0 = W * (centre + value)
            v0_out[0, layer, row : row + step] = v0
            if layer == 0:
                once[0, PAD + row : PAD + row + step] = (W * in_left) * centre
                pack_out(0, 0, row, centre)
                pack_out(0, 1, row, v0)
            if layer == 1:
                pack_out(0, 2, row, v0)
            if layer == slab - 2:
                pack_out(1, 2, row, v0)
            if layer == slab - 1:
                once[slab + 1, PAD + row : PAD + row + step] = (W * in_right) * centre
                pack_out(1, 0, row, centre)
                pack_out(1, 1, row, v0)

    def twice(layer, row):
        if layer == -2:
            return W * read(once, 0, row, step)
        if layer == slab + 1:
            return W * read(once, slab + 1, row, step)
        at = layer + 1
        centre = read(once, at, row, step)
        total = around(once, at, row, step, centre)
        if at > 0:
            total = total + read(once, at - 1, row, step)
        if at < slab + 1:
            total = total + read(once, at + 1, row, step)
        return C * centre + W * total

    for row in range(0, rows_y, step):
        for coarse in range(slab // 2 + 2):
            pair_sum = twice(2 * coarse - 2, row) + twice(2 * coarse - 1, row)
            sums[coarse, row : row + step] = pair_sum

    def folded(coarse):
        half = rows_y // 2
        return sums[coarse, pl.ds(0, half, stride=2), :] + sums[coarse, pl.ds(1, half, stride=2), :]

    def together(left, right):
        both = jnp.concatenate([folded(left), folded(right)], axis=1)
        high, low = high_low(both)
        return dot(high, fold[...]) + dot(low, fold[...])

    own_high, own_low = high_low(together(1, 2))
    edge = together(3, 0).astype(BF16)
    parts, part_rows = shares.shape[1], shares.shape[3]
    for part in range(parts):
        rows = slice(part * part_rows, (part + 1) * part_rows)
        shares[0, part, 0] = own_high[rows]
        shares[0, part, 1] = own_low[rows]
        shares[0, part, 2] = edge[rows]


def middle_kernel(place, *refs):
    parts = (len(refs) - 10)
    received = refs[:parts]
    modes, table_y, inverse, back, out, source, field_a, field_b, smooth, edge = refs[parts:]
    slabs, _, part_rows, lanes = received[0].shape
    rows_y = parts * part_rows
    own_part = place[3]
    left = lax.broadcasted_iota(jnp.int32, (part_rows, lanes), 1) < lanes // 2
    for ref in (source, field_a, field_b):
        zero_rims(ref)
    for turn in range(parts):
        at = own_part + turn
        at = jnp.where(at >= parts, at - parts, at) * part_rows
        at = pl.multiple_of(at, part_rows)
        ref = received[turn]
        for d in range(slabs):
            value = ref[d, 0].astype(F32) + ref[d, 1].astype(F32)
            before = ref[d - 1, 2].astype(F32) if d > 0 else jnp.zeros_like(value)
            after = ref[d + 1, 2].astype(F32) if d < slabs - 1 else jnp.zeros_like(value)
            source[d, pl.ds(PAD + at, part_rows)] = value + jnp.where(left, before, after)

    half = lanes // 2
    left = lax.broadcasted_iota(jnp.int32, (rows_y, lanes), 1) < half

    def swapped(ref, d):
        return pltpu.roll(read(ref, d, 0, rows_y), half, 1)

    def apply(ref, each):
        zeros = jnp.zeros((rows_y, lanes), F32)
        before, here = zeros, swapped(ref, 0)
        for d in range(slabs):
            after = swapped(ref, d + 1) if d < slabs - 1 else zeros
            centre = read(ref, d, 0, rows_y)
            total = around(ref, d, 0, rows_y, centre, 2) + here + jnp.where(left, before, after)
            each(d, C * centre + W * total)
            before, here = here, after

    def write(ref, d, value):
        ref[d, PAD : PAD + rows_y] = value

    apply(source, lambda d, value: write(field_a, d, value))

    def to_coarse(d, value):
        smooth[d] = W * (read(source, d, 0, rows_y) + read(field_a, d, 0, rows_y))
        write(field_b, d, value)

    apply(field_a, to_coarse)
    highest = lax.Precision.HIGHEST
    pieces = []
    for d in range(slabs):
        even_rows = field_b[d, pl.ds(PAD, rows_y // 2, stride=2), :]
        odd_rows = field_b[d, pl.ds(PAD + 1, rows_y // 2, stride=2), :]
        pieces.append(even_rows + odd_rows)
    spectral = dot(jnp.concatenate(pieces, axis=1), modes[...], precision=highest)
    spectral = dot(table_y[...], spectral, precision=highest) * inverse[...]
    spread = dot(dot(table_y[...], spectral, precision=highest), back[...], precision=highest)
    for d in range(slabs):
        value = spread[:, d * lanes : (d + 1) * lanes]
        field_b[d, pl.ds(PAD, rows_y // 2, stride=2), :] = value
        field_b[d, pl.ds(PAD + 1, rows_y // 2, stride=2), :] = value
    for d in range(slabs):
        write(field_a, d, smooth[d] + read(field_b, d, 0, rows_y))

    def add_source(ref):
        return lambda d, value: write(ref, d, value + W * read(source, d, 0, rows_y))

    apply(field_a, add_source(field_b))
    apply(field_b, add_source(field_a))
    zeros = jnp.zeros((rows_y, lanes), F32)
    before, here = zeros, swapped(field_a, 0)
    for d in range(slabs):
        after = swapped(field_a, d + 1) if d < slabs - 1 else zeros
        edge[d] = jnp.where(left, before, after) - read(field_a, d, 0, rows_y)
        before, here = here, after
    at = pl.multiple_of(own_part * part_rows, part_rows)
    for d in range(slabs):
        high, low = high_low(field_a[d, pl.ds(PAD + at, part_rows)])
        out[d, 0] = high
        out[d, 1] = low
        out[d, 2] = edge[d, pl.ds(at, part_rows)].astype(BF16)


def final_kernel(
    own_ids, ids, place, occ, vir, v0, coarse, first, second, spread, all_occ, all_vir,
    out, panel, wide, start, swept, kept, occ_copy, vir_copy, sems,
):
    slab, rows_y, lanes = occ.shape[1:]
    pair, pairs = pl.program_id(0), kept.shape[1]
    step = 64
    in_left = jnp.where(place[0] == 0, 0.0, 1.0)
    in_right = jnp.where(place[1] == 0, 0.0, 1.0)
    even = place[2] == 0
    copies = [
        pltpu.make_async_copy(all_occ, occ_copy, sems.at[0]),
        pltpu.make_async_copy(all_vir, vir_copy, sems.at[1]),
    ]

    @pl.when(pair == 0)
    def _():
        for copy in copies:
            copy.start()

    zero_rims(start)
    zero_rims(swept)
    parts, part_rows = coarse.shape[1], coarse.shape[3]
    for part in range(parts):
        table = spread[...]
        own = dot(coarse[0, part, 0], table) + dot(coarse[0, part, 1], table)
        beyond = own + dot(coarse[0, part, 2], table)
        for at, value in enumerate((beyond[:, :lanes], own[:, :lanes], own[:, lanes:], beyond[:, lanes:])):
            rows = 2 * part * part_rows
            wide[at, pl.ds(rows, part_rows, stride=2), :] = value
            wide[at, pl.ds(rows + 1, part_rows, stride=2), :] = value

    def halo(edge, index, row):
        rows = slice(row, row + step)
        one, two = first[0, index, rows].astype(F32), second[0, index, rows].astype(F32)
        return jnp.where(even == (edge == 1), one, two)

    def density(layer, row):
        rows = slice(row, row + step)
        return occ[0, layer, rows].astype(F32) * vir[0, layer, rows].astype(F32)

    def put(ref, layer, row, value):
        ref[layer, PAD + row : PAD + row + step] = value

    for row in range(0, rows_y, step):
        rows = slice(row, row + step)
        for layer in range(slab):
            value = v0[0, layer, rows] + wide[1 + layer // 2, rows]
            if layer == 0:
                value = value + (W * W) * halo(0, 0, row)
            if layer == slab - 1:
                value = value + (W * W) * halo(1, 0, row)
            put(start, layer + 2, row, value)
        near = halo(0, 1, row) + (W * W) * density(0, row) + wide[0, rows]
        put(start, 1, row, in_left * near)
        put(start, 0, row, in_left * (halo(0, 2, row) + wide[0, rows]))
        near = halo(1, 1, row) + (W * W) * density(slab - 1, row) + wide[3, rows]
        put(start, slab + 2, row, in_right * near)
        put(start, slab + 3, row, in_right * (halo(1, 2, row) + wide[3, rows]))

    def sweep(ref, at, row, source):
        centre = read(ref, at, row, step)
        total = around(ref, at, row, step, centre)
        total = total + read(ref, at - 1, row, step) + read(ref, at + 1, row, step) + source
        return C * centre + W * total

    for row in range(0, rows_y, step):
        put(swept, 0, row, in_left * sweep(start, 1, row, halo(0, 0, row)))
        for layer in range(slab):
            put(swept, layer + 1, row, sweep(start, layer + 2, row, density(layer, row)))
        put(swept, slab + 1, row, in_right * sweep(start, slab + 2, row, halo(1, 0, row)))
    for row in range(0, rows_y, step):
        rows = slice(row, row + step)
        for layer in range(slab):
            value = sweep(swept, layer + 1, row, density(layer, row)).astype(BF16)
            out[0, layer, rows] = value
            kept[layer, pair, rows] = value

    @pl.when(pair == pairs - 1)
    def _():
        for copy in copies:
            copy.wait()
        lane = lax.broadcasted_iota(jnp.int32, (lanes, lanes), 0)
        diagonal = lane == lax.broadcasted_iota(jnp.int32, (lanes, lanes), 1)
        count = ids.shape[0]
        fields = [jnp.concatenate([kept[layer, q] for q in range(pairs)], axis=1) for layer in range(slab)]
        for p in range(count):
            i, a = ids[p, 0], ids[p, 1]
            row = place[4] + p
            row = jnp.where(row >= count, row - count, row)
            product = jnp.zeros((pairs * lanes, lanes), F32)
            for layer in range(slab):
                rho = (occ_copy[i, layer].astype(F32) * vir_copy[a, layer].astype(F32)).astype(BF16)
                product = product + dot(fields[layer], rho, ((0,), (0,)))
            for q in range(pairs):
                block = jnp.where(diagonal, product[q * lanes : (q + 1) * lanes], 0.0)
                panel[row, q : q + 1, :] = jnp.sum(block, axis=0, keepdims=True)


def sine_table(length):
    steps = np.arange(length, dtype=np.float64) + 1.0
    return math.sqrt(2.0 / (length + 1)) * np.sin(np.pi * steps[:, None] * steps[None, :] / (length + 1))


def eigenvalues(length):
    return 2.0 - 2.0 * np.cos(np.pi * (np.arange(length, dtype=np.float64) + 1.0) / (length + 1))


def coarse_tables(size_x, size_y, size_z):
    sine_x, sine_z = sine_table(size_x), sine_table(size_z)
    back = np.einsum("dk,zl->dzkl", sine_x, np.repeat(sine_z, 2, axis=0))
    back = np.repeat(back[:, None], 2, axis=1).reshape(size_x * 4 * size_z, size_x * size_z)
    total = eigenvalues(size_y)[:, None, None] + eigenvalues(size_x)[None, :, None] + eigenvalues(size_z)[None, None, :]
    inverse = (1.0 / total).reshape(size_y, size_x * size_z)
    as_f32 = lambda x: jnp.asarray(np.ascontiguousarray(x), F32)
    return as_f32(0.5 * back), as_f32(sine_table(size_y)), as_f32(inverse), as_f32(back.T)


def shards(occupied, virtual, pair_ids):
    _, slab, rows_y, lanes = occupied.shape
    pairs = pair_ids.shape[0]
    slabs = lax.axis_size("dom")
    me = lax.axis_index("dom")
    parts = slabs // pairs
    half_y = rows_y // 2
    part_rows = half_y // parts
    first_pair = lax.axis_index("pair") * pairs
    place = jnp.stack([me, slabs - 1 - me, me % 2, me % parts, first_pair]).astype(jnp.int32)
    fold = np.zeros((2 * lanes, lanes), np.float32)
    fold[np.arange(2 * lanes), np.arange(2 * lanes) // 2] = 0.5
    spread = (2.0 * fold).T
    by_pair = lambda *tail: (lambda p, *_: (p,) + tail)
    row_of = lambda column: (lambda p, ids, *_: (ids[p, column], 0, 0, 0))
    orbital = (1, slab, rows_y, lanes)

    shares, first, second, v0 = pl.pallas_call(
        source_kernel,
        grid_spec=pltpu.PrefetchScalarGridSpec(
            num_scalar_prefetch=2,
            grid=(pairs,),
            in_specs=[
                pl.BlockSpec(orbital, row_of(0)),
                pl.BlockSpec(orbital, row_of(1)),
                pl.BlockSpec((2 * lanes, lanes), lambda p, *_: (0, 0)),
            ],
            out_specs=[
                pl.BlockSpec((1, parts, 3, part_rows, lanes), by_pair(0, 0, 0, 0)),
                pl.BlockSpec((1, 3, rows_y, lanes), by_pair(0, 0, 0)),
                pl.BlockSpec((1, 3, rows_y, lanes), by_pair(0, 0, 0)),
                pl.BlockSpec(orbital, by_pair(0, 0, 0)),
            ],
            scratch_shapes=[
                pltpu.VMEM((slab, rows_y + 2 * PAD, lanes), F32),
                pltpu.VMEM((slab + 2, rows_y + 2 * PAD, lanes), F32),
                pltpu.VMEM((slab // 2 + 2, rows_y, lanes), F32),
            ],
        ),
        out_shape=[
            jax.ShapeDtypeStruct((pairs, parts, 3, part_rows, lanes), BF16),
            jax.ShapeDtypeStruct((pairs, 3, rows_y, lanes), BF16),
            jax.ShapeDtypeStruct((pairs, 3, rows_y, lanes), BF16),
            jax.ShapeDtypeStruct((pairs, slab, rows_y, lanes), F32),
        ],
        compiler_params=pltpu.CompilerParams(vmem_limit_bytes=60 * 1024 * 1024),
        name="source",
    )(pair_ids, place, occupied, virtual, jnp.asarray(fold, BF16))

    inside = [(i, i ^ 1) for i in range(slabs)]
    across = [(i, i + 1) for i in range(1, slabs - 1, 2)]
    across = across + [(j, i) for i, j in across]
    first_halo = lax.ppermute(first, "dom", inside)
    second_halo = lax.ppermute(second, "dom", across)

    received = lax.all_to_all(shares.reshape(slabs, 3, part_rows, lanes), "dom", 0, 0)
    views = [received]
    for turn in range(1, parts):
        perm = [(g * parts + (h + turn) % parts, g * parts + h) for g in range(slabs // parts) for h in range(parts)]
        views.append(lax.ppermute(received, "dom", perm))
    tables = coarse_tables(slabs, half_y // 2, lanes // 4)
    vmem = pl.BlockSpec(memory_space=pltpu.VMEM)
    padded = (slabs, half_y + 2 * PAD, lanes)
    smoothed = pl.pallas_call(
        middle_kernel,
        in_specs=[pl.BlockSpec(memory_space=pltpu.SMEM)] + [vmem] * (parts + 4),
        out_specs=vmem,
        out_shape=jax.ShapeDtypeStruct((slabs, 3, part_rows, lanes), BF16),
        scratch_shapes=[
            pltpu.VMEM(padded, F32),
            pltpu.VMEM(padded, F32),
            pltpu.VMEM(padded, F32),
            pltpu.VMEM((slabs, half_y, lanes), F32),
            pltpu.VMEM((slabs, half_y, lanes), F32),
        ],
        compiler_params=pltpu.CompilerParams(vmem_limit_bytes=50 * 1024 * 1024),
        name="middle",
    )(place, *views, *tables)
    groups = lax.axis_size("pair")
    ids, smoothed = lax.optimization_barrier((pair_ids, smoothed))
    turns = [[((g + turn) % groups, g) for g in range(groups)] for turn in range(1, groups)]
    all_ids = jnp.concatenate([ids] + [lax.ppermute(ids, "pair", perm) for perm in turns], axis=0)
    returned = lax.all_to_all(smoothed, "dom", 0, 0).reshape(pairs, parts, 3, part_rows, lanes)

    count = all_ids.shape[0]
    potentials, panel = pl.pallas_call(
        final_kernel,
        grid_spec=pltpu.PrefetchScalarGridSpec(
            num_scalar_prefetch=3,
            grid=(pairs,),
            in_specs=[
                pl.BlockSpec(orbital, row_of(0)),
                pl.BlockSpec(orbital, row_of(1)),
                pl.BlockSpec(orbital, by_pair(0, 0, 0)),
                pl.BlockSpec((1, parts, 3, part_rows, lanes), by_pair(0, 0, 0, 0)),
                pl.BlockSpec((1, 3, rows_y, lanes), by_pair(0, 0, 0)),
                pl.BlockSpec((1, 3, rows_y, lanes), by_pair(0, 0, 0)),
                pl.BlockSpec((lanes, 2 * lanes), lambda p, *_: (0, 0)),
                pl.BlockSpec(memory_space=pl.ANY),
                pl.BlockSpec(memory_space=pl.ANY),
            ],
            out_specs=[
                pl.BlockSpec(orbital, by_pair(0, 0, 0)),
                pl.BlockSpec((count, pairs, lanes), lambda p, *_: (0, 0, 0)),
            ],
            scratch_shapes=[
                pltpu.VMEM((4, rows_y, lanes), F32),
                pltpu.VMEM((slab + 4, rows_y + 2 * PAD, lanes), F32),
                pltpu.VMEM((slab + 2, rows_y + 2 * PAD, lanes), F32),
                pltpu.VMEM((slab, pairs, rows_y, lanes), BF16),
                pltpu.VMEM(occupied.shape, BF16),
                pltpu.VMEM(virtual.shape, BF16),
                pltpu.SemaphoreType.DMA((2,)),
            ],
        ),
        out_shape=[
            jax.ShapeDtypeStruct((pairs, slab, rows_y, lanes), BF16),
            jax.ShapeDtypeStruct((count, pairs, lanes), F32),
        ],
        compiler_params=pltpu.CompilerParams(vmem_limit_bytes=60 * 1024 * 1024),
        name="final",
    )(
        pair_ids, all_ids, place, occupied, virtual, v0, returned, first_halo, second_halo,
        jnp.asarray(spread, BF16), occupied, virtual,
    )
    sums = jnp.sum(panel, axis=2).reshape(slabs, count // slabs, pairs)
    blocks = lax.all_to_all(sums, "dom", 0, 0)
    return potentials, jnp.sum(blocks, axis=0) / float(slab * rows_y * lanes * slabs)


def solution(mesh):
    placed = (P(None, "dom", None, None), P(None, "dom", None, None), P("pair", None))
    return jax.shard_map(
        shards,
        mesh=mesh,
        in_specs=placed,
        out_specs=(P("pair", "dom", None, None), P("dom", "pair")),
        check_vma=False,
    )
```

time: 308 us -> 71.5 us (0.23)
  local copies, waits for them, and re-layouts: 121 us -> 3.45 us
  other arithmetic: 46.6 us -> 1.51 us
  starting transfers between devices: 60.4 us -> 16.3 us
  blocking collectives: 50.1 us -> 7.87 us
  Pallas kernels: 0 us -> 29.8 us
  between operations: 15.5 us -> 0.73 us
  matrix products: 8.89 us -> 0 us
  waiting for transfers between devices: 4.24 us -> 11.3 us
    slice x30 -> x0, local copies, waits for them, and re-layouts: 97.1 us -> none  [the longest x4 86.5 us: restrict(): half_z = field[:, :, :, 0::2] + field[:, :, :, 1::2]]
    ppermute x16 -> x6, starting transfers between devices: 60.4 us -> 7.63 us  [the longest x3 5.57 us: shards(): lax.ppermute(ids, 'pair', perm)]
    pallas_call x0 -> x3, Pallas kernels: none -> 29.8 us  [the longest x1 13.4 us: shards(): pl.pallas_call(final_kernel, grid_spec=pltpu.PrefetchScalarGridSpec(num_s...]
    unnamed x1 -> x0, blocking collectives: 26.6 us -> none
    all_gather x1 -> x0, blocking collectives: 23.6 us -> none  [coarse_solve(): gathered = lax.all_gather(spectral, 'dom', axis=1, tiled=True)]
    sub x5 -> x0, other arithmetic: 15.4 us -> none  [the longest x2 11.1 us: solve_lines(): solved = lax.linalg.tridiagonal_solve(lower, main, upper, systems)]
    unnamed x27 -> x17, local copies, waits for them, and re-layouts: 17.2 us -> 2.11 us
    add x14 -> x0, other arithmetic: 13.1 us -> none  [the longest x4 6.26 us: sweep_single(): return field + relax_step * (source - apply_operator(rim_of(field)))]
  transfers between devices with their start and end apart: 17 -> 8, of which waited for: 7 -> 5; matrix products, arithmetic and copies ran while one was open for 49% -> 1% of each run, Pallas kernels for 0% -> 7%
where the time goes in v1:
time: 71.5 us; the launch traced here: 70.9 us
  Pallas kernels  29.8 us (42%)
  starting transfers between devices  16.3 us (23%)
  waiting for transfers between devices  11.3 us (16%)
  blocking collectives  7.87 us (11%)
  local copies, waits for them, and re-layouts  3.45 us (5%)
  other arithmetic  1.51 us (2%)
  between operations  0.73 us (1%)
    pallas_call x1, Pallas kernels, shards(): pl.pallas_call(final_kernel, grid_spec=pltpu.PrefetchScalarGridSpec(num_s...  13.4 us
    pallas_call x1, Pallas kernels, shards(): pl.pallas_call(source_kernel, grid_spec=pltpu.PrefetchScalarGridSpec(num_...  11.7 us
    all_to_all x1, blocking collectives, shards(): blocks = lax.all_to_all(sums, 'dom', 0, 0)  7.87 us
    all_to_all x1, waiting for transfers between devices, shards(): lax.all_to_all(shares.reshape(slabs, 3, part_rows, lanes), 'dom', 0, 0)  6.28 us
    ppermute x3, starting transfers between devices, shards(): lax.ppermute(ids, 'pair', perm)  5.57 us
    all_to_all x1, starting transfers between devices, shards(): lax.all_to_all(shares.reshape(slabs, 3, part_rows, lanes), 'dom', 0, 0)  5.18 us
    pallas_call x1, Pallas kernels, shards(): pl.pallas_call(middle_kernel, in_specs=[pl.BlockSpec(memory_space=pltpu.S...  4.7 us
    all_to_all x1, starting transfers between devices, shards(): lax.all_to_all(smoothed, 'dom', 0, 0)  3.45 us
  transfers between devices with their start and end apart: 8, of which 5 were waited for; matrix products, arithmetic and copies ran while one was open for 1% of the time, Pallas kernels for 7%

profile of v1, /device:TPU:0, one launch (start us, length us, event | category | flops | bytes accessed | tf_op | source)
XLA Modules:
  0.0 70.9 jit_solution(18131797004895050673)
XLA Ops:
  0.6 1.3 %copy.18.ids.own_ids = s32[4,2]{1,0:T(4,128)} copy(s32[4,2]{0,1:T(2,128)} %param.11) | data formatting | bytes 64 | tf_op args[2]
  2.0 0.7 stack.20.place
  2.6 0.0 copy-start
  2.6 0.0 copy-start.1
  2.6 0.0 copy-start.2
  2.6 0.0 copy-start.3
  2.6 0.0 copy-start.4
  2.7 11.7 %source.1 = (bf16[4,2,3,64,128]{4,3,2,1,0:T(8,128)(2,1)}, bf16[4,3,256,128]{3,2,1,0:T(8,128)(2,1)}, bf16[4,3,256,128]{3,2,1,0:T(8,128)(2,1)}, f32[4,4,256,128]{3,2,1,0:T(8,128)}) custom-call(s32[4,2]{1,0:T(4,128)} %copy.18.ids.own_ids, s32[5]{0:T(128)} %stack.20.place, bf16[12,4,256,128]{3,2,1,0:T(8,128)(2,1)} %all_occ.1, bf16[12,4,256,128]{3,2,1,0:T(8,128)(2,1)} %all_vir.1, ...), custom_call_target="tpu_custom_call" | custom-call | tf_op jit(solution)/shard_map/source/pallas_call | solution.py:351
  14.3 0.0 copy-start.7
  14.4 5.2 %all-to-all-start = ((bf16[8,3,64,128]{3,2,1,0:T(8,128)(2,1)}), bf16[8,3,64,128]{3,2,1,0:T(8,128)(2,1)S(1)}, u32[]{:S(2)}, u32[]{:S(2)}) async-start(bf16[8,3,64,128]{3,2,1,0:T(8,128)(2,1)} %bitcast.8), calls=%async_computation | async-start | bytes 786432 | tf_op jit(solution)/shard_map/all_to_all | solution.py:389
  19.5 0.5 collective-permute-start.4
  20.0 1.6 %collective-permute-start.5 = (bf16[4,3,256,128]{3,2,1,0:T(8,128)(2,1)}, bf16[4,3,256,128]{3,2,1,0:T(8,128)(2,1)}, u32[]{:S(2)}, u32[]{:S(2)}) collective-permute-start(bf16[4,3,256,128]{3,2,1,0:T(8,128)(2,1)} %get-tuple-element.15), channel_id=1, source_target_pairs={{4,8},{12,16},{20,24},{8,4},{16,12},{24,20},{5,9},{13,17},{21,25},... | collective-permute-start | bytes 2359304 | tf_op jit(solution)/shard_map/ppermute | solution.py:387
  21.6 6.3 %all-to-all-done.refs_0_ = bf16[8,3,64,128]{3,2,1,0:T(8,128)(2,1)S(1)} async-done(((bf16[8,3,64,128]{3,2,1,0:T(8,128)(2,1)}), bf16[8,3,64,128]{3,2,1,0:T(8,128)(2,1)S(1)}, u32[]{:S(2)}, u32[]{:S(2)}) %all-to-all-start) | async-done | bytes 393248 | tf_op jit(solution)/shard_map/all_to_all | solution.py:389
  27.9 0.0 collective-permute-start
  27.9 1.7 %collective-permute-done.refs_1_ = bf16[8,3,64,128]{3,2,1,0:T(8,128)(2,1)S(1)} collective-permute-done((bf16[8,3,64,128]{3,2,1,0:T(8,128)(2,1)S(1)}, bf16[8,3,64,128]{3,2,1,0:T(8,128)(2,1)S(1)}, u32[]{:S(2)}, u32[]{:S(2)}) %collective-permute-start) | collective-permute-done | bytes 393248 | tf_op jit(solution)/shard_map/ppermute | solution.py:393
  29.6 0.0 copy-done
  29.6 0.0 copy-done.1
  29.6 0.0 copy-done.2
  29.6 0.0 copy-done.3
  29.6 0.0 copy-done.4
  29.6 4.7 %middle.1 = bf16[8,3,64,128]{3,2,1,0:T(8,128)(2,1)} custom-call(s32[5]{0:T(128)S(1)} %copy-done.4, bf16[8,3,64,128]{3,2,1,0:T(8,128)(2,1)S(1)} %all-to-all-done.refs_0_, bf16[8,3,64,128]{3,2,1,0:T(8,128)(2,1)S(1)} %collective-permute-done.refs_1_, f32[1024,256]{1,0:T(8,128)S(1)} %copy-done.1, f32[64,64]{1,0:T(8,128)S(1)} %copy-done.3, ...), custom_call_target="tpu_custom_call" | custom-call | tf_op jit(solution)/shard_map/middle/pallas_call | solution.py:397
  34.3 3.5 %all-to-all-start.1 = ((bf16[8,3,64,128]{3,2,1,0:T(8,128)(2,1)}), bf16[8,3,64,128]{3,2,1,0:T(8,128)(2,1)S(1)}, u32[]{:S(2)}, u32[]{:S(2)}) async-start(bf16[8,3,64,128]{3,2,1,0:T(8,128)(2,1)} %middle.1), calls=%async_computation.1 | async-start | bytes 786432 | tf_op jit(solution)/shard_map/all_to_all | solution.py:416
  37.8 0.0 copy-done.7
  37.8 1.6 %collective-permute-start.3 = (s32[4,2]{0,1:T(2,128)S(1)}, s32[4,2]{0,1:T(2,128)S(1)}, u32[]{:S(2)}, u32[]{:S(2)}) collective-permute-start(s32[4,2]{0,1:T(2,128)S(1)} %copy-done.7), channel_id=1, source_target_pairs={{3,0},{0,1},{1,2},{2,3},{7,4},{4,5},{5,6},{6,7},{11,8},{8,9},{9,10... | collective-permute-start | bytes 104 | tf_op jit(solution)/shard_map/ppermute | solution.py:415
  39.4 2.6 %collective-permute-start.2 = (s32[4,2]{0,1:T(2,128)S(1)}, s32[4,2]{0,1:T(2,128)S(1)}, u32[]{:S(2)}, u32[]{:S(2)}) collective-permute-start(s32[4,2]{0,1:T(2,128)S(1)} %copy-done.7), channel_id=1, source_target_pairs={{2,0},{3,1},{0,2},{1,3},{6,4},{7,5},{4,6},{5,7},{10,8},{11,9},{8,1... | collective-permute-start | bytes 104 | tf_op jit(solution)/shard_map/ppermute | solution.py:415
  42.0 1.3 %collective-permute-start.1 = (s32[4,2]{0,1:T(2,128)S(1)}, s32[4,2]{0,1:T(2,128)S(1)}, u32[]{:S(2)}, u32[]{:S(2)}) collective-permute-start(s32[4,2]{0,1:T(2,128)S(1)} %copy-done.7), channel_id=1, source_target_pairs={{1,0},{2,1},{3,2},{0,3},{5,4},{6,5},{7,6},{4,7},{9,8},{10,9},{11,1... | collective-permute-start | bytes 104 | tf_op jit(solution)/shard_map/ppermute | solution.py:415
  43.4 0.0 collective-permute-done.3
  43.4 0.5 collective-permute-done.2
  43.9 1.7 %collective-permute-done.1 = s32[4,2]{0,1:T(2,128)S(1)} collective-permute-done((s32[4,2]{0,1:T(2,128)S(1)}, s32[4,2]{0,1:T(2,128)S(1)}, u32[]{:S(2)}, u32[]{:S(2)}) %collective-permute-start.1) | collective-permute-done | bytes 64 | tf_op jit(solution)/shard_map/ppermute | solution.py:415
  45.6 0.1 pad_add_fusion
  45.7 0.7 copy.19.ids
  46.4 0.0 collective-permute-done.4.first
  46.4 0.0 copy-start.6
  46.4 0.0 collective-permute-done.5.second
  46.4 1.1 %all-to-all-done.1 = bf16[8,3,64,128]{3,2,1,0:T(8,128)(2,1)S(1)} async-done(((bf16[8,3,64,128]{3,2,1,0:T(8,128)(2,1)}), bf16[8,3,64,128]{3,2,1,0:T(8,128)(2,1)S(1)}, u32[]{:S(2)}, u32[]{:S(2)}) %all-to-all-start.1) | async-done | bytes 393248 | tf_op jit(solution)/shard_map/all_to_all | solution.py:416
  47.5 0.0 copy-start.5
  47.5 0.0 copy-done.6
  47.5 0.7 %copy-done.5 = bf16[8,3,64,128]{3,2,1,0:T(8,128)(2,1)} copy-done((bf16[8,3,64,128]{3,2,1,0:T(8,128)(2,1)}, bf16[8,3,64,128]{3,2,1,0:T(8,128)(2,1)S(1)}, u32[]{:S(2)}) %copy-start.5) | copy-done | bytes 393240
  48.2 13.4 %final.1 = (bf16[4,4,256,128]{3,2,1,0:T(8,128)(2,1)}, f32[16,4,128]{2,1,0:T(4,128)}) custom-call(s32[4,2]{1,0:T(4,128)} %copy.18.ids.own_ids, s32[16,2]{1,0:T(8,128)} %copy.19.ids, s32[5]{0:T(128)} %stack.20.place, bf16[12,4,256,128]{3,2,1,0:T(8,128)(2,1)} %all_occ.1, bf16[12,4,256,128]{3,2,1,0:T(8,128)(2,1)} %all_vir.1, ...), custom_call_target="tpu_custom_call" | custom-call | tf_op jit(solution)/shard_map/final/pallas_call | solution.py:419
  61.6 0.8 %reduce_sum.18 = f32[16,4]{1,0:T(8,128)S(1)} reduce(f32[16,4,128]{2,1,0:T(4,128)} %get-tuple-element.17, f32[]{:T(128)} %constant.43.clone.1), dimensions={2}, to_apply=%region_0.1 | reduce | flops 8128 | bytes 33028 | tf_op jit(solution)/shard_map/reduce_sum | solution.py:459
  62.5 7.9 %all_to_all.15 = f32[8,2,4]{2,1,0:T(2,128)S(1)} all-to-all(f32[8,2,4]{2,1,0:T(2,128)S(1)} %bitcast.9), channel_id=1, replica_groups=mesh['dom'=8,'pair'=4] {'dom'}, dimensions={0} | all-to-all | bytes 512 | tf_op jit(solution)/shard_map/all_to_all | solution.py:460
  70.4 0.6 broadcast_multiply_fusion
  (1 shorter events, 0.0 us)
Async XLA Ops:
  2.6 27.0 %copy-start = (f32[256,1024]{1,0:T(8,128)S(1)}, f32[256,1024]{1,0:T(8,128)}, u32[]{:S(2)}) copy-start(f32[256,1024]{1,0:T(8,128)} %constant.49.clone.refs_5_) | copy-start | bytes 3145732
  2.6 27.0 %copy-start.1 = (f32[1024,256]{1,0:T(8,128)S(1)}, f32[1024,256]{1,0:T(8,128)}, u32[]{:S(2)}) copy-start(f32[1024,256]{1,0:T(8,128)} %constant.46.clone.refs_2_) | copy-start | bytes 3145732
  2.6 27.0 %copy-start.2 = (f32[64,256]{1,0:T(8,128)S(1)}, f32[64,256]{1,0:T(8,128)}, u32[]{:S(2)}) copy-start(f32[64,256]{1,0:T(8,128)} %constant.48.clone.refs_4_) | copy-start | bytes 196612
  2.6 27.0 %copy-start.3 = (f32[64,64]{1,0:T(8,128)S(1)}, f32[64,64]{1,0:T(8,128)}, u32[]{:S(2)}) copy-start(f32[64,64]{1,0:T(8,128)} %constant.47.clone.refs_3_) | copy-start | bytes 49156
  2.6 27.0 %copy-start.4 = (s32[5]{0:T(128)S(1)}, s32[5]{0:T(128)}, u32[]{:S(2)}) copy-start(s32[5]{0:T(128)} %stack.20.place) | copy-start | bytes 64
  14.3 23.5 %copy-start.7 = (s32[4,2]{0,1:T(2,128)S(1)}, s32[4,2]{0,1:T(2,128)}, u32[]{:S(2)}) copy-start(s32[4,2]{0,1:T(2,128)} %param.11) | copy-start | bytes 100
  14.4 13.5 %all-to-all-start = ((bf16[8,3,64,128]{3,2,1,0:T(8,128)(2,1)}), bf16[8,3,64,128]{3,2,1,0:T(8,128)(2,1)S(1)}, u32[]{:S(2)}, u32[]{:S(2)}) async-start(bf16[8,3,64,128]{3,2,1,0:T(8,128)(2,1)} %bitcast.8), calls=%async_computation | async-start | bytes 786432 | tf_op jit(solution)/shard_map/all_to_all | solution.py:389
  19.5 26.8 %collective-permute-start.4 = (bf16[4,3,256,128]{3,2,1,0:T(8,128)(2,1)}, bf16[4,3,256,128]{3,2,1,0:T(8,128)(2,1)S(1)}, u32[]{:S(2)}, u32[]{:S(2)}) collective-permute-start(bf16[4,3,256,128]{3,2,1,0:T(8,128)(2,1)} %get-tuple-element.14), channel_id=1, source_target_pairs={{0,4},{4,0},{8,12},{12,8},{16,20},{20,16},{24,28},{28,24},{1,5},{5... | collective-permute-start | bytes 2359304 | tf_op jit(solution)/shard_map/ppermute | solution.py:386
  20.0 26.3 %collective-permute-start.5 = (bf16[4,3,256,128]{3,2,1,0:T(8,128)(2,1)}, bf16[4,3,256,128]{3,2,1,0:T(8,128)(2,1)}, u32[]{:S(2)}, u32[]{:S(2)}) collective-permute-start(bf16[4,3,256,128]{3,2,1,0:T(8,128)(2,1)} %get-tuple-element.15), channel_id=1, source_target_pairs={{4,8},{12,16},{20,24},{8,4},{16,12},{24,20},{5,9},{13,17},{21,25},... | collective-permute-start | bytes 2359304 | tf_op jit(solution)/shard_map/ppermute | solution.py:387
  27.9 1.7 %collective-permute-start = (bf16[8,3,64,128]{3,2,1,0:T(8,128)(2,1)S(1)}, bf16[8,3,64,128]{3,2,1,0:T(8,128)(2,1)S(1)}, u32[]{:S(2)}, u32[]{:S(2)}) collective-permute-start(bf16[8,3,64,128]{3,2,1,0:T(8,128)(2,1)S(1)} %all-to-all-done.refs_0_), channel_id=1, source_target_pairs={{4,0},{0,4},{12,8},{8,12},{20,16},{16,20},{28,24},{24,28},{5,1},{1... | collective-permute-start | bytes 1179656 | tf_op jit(solution)/shard_map/ppermute | solution.py:393
  34.3 13.1 %all-to-all-start.1 = ((bf16[8,3,64,128]{3,2,1,0:T(8,128)(2,1)}), bf16[8,3,64,128]{3,2,1,0:T(8,128)(2,1)S(1)}, u32[]{:S(2)}, u32[]{:S(2)}) async-start(bf16[8,3,64,128]{3,2,1,0:T(8,128)(2,1)} %middle.1), calls=%async_computation.1 | async-start | bytes 786432 | tf_op jit(solution)/shard_map/all_to_all | solution.py:416
  37.8 5.6 %collective-permute-start.3 = (s32[4,2]{0,1:T(2,128)S(1)}, s32[4,2]{0,1:T(2,128)S(1)}, u32[]{:S(2)}, u32[]{:S(2)}) collective-permute-start(s32[4,2]{0,1:T(2,128)S(1)} %copy-done.7), channel_id=1, source_target_pairs={{3,0},{0,1},{1,2},{2,3},{7,4},{4,5},{5,6},{6,7},{11,8},{8,9},{9,10... | collective-permute-start | bytes 104 | tf_op jit(solution)/shard_map/ppermute | solution.py:415
  39.4 4.5 %collective-permute-start.2 = (s32[4,2]{0,1:T(2,128)S(1)}, s32[4,2]{0,1:T(2,128)S(1)}, u32[]{:S(2)}, u32[]{:S(2)}) collective-permute-start(s32[4,2]{0,1:T(2,128)S(1)} %copy-done.7), channel_id=1, source_target_pairs={{2,0},{3,1},{0,2},{1,3},{6,4},{7,5},{4,6},{5,7},{10,8},{11,9},{8,1... | collective-permute-start | bytes 104 | tf_op jit(solution)/shard_map/ppermute | solution.py:415
  42.0 3.6 %collective-permute-start.1 = (s32[4,2]{0,1:T(2,128)S(1)}, s32[4,2]{0,1:T(2,128)S(1)}, u32[]{:S(2)}, u32[]{:S(2)}) collective-permute-start(s32[4,2]{0,1:T(2,128)S(1)} %copy-done.7), channel_id=1, source_target_pairs={{1,0},{2,1},{3,2},{0,3},{5,4},{6,5},{7,6},{4,7},{9,8},{10,9},{11,1... | collective-permute-start | bytes 104 | tf_op jit(solution)/shard_map/ppermute | solution.py:415
  46.4 1.1 %copy-start.6 = (bf16[4,3,256,128]{3,2,1,0:T(8,128)(2,1)}, bf16[4,3,256,128]{3,2,1,0:T(8,128)(2,1)S(1)}, u32[]{:S(2)}) copy-start(bf16[4,3,256,128]{3,2,1,0:T(8,128)(2,1)S(1)} %collective-permute-done.4.first) | copy-start | bytes 2359300
  47.5 0.8 %copy-start.5 = (bf16[8,3,64,128]{3,2,1,0:T(8,128)(2,1)}, bf16[8,3,64,128]{3,2,1,0:T(8,128)(2,1)S(1)}, u32[]{:S(2)}) copy-start(bf16[8,3,64,128]{3,2,1,0:T(8,128)(2,1)S(1)} %all-to-all-done.1) | copy-start | bytes 1179652

commit v2 on v0

v2 whole, which is shorter than its diff:
```python
import math

import jax
import jax.numpy as jnp
import numpy as np
from jax import lax
from jax.experimental import pallas as pl
from jax.experimental.pallas import tpu as pltpu
from jax.sharding import PartitionSpec as P

W = 0.8 / 6.0
CENTRE = 1.5
PAD = 8
STEP = 64
F32 = jnp.float32
BF16 = jnp.bfloat16
MIB = 1024 * 1024
HIGHEST = lax.Precision.HIGHEST


def dot(a, b, contract=((1,), (0,)), precision=None):
    return lax.dot_general(a, b, (contract, ((), ())), precision=precision, preferred_element_type=F32)


def high_low(x):
    high = x.astype(BF16)
    return high, (x - high.astype(F32)).astype(BF16)


def dot_split(a, table, contract=((1,), (0,))):
    high, low = high_low(a)
    return dot(high, table[0], contract) + (dot(low, table[0], contract) + dot(high, table[1], contract))


def zero_rims(ref):
    zeros = jnp.zeros((ref.shape[0], PAD, ref.shape[2]), F32)
    ref[:, :PAD] = zeros
    ref[:, ref.shape[1] - PAD :] = zeros


def read(ref, layer, row, rows=STEP):
    return ref[layer, PAD + row : PAD + row + rows, :]


def put(ref, layer, row, value):
    ref[layer, PAD + row : PAD + row + value.shape[0]] = value


def across(centre, blocks=1):
    lane = lax.broadcasted_iota(jnp.int32, centre.shape, 1)
    width = centre.shape[1] // blocks
    first = lane % width == 0 if blocks > 1 else lane == 0
    last = lane % width == width - 1 if blocks > 1 else lane == width - 1
    lower = jnp.where(first, 0.0, pltpu.roll(centre, 1, 1))
    upper = jnp.where(last, 0.0, pltpu.roll(centre, centre.shape[1] - 1, 1))
    return CENTRE * centre + lower + upper


def across_by_matrix(centre, band):
    high, low = high_low(centre)
    return dot(jnp.concatenate([high, low], axis=1), band)


def beside(ref, layer, row, rows=STEP):
    return read(ref, layer, row - 1, rows) + read(ref, layer, row + 1, rows)


def stencil(ref, layer, row, band):
    centre = read(ref, layer, row)
    along_z = across(centre) if layer % 2 else across_by_matrix(centre, band)
    return along_z + beside(ref, layer, row)


def fill_band(ref):
    lanes = ref.shape[1]
    line = lax.rem(lax.broadcasted_iota(jnp.int32, ref.shape, 0), lanes)
    apart = jnp.abs(line - lax.broadcasted_iota(jnp.int32, ref.shape, 1))
    ref[...] = jnp.where(apart == 0, CENTRE, jnp.where(apart == 1, 1.0, 0.0)).astype(BF16)


def fill_children(ref, value, axis):
    child = lax.broadcasted_iota(jnp.int32, ref.shape, axis)
    parent = lax.broadcasted_iota(jnp.int32, ref.shape, 1 - axis)
    ref[...] = jnp.where(child // 2 == parent, value, 0.0).astype(BF16)


def sides(axis="dom"):
    me, count = lax.axis_index(axis), lax.axis_size(axis)
    below = jnp.where(me == 0, 0.0, 1.0).astype(F32)
    above = jnp.where(me == count - 1, 0.0, 1.0).astype(F32)
    return below, above, lax.rem(me, 2) == 0


def source_kernel(
    ids_hbm, occ, vir, shares, first, second, v0_out, ids_out,
    ids, occ_rows, vir_rows, band, fold, own, once, v0s, sums, packed, share, ids_tile, ids_sems, in_sems, out_sems,
):
    pairs, slab, rows_y, lanes = occ_rows.shape
    parts, part_rows = share.shape[1], share.shape[3]
    in_left, in_right, even = sides()
    upper = jnp.where(even, 1, 0)

    copy = pltpu.make_async_copy(ids_hbm, ids, ids_sems.at[0])
    copy.start()
    copy.wait()

    def inputs(p):
        return (
            pltpu.make_async_copy(occ.at[ids[0, p]], occ_rows.at[p], in_sems.at[0, p]),
            pltpu.make_async_copy(vir.at[ids[1, p]], vir_rows.at[p], in_sems.at[1, p]),
        )

    def outputs(p):
        return (
            pltpu.make_async_copy(share.at[p], shares.at[p], out_sems.at[0, p]),
            pltpu.make_async_copy(packed.at[p, upper], first.at[p], out_sems.at[1, p]),
            pltpu.make_async_copy(packed.at[p, 1 - upper], second.at[p], out_sems.at[2, p]),
            pltpu.make_async_copy(v0s.at[p], v0_out.at[p], out_sems.at[3, p]),
        )

    for p in range(pairs):
        for copy in inputs(p):
            copy.start()
    line = lax.broadcasted_iota(jnp.int32, ids_tile.shape, 0)
    lane = lax.broadcasted_iota(jnp.int32, ids_tile.shape, 1)
    tile = jnp.zeros(ids_tile.shape, F32)
    for p in range(pairs):
        for j in range(2):
            tile = jnp.where((line == j) & (lane == p), ids[j, p].astype(F32), tile)
    ids_tile[...] = tile.astype(BF16)
    ids_copy = pltpu.make_async_copy(ids_tile, ids_out, ids_sems.at[1])
    ids_copy.start()
    fill_band(band)
    fill_children(fold, 0.5, 0)
    zero_rims(own)
    zero_rims(once)

    def one_pair(p, carry):
        for copy in inputs(p):
            copy.wait()
        for layer in range(slab):
            own[layer, PAD : PAD + rows_y] = occ_rows[p, layer].astype(F32) * vir_rows[p, layer].astype(F32)

        for row in range(0, rows_y, STEP):
            rows = slice(row, row + STEP)
            for layer in range(slab):
                centre = read(own, layer, row)
                total = stencil(own, layer, row, band[...])
                if layer > 0:
                    total = total + read(own, layer - 1, row)
                if layer < slab - 1:
                    total = total + read(own, layer + 1, row)
                value = W * total
                put(once, layer + 1, row, value)
                v0 = W * (centre + value)
                v0s[p, layer, rows] = v0
                if layer == 0:
                    put(once, 0, row, (W * in_left) * centre)
                    packed[p, 0, 0, rows] = centre.astype(BF16)
                    packed[p, 0, 1, rows] = v0.astype(BF16)
                if layer == 1:
                    packed[p, 0, 2, rows] = v0.astype(BF16)
                if layer == slab - 2:
                    packed[p, 1, 2, rows] = v0.astype(BF16)
                if layer == slab - 1:
                    put(once, slab + 1, row, (W * in_right) * centre)
                    packed[p, 1, 0, rows] = centre.astype(BF16)
                    packed[p, 1, 1, rows] = v0.astype(BF16)

        def twice(layer, row):
            if layer == -2:
                return read(once, 0, row)
            if layer == slab + 1:
                return read(once, slab + 1, row)
            at = layer + 1
            total = stencil(once, at, row, band[...])
            if at > 0:
                total = total + read(once, at - 1, row)
            if at < slab + 1:
                total = total + read(once, at + 1, row)
            return total

        for row in range(0, rows_y, STEP):
            for coarse in range(slab // 2 + 2):
                pair_sum = twice(2 * coarse - 2, row) + twice(2 * coarse - 1, row)
                sums[coarse, row : row + STEP] = W * pair_sum

        half = rows_y // 2

        def folded(coarse):
            return sums[coarse, pl.ds(0, half, stride=2), :] + sums[coarse, pl.ds(1, half, stride=2), :]

        def together(left, right):
            both = jnp.concatenate([folded(left), folded(right)], axis=1)
            high, low = high_low(both)
            return dot(high, fold[...]) + dot(low, fold[...])

        outer = together(3, 0)
        edge = outer.astype(BF16)
        lane = lax.broadcasted_iota(jnp.int32, outer.shape, 1)
        rest = pltpu.roll(outer - edge.astype(F32), lanes // 2, 1) * jnp.where(lane < lanes // 2, in_left, in_right)
        own_high, own_low = high_low(together(1, 2) + rest)
        for part in range(parts):
            rows = slice(part * part_rows, (part + 1) * part_rows)
            share[p, part, 0] = own_high[rows]
            share[p, part, 1] = own_low[rows]
            share[p, part, 2] = edge[rows]
        for copy in outputs(p):
            copy.start()
        return carry

    lax.fori_loop(0, pairs, one_pair, 0)
    ids_copy.wait()
    for p in range(pairs):
        for copy in outputs(p):
            copy.wait()


def middle_kernel(*refs):
    parts = len(refs) - 10
    received = refs[:parts]
    modes, table_y, inverse, ids_tile, out = refs[parts : parts + 5]
    source, field_a, field_b, smooth, edge = refs[parts + 5 :]
    slabs, _, part_rows, lanes = received[0].shape
    rows_y = parts * part_rows
    own_part = lax.rem(lax.axis_index("dom"), parts)
    left = lax.broadcasted_iota(jnp.int32, (part_rows, lanes), 1) < lanes // 2
    for ref in (source, field_a, field_b):
        zero_rims(ref)
    for turn in range(parts):
        at = own_part + turn
        at = jnp.where(at >= parts, at - parts, at) * part_rows
        at = pl.multiple_of(at, part_rows)
        ref = received[turn]
        for d in range(slabs):
            value = ref[d, 0].astype(F32) + ref[d, 1].astype(F32)
            before = ref[d - 1, 2].astype(F32) if d > 0 else jnp.zeros_like(value)
            after = ref[d + 1, 2].astype(F32) if d < slabs - 1 else jnp.zeros_like(value)
            source[d, pl.ds(PAD + at, part_rows)] = value + jnp.where(left, before, after)

    half = lanes // 2
    left = lax.broadcasted_iota(jnp.int32, (rows_y, lanes), 1) < half

    def swapped(ref, d):
        return pltpu.roll(read(ref, d, 0, rows_y), half, 1)

    def apply(ref, each):
        zeros = jnp.zeros((rows_y, lanes), F32)
        before, here = zeros, swapped(ref, 0)
        for d in range(slabs):
            after = swapped(ref, d + 1) if d < slabs - 1 else zeros
            total = across(read(ref, d, 0, rows_y), 2) + beside(ref, d, 0, rows_y)
            each(d, total + here + jnp.where(left, before, after))
            before, here = here, after

    apply(source, lambda d, total: put(field_a, d, 0, W * total))

    def to_coarse(d, total):
        smooth[d] = W * (read(source, d, 0, rows_y) + read(field_a, d, 0, rows_y))
        put(field_b, d, 0, W * total)

    apply(field_a, to_coarse)
    pieces = []
    for d in range(slabs):
        even_rows = field_b[d, pl.ds(PAD, rows_y // 2, stride=2), :]
        odd_rows = field_b[d, pl.ds(PAD + 1, rows_y // 2, stride=2), :]
        pieces.append(even_rows + odd_rows)
    spectral = dot_split(jnp.concatenate(pieces, axis=1), modes)
    spectral = dot(table_y[...], spectral, precision=HIGHEST) * inverse[...]
    spread = dot_split(dot(table_y[...], spectral, precision=HIGHEST), modes, ((1,), (1,)))
    for d in range(slabs):
        value = spread[:, d * lanes : (d + 1) * lanes]
        field_b[d, pl.ds(PAD, rows_y // 2, stride=2), :] = value
        field_b[d, pl.ds(PAD + 1, rows_y // 2, stride=2), :] = value
    for d in range(slabs):
        put(field_a, d, 0, smooth[d] + read(field_b, d, 0, rows_y))

    def add_source(ref):
        return lambda d, total: put(ref, d, 0, W * (total + read(source, d, 0, rows_y)))

    apply(field_a, add_source(field_b))
    apply(field_b, add_source(field_a))
    zeros = jnp.zeros((rows_y, lanes), F32)
    before, here = zeros, swapped(field_a, 0)
    for d in range(slabs):
        after = swapped(field_a, d + 1) if d < slabs - 1 else zeros
        edge[d] = jnp.where(left, before, after) - read(field_a, d, 0, rows_y)
        before, here = here, after
    at = pl.multiple_of(own_part * part_rows, part_rows)
    for d in range(slabs):
        high, low = high_low(field_a[d, pl.ds(PAD + at, part_rows)])
        out[d, :part_rows] = high
        out[d, part_rows : 2 * part_rows] = low
        out[d, 2 * part_rows : 3 * part_rows] = edge[d, pl.ds(at, part_rows)].astype(BF16)
        out[d, 3 * part_rows :] = ids_tile[...]


def final_kernel(
    ids_hbm, all_occ, all_vir, v0_hbm, coarse, first, second, out, panel,
    ids, occ_rows, vir_rows, v0, band, spread, identity, own_field, wide, start, swept, kept,
    occ, vir, late_vector, late_ids, turned, sums, ids_sem, in_sems, out_sems, late_sems,
):
    pairs, slab, rows_y, lanes = kept.shape
    groups = late_vector.shape[0]
    parts, part_rows = coarse.shape[0] // pairs, (coarse.shape[1] - 16) // 3
    in_left, in_right, even = sides()

    ids_copy = pltpu.make_async_copy(ids_hbm, ids, ids_sem)
    ids_copy.start()

    def inputs(p):
        return [pltpu.make_async_copy(v0_hbm.at[p], v0.at[p], in_sems.at[0, p])]

    def own_rows(p):
        return [
            pltpu.make_async_copy(all_occ.at[ids[0, p]], occ_rows.at[p], in_sems.at[1, p]),
            pltpu.make_async_copy(all_vir.at[ids[1, p]], vir_rows.at[p], in_sems.at[2, p]),
        ]

    def output(p):
        return pltpu.make_async_copy(kept.at[p], out.at[p], out_sems.at[p])

    for copy in inputs(0):
        copy.start()
    ids_copy.wait()
    for copy in own_rows(0):
        copy.start()
    for p in range(1, pairs):
        for copy in inputs(p) + own_rows(p):
            copy.start()
    late = [pltpu.make_async_copy(all_occ, occ, late_sems.at[0]), pltpu.make_async_copy(all_vir, vir, late_sems.at[1])]
    for copy in late:
        copy.start()
    fill_band(band)
    fill_children(spread, 1.0, 1)
    line = lax.broadcasted_iota(jnp.int32, identity.shape, 0)
    identity[...] = jnp.where(line == lax.broadcasted_iota(jnp.int32, identity.shape, 1), 1.0, 0.0).astype(BF16)
    zero_rims(start)
    zero_rims(swept)

    def one_pair(p, carry):
        for copy in inputs(p) + own_rows(p):
            copy.wait()
        for layer in range(slab):
            own_field[layer] = occ_rows[p, layer].astype(F32) * vir_rows[p, layer].astype(F32)
        for part in range(parts):
            table = spread[...]
            at = p * parts + part
            own = dot(coarse[at, :part_rows], table) + dot(coarse[at, part_rows : 2 * part_rows], table)
            beyond = own + dot(coarse[at, 2 * part_rows : 3 * part_rows], table)
            for at, value in enumerate((beyond[:, :lanes], own[:, :lanes], own[:, lanes:], beyond[:, lanes:])):
                rows = 2 * part * part_rows
                wide[at, pl.ds(rows, part_rows, stride=2), :] = value
                wide[at, pl.ds(rows + 1, part_rows, stride=2), :] = value

        def halo(edge, index, row):
            rows = slice(row, row + STEP)
            one, two = first[p, index, rows].astype(F32), second[p, index, rows].astype(F32)
            return jnp.where(even == (edge == 1), one, two)

        for row in range(0, rows_y, STEP):
            rows = slice(row, row + STEP)
            for layer in range(slab):
                value = v0[p, layer, rows] + wide[1 + layer // 2, rows]
                if layer == 0:
                    value = value + (W * W) * halo(0, 0, row)
                if layer == slab - 1:
                    value = value + (W * W) * halo(1, 0, row)
                put(start, layer + 2, row, value)
            near = halo(0, 1, row) + (W * W) * own_field[0, rows] + wide[0, rows]
            put(start, 1, row, in_left * near)
            put(start, 0, row, in_left * (halo(0, 2, row) + wide[0, rows]))
            near = halo(1, 1, row) + (W * W) * own_field[slab - 1, rows] + wide[3, rows]
            put(start, slab + 2, row, in_right * near)
            put(start, slab + 3, row, in_right * (halo(1, 2, row) + wide[3, rows]))

        def sweep(ref, at, row, source):
            total = stencil(ref, at, row, band[...])
            return W * (total + read(ref, at - 1, row) + read(ref, at + 1, row) + source)

        for row in range(0, rows_y, STEP):
            rows = slice(row, row + STEP)
            put(swept, 0, row, in_left * sweep(start, 1, row, halo(0, 0, row)))
            for layer in range(slab):
                put(swept, layer + 1, row, sweep(start, layer + 2, row, own_field[layer, rows]))
            put(swept, slab + 1, row, in_right * sweep(start, slab + 2, row, halo(1, 0, row)))
        for row in range(0, rows_y, STEP):
            rows = slice(row, row + STEP)
            for layer in range(slab):
                value = sweep(swept, layer + 1, row, own_field[layer, rows]).astype(BF16)
                kept[p, layer, rows] = value
        output(p).start()
        return carry

    lax.fori_loop(0, pairs, one_pair, 0)

    for copy in late:
        copy.wait()
    for turn in range(groups):
        late_vector[turn] = coarse[turn, 3 * part_rows :].astype(F32).astype(jnp.int32)
    copy = pltpu.make_async_copy(late_vector, late_ids, ids_sem)
    copy.start()
    half = lanes // 2
    for q in range(pairs):
        for layer in range(slab):
            value = dot(identity[...], kept[q, layer], ((1,), (1,))).astype(BF16)
            column = 2 * layer * rows_y
            turned[q * half : (q + 1) * half, column : column + rows_y] = value[:half]
            turned[q * half : (q + 1) * half, column + rows_y : column + 2 * rows_y] = value[half:]
    copy.wait()
    count = groups * pairs
    first_row = lax.axis_index("pair") * pairs
    left = lax.broadcasted_iota(jnp.int32, (rows_y, lanes), 1) < half
    diagonal = lax.broadcasted_iota(jnp.int32, (half, 2 * lanes), 0) == lax.rem(
        lax.broadcasted_iota(jnp.int32, (half, 2 * lanes), 1), half
    )

    def density16(p, layer):
        turn, k = p // pairs, lax.rem(p, pairs)
        i, a = late_ids[turn, 0, k], late_ids[turn, 1, k]
        return (occ[i, layer].astype(F32) * vir[a, layer].astype(F32)).astype(BF16)

    def four_rows(turn, carry):
        p = 4 * turn
        pieces = []
        for layer in range(slab):
            upper_row, lower_row = [], []
            for j in (0, 2):
                one, two = density16(p + j, layer), density16(p + j + 1, layer)
                upper_row.append(jnp.where(left, one, pltpu.roll(two, half, 1)))
                lower_row.append(jnp.where(left, pltpu.roll(one, half, 1), two))
            pieces += [jnp.concatenate(upper_row, axis=1), jnp.concatenate(lower_row, axis=1)]
        product = dot(turned[...], jnp.concatenate(pieces, axis=0))
        row = first_row + p
        row = jnp.where(row >= count, row - count, row) // 2
        for q in range(pairs):
            block = jnp.where(diagonal, product[q * half : (q + 1) * half], 0.0)
            block = jnp.sum(block, axis=0, keepdims=True)
            sums[row, q : q + 1] = block[:, :lanes]
            sums[row + 1, q : q + 1] = block[:, lanes:]
        return carry

    lax.fori_loop(0, count // 4, four_rows, 0)
    scale = 1.0 / float(slab * rows_y * lanes * lax.axis_size("dom"))
    total = scale * sums[...]
    left = lax.broadcasted_iota(jnp.int32, total.shape, 2) < half
    panel[0] = jnp.sum(jnp.where(left, total, 0.0), axis=2)
    panel[1] = jnp.sum(jnp.where(left, 0.0, total), axis=2)
    for p in range(pairs):
        output(p).wait()


def sine_table(length):
    steps = np.arange(length, dtype=np.float64) + 1.0
    return math.sqrt(2.0 / (length + 1)) * np.sin(np.pi * steps[:, None] * steps[None, :] / (length + 1))


def eigenvalues(length):
    return 2.0 - 2.0 * np.cos(np.pi * (np.arange(length, dtype=np.float64) + 1.0) / (length + 1))


def coarse_tables(size_x, size_y, size_z):
    sine_x, sine_z = sine_table(size_x), sine_table(size_z)
    modes = np.einsum("dk,zl->dzkl", sine_x, np.repeat(sine_z, 2, axis=0))
    modes = np.repeat(modes[:, None], 2, axis=1).reshape(size_x * 4 * size_z, size_x * size_z)
    high = modes.astype(BF16)
    low = (modes - high.astype(np.float64)).astype(BF16)
    total = eigenvalues(size_y)[:, None, None] + eigenvalues(size_x)[None, :, None] + eigenvalues(size_z)[None, None, :]
    inverse = (0.5 / total).reshape(size_y, size_x * size_z)
    return jnp.asarray(np.stack([high, low])), jnp.asarray(sine_table(size_y), F32), jnp.asarray(inverse, F32)


def shards(occupied, virtual, pair_ids):
    orbitals, slab, rows_y, lanes = occupied.shape
    pairs = pair_ids.shape[0]
    slabs = lax.axis_size("dom")
    parts = slabs // pairs
    half_y = rows_y // 2
    part_rows = half_y // parts
    padded_y = rows_y + 2 * PAD
    ids = pair_ids.T

    hbm, vmem = pl.BlockSpec(memory_space=pltpu.HBM), pl.BlockSpec(memory_space=pltpu.VMEM)
    anywhere = pl.BlockSpec(memory_space=pl.ANY)
    in_hbm = lambda x: pltpu.with_memory_space_constraint(x, pltpu.HBM)
    halo = (pairs, 3, rows_y, lanes)
    own = (pairs, slab, rows_y, lanes)
    share = (pairs, parts, 3, part_rows, lanes)
    tile = (16, lanes)
    shares, first, second, v0, ids_tile = pl.pallas_call(
        source_kernel,
        in_specs=[hbm, hbm, hbm],
        out_specs=[hbm] * 5,
        out_shape=[
            pltpu.HBM(share, BF16),
            pltpu.HBM(halo, BF16),
            pltpu.HBM(halo, BF16),
            pltpu.HBM(own, F32),
            pltpu.HBM(tile, BF16),
        ],
        scratch_shapes=[
            pltpu.SMEM(ids.shape, jnp.int32),
            pltpu.VMEM(own, BF16),
            pltpu.VMEM(own, BF16),
            pltpu.VMEM((2 * lanes, lanes), BF16),
            pltpu.VMEM((2 * lanes, lanes), BF16),
            pltpu.VMEM((slab, padded_y, lanes), F32),
            pltpu.VMEM((slab + 2, padded_y, lanes), F32),
            pltpu.VMEM(own, F32),
            pltpu.VMEM((slab // 2 + 2, rows_y, lanes), F32),
            pltpu.VMEM((pairs, 2, 3, rows_y, lanes), BF16),
            pltpu.VMEM(share, BF16),
            pltpu.VMEM(tile, BF16),
            pltpu.SemaphoreType.DMA((2,)),
            pltpu.SemaphoreType.DMA((2, pairs)),
            pltpu.SemaphoreType.DMA((4, pairs)),
        ],
        compiler_params=pltpu.CompilerParams(vmem_limit_bytes=32 * MIB),
        name="source",
    )(in_hbm(ids), in_hbm(occupied), in_hbm(virtual))

    inside = [(i, i ^ 1) for i in range(slabs)]
    outside = [(i, i + 1) for i in range(1, slabs - 1, 2)]
    outside = outside + [(j, i) for i, j in outside]
    first_halo = lax.ppermute(first, "dom", inside)
    second_halo = lax.ppermute(second, "dom", outside)
    groups = lax.axis_size("pair")
    perm = [(d * groups + (g + d) % groups, d * groups + g) for d in range(slabs) for g in range(groups)]
    ids_tile = lax.ppermute(ids_tile, ("dom", "pair"), perm)

    received = lax.all_to_all(shares.reshape(slabs, 3, part_rows, lanes), "dom", 0, 0)
    views = [received]
    for turn in range(1, parts):
        perm = [(g * parts + (h + turn) % parts, g * parts + h) for g in range(slabs // parts) for h in range(parts)]
        views.append(lax.ppermute(received, "dom", perm))
    tables = coarse_tables(slabs, half_y // 2, lanes // 4)
    padded = pltpu.VMEM((slabs, half_y + 2 * PAD, lanes), F32)
    plain = pltpu.VMEM((slabs, half_y, lanes), F32)
    smoothed = pl.pallas_call(
        middle_kernel,
        in_specs=[vmem] * (parts + 4),
        out_specs=vmem,
        out_shape=jax.ShapeDtypeStruct((slabs, 3 * part_rows + 16, lanes), BF16),
        scratch_shapes=[padded, padded, padded, plain, plain],
        compiler_params=pltpu.CompilerParams(vmem_limit_bytes=32 * MIB),
        name="middle",
    )(*views, *tables, ids_tile)
    returned = lax.all_to_all(smoothed, "dom", 0, 0)

    count = groups * pairs
    potentials, panel = pl.pallas_call(
        final_kernel,
        in_specs=[hbm] * 4 + [vmem] * 3,
        out_specs=[hbm, vmem],
        out_shape=[pltpu.HBM(own, BF16), jax.ShapeDtypeStruct((2, count // 2, pairs), F32)],
        scratch_shapes=[
            pltpu.SMEM(ids.shape, jnp.int32),
            pltpu.VMEM(own, BF16),
            pltpu.VMEM(own, BF16),
            pltpu.VMEM(own, F32),
            pltpu.VMEM((2 * lanes, lanes), BF16),
            pltpu.VMEM((lanes, 2 * lanes), BF16),
            pltpu.VMEM((lanes, lanes), BF16),
            pltpu.VMEM((slab, rows_y, lanes), F32),
            pltpu.VMEM((4, rows_y, lanes), F32),
            pltpu.VMEM((slab + 4, padded_y, lanes), F32),
            pltpu.VMEM((slab + 2, padded_y, lanes), F32),
            pltpu.VMEM(own, BF16),
            pltpu.VMEM(occupied.shape, BF16),
            pltpu.VMEM(virtual.shape, BF16),
            pltpu.VMEM((groups,) + tile, jnp.int32),
            pltpu.SMEM((groups,) + tile, jnp.int32),
            pltpu.VMEM((pairs * lanes // 2, 2 * slab * rows_y), BF16),
            pltpu.VMEM((count // 2, pairs, lanes), F32),
            pltpu.SemaphoreType.DMA,
            pltpu.SemaphoreType.DMA((3, pairs)),
            pltpu.SemaphoreType.DMA((pairs,)),
            pltpu.SemaphoreType.DMA((2,)),
        ],
        compiler_params=pltpu.CompilerParams(vmem_limit_bytes=24 * MIB),
        name="final",
    )(in_hbm(ids), in_hbm(occupied), in_hbm(virtual), in_hbm(v0), returned, first_halo, second_halo)
    panel = jnp.swapaxes(panel, 0, 1).reshape(slabs, count // slabs, pairs)
    return potentials, jnp.sum(lax.all_to_all(panel, "dom", 0, 0), axis=0)


def solution(mesh):
    placed = (P(None, "dom", None, None), P(None, "dom", None, None), P("pair", None))
    return jax.shard_map(
        shards,
        mesh=mesh,
        in_specs=placed,
        out_specs=(P("pair", "dom", None, None), P("dom", "pair")),
        check_vma=False,
    )
```

time: 308 us -> 60 us (0.19)
  local copies, waits for them, and re-layouts: 121 us -> 0.03 us
  other arithmetic: 46.6 us -> 0.58 us
  starting transfers between devices: 60.4 us -> 14.9 us
  blocking collectives: 50.1 us -> 7.07 us
  Pallas kernels: 0 us -> 20.1 us
  between operations: 15.5 us -> 0.71 us
  waiting for transfers between devices: 4.24 us -> 16.2 us
  matrix products: 8.89 us -> 0 us
    slice x30 -> x0, local copies, waits for them, and re-layouts: 97.1 us -> none  [the longest x4 86.5 us: restrict(): half_z = field[:, :, :, 0::2] + field[:, :, :, 1::2]]
    ppermute x16 -> x4, starting transfers between devices: 60.4 us -> 2.53 us  [the longest x1 1.33 us: shards(): ids_tile = lax.ppermute(ids_tile, ('dom', 'pair'), perm)]
    unnamed x1 -> x0, blocking collectives: 26.6 us -> none
    all_gather x1 -> x0, blocking collectives: 23.6 us -> none  [coarse_solve(): gathered = lax.all_gather(spectral, 'dom', axis=1, tiled=True)]
    pallas_call x0 -> x3, Pallas kernels: none -> 20.1 us  [the longest x1 9.55 us: shards(): pl.pallas_call(final_kernel, in_specs=[hbm] * 4 + [vmem] * 3, out_specs=[...]
    unnamed x27 -> x6, local copies, waits for them, and re-layouts: 17.2 us -> 0.02 us
    all_to_all x0 -> x2, waiting for transfers between devices: none -> 15.8 us  [the longest x1 8.68 us: shards(): returned = lax.all_to_all(smoothed, 'dom', 0, 0)]
    sub x5 -> x0, other arithmetic: 15.4 us -> none  [the longest x2 11.1 us: solve_lines(): solved = lax.linalg.tridiagonal_solve(lower, main, upper, systems)]
  transfers between devices with their start and end apart: 17 -> 6, of which waited for: 7 -> 3; matrix products, arithmetic and copies ran while one was open for 49% -> 0% of each run, Pallas kernels for 0% -> 7%
where the time goes in v2:
time: 60 us; the launch traced here: 59.6 us
  Pallas kernels  20.1 us (34%)
  waiting for transfers between devices  16.2 us (27%)
  starting transfers between devices  14.9 us (25%)
  blocking collectives  7.07 us (12%)
  between operations  0.71 us (1%)
    pallas_call x1, Pallas kernels, shards(): pl.pallas_call(final_kernel, in_specs=[hbm] * 4 + [vmem] * 3, out_specs=[...  9.55 us
    all_to_all x1, waiting for transfers between devices, shards(): returned = lax.all_to_all(smoothed, 'dom', 0, 0)  8.68 us
    all_to_all x1, starting transfers between devices, shards(): returned = lax.all_to_all(smoothed, 'dom', 0, 0)  7.2 us
    all_to_all x1, waiting for transfers between devices, shards(): lax.all_to_all(shares.reshape(slabs, 3, part_rows, lanes), 'dom', 0, 0)  7.13 us
    all_to_all x1, blocking collectives, shards(): return (potentials, jnp.sum(lax.all_to_all(panel, 'dom', 0, 0), axis=0))  7.07 us
    pallas_call x1, Pallas kernels, shards(): pl.pallas_call(source_kernel, in_specs=[hbm, hbm, hbm], out_specs=[hbm] *...  6.37 us
    all_to_all x1, starting transfers between devices, shards(): lax.all_to_all(shares.reshape(slabs, 3, part_rows, lanes), 'dom', 0, 0)  5.19 us
    pallas_call x1, Pallas kernels, shards(): pl.pallas_call(middle_kernel, in_specs=[vmem] * (parts + 4), out_specs=vm...  4.18 us
  transfers between devices with their start and end apart: 6, of which 3 were waited for; matrix products, arithmetic and copies ran while one was open for 0% of the time, Pallas kernels for 7%

profile of v2, /device:TPU:0, one launch (start us, length us, event | category | flops | bytes accessed | tf_op | source)
XLA Modules:
  0.0 59.6 jit_solution(5098237797072181548)
XLA Ops:
  0.6 0.0 copy-start
  0.6 0.0 copy-start.1
  0.7 0.0 copy-start.2
  0.7 6.4 %source.1 = (bf16[4,2,3,64,128]{4,3,2,1,0:T(8,128)(2,1)}, bf16[4,3,256,128]{3,2,1,0:T(8,128)(2,1)}, bf16[4,3,256,128]{3,2,1,0:T(8,128)(2,1)}, f32[4,4,256,128]{3,2,1,0:T(8,128)}, bf16[16,128]{1,0:T(8,128)(2,1)}) custom-call(s32[2,4]{1,0:T(2,128)} %bitcast.5, bf16[12,4,256,128]{3,2,1,0:T(8,128)(2,1)} %all_occ.1, bf16[12,4,256,128]{3,2,1,0:T(8,128)(2,1)} %all_vir.1), custom_call_target="tpu_custom_call" | custom-call | tf_op jit(solution)/shard_map/source/pallas_call | solution.py:490
  7.0 5.2 %all-to-all-start = ((bf16[8,3,64,128]{3,2,1,0:T(8,128)(2,1)}), bf16[8,3,64,128]{3,2,1,0:T(8,128)(2,1)S(1)}, u32[]{:S(2)}, u32[]{:S(2)}) async-start(bf16[8,3,64,128]{3,2,1,0:T(8,128)(2,1)} %bitcast.4), calls=%async_computation | async-start | bytes 786432 | tf_op jit(solution)/shard_map/all_to_all | solution.py:531
  12.2 0.5 collective-permute-start.2
  12.7 0.7 %collective-permute-start.3 = (bf16[4,3,256,128]{3,2,1,0:T(8,128)(2,1)}, bf16[4,3,256,128]{3,2,1,0:T(8,128)(2,1)S(1)}, u32[]{:S(2)}, u32[]{:S(2)}) collective-permute-start(bf16[4,3,256,128]{3,2,1,0:T(8,128)(2,1)} %get-tuple-element.13), channel_id=1, source_target_pairs={{4,8},{12,16},{20,24},{8,4},{16,12},{24,20},{5,9},{13,17},{21,25},... | collective-permute-start | bytes 2359304 | tf_op jit(solution)/shard_map/ppermute | solution.py:526
  13.4 7.1 %all-to-all-done.refs_0_ = bf16[8,3,64,128]{3,2,1,0:T(8,128)(2,1)S(1)} async-done(((bf16[8,3,64,128]{3,2,1,0:T(8,128)(2,1)}), bf16[8,3,64,128]{3,2,1,0:T(8,128)(2,1)S(1)}, u32[]{:S(2)}, u32[]{:S(2)}) %all-to-all-start) | async-done | bytes 393248 | tf_op jit(solution)/shard_map/all_to_all | solution.py:531
  20.6 0.0 collective-permute-start
  20.6 1.3 %collective-permute-start.1 = (bf16[16,128]{1,0:T(8,128)(2,1)}, bf16[16,128]{1,0:T(8,128)(2,1)S(1)}, u32[]{:S(2)}, u32[]{:S(2)}) collective-permute-start(bf16[16,128]{1,0:T(8,128)(2,1)} %get-tuple-element.11), channel_id=1, source_target_pairs={{0,0},{1,1},{2,2},{3,3},{5,4},{6,5},{7,6},{4,7},{10,8},{11,9},{8,1... | collective-permute-start | bytes 12296 | tf_op jit(solution)/shard_map/ppermute | solution.py:529
  21.9 0.0 collective-permute-done.1.refs_5_
  21.9 0.4 collective-permute-done.refs_1_
  22.3 0.0 copy-done
  22.3 0.0 copy-done.1
  22.3 0.0 copy-done.2
  22.3 4.2 %middle.1 = bf16[8,208,128]{2,1,0:T(8,128)(2,1)} custom-call(bf16[8,3,64,128]{3,2,1,0:T(8,128)(2,1)S(1)} %all-to-all-done.refs_0_, bf16[8,3,64,128]{3,2,1,0:T(8,128)(2,1)S(1)} %collective-permute-done.refs_1_, bf16[2,1024,256]{2,1,0:T(8,128)(2,1)S(1)} %copy-done, f32[64,64]{1,0:T(8,128)S(1)} %copy-done.2, f32[64,256]{1,0:T(8,128)S(1)} %copy-done.1, ...), custom_call_target="tpu_custom_call" | custom-call | tf_op jit(solution)/shard_map/middle/pallas_call | solution.py:539
  26.5 7.2 %all-to-all-start.1 = ((bf16[8,208,128]{2,1,0:T(8,128)(2,1)}), bf16[8,208,128]{2,1,0:T(8,128)(2,1)S(1)}, u32[]{:S(2)}, u32[]{:S(2)}) async-start(bf16[8,208,128]{2,1,0:T(8,128)(2,1)} %middle.1), calls=%async_computation.1 | async-start | bytes 851968 | tf_op jit(solution)/shard_map/all_to_all | solution.py:548
  33.7 0.0 collective-permute-done.2.first
  33.7 0.0 collective-permute-done.3.second
  33.7 8.7 %all-to-all-done.1.coarse = bf16[8,208,128]{2,1,0:T(8,128)(2,1)S(1)} async-done(((bf16[8,208,128]{2,1,0:T(8,128)(2,1)}), bf16[8,208,128]{2,1,0:T(8,128)(2,1)S(1)}, u32[]{:S(2)}, u32[]{:S(2)}) %all-to-all-start.1) | async-done | bytes 426016 | tf_op jit(solution)/shard_map/all_to_all | solution.py:548
  42.4 9.5 %final.1 = (bf16[4,4,256,128]{3,2,1,0:T(8,128)(2,1)}, f32[2,8,4]{2,1,0:T(8,128)S(1)}) custom-call(s32[2,4]{1,0:T(2,128)} %bitcast.6, bf16[12,4,256,128]{3,2,1,0:T(8,128)(2,1)} %all_occ.1, bf16[12,4,256,128]{3,2,1,0:T(8,128)(2,1)} %all_vir.1, f32[4,4,256,128]{3,2,1,0:T(8,128)} %get-tuple-element.9.v0_hbm, bf16[8,208,128]{2,1,0:T(8,128)(2,1)S(1)} %all-to-all-done.1.coarse, ...), custom_call_target="tpu_custom_call" | custom-call | tf_op jit(solution)/shard_map/final/pallas_call | solution.py:551
  51.9 7.1 %all_to_all.15 = f32[8,2,4]{2,1,0:T(2,128)S(1)} all-to-all(f32[8,2,4]{2,1,0:T(2,128)S(1)} %copy.8), channel_id=1, replica_groups=mesh['dom'=8,'pair'=4] {'dom'}, dimensions={0} | all-to-all | bytes 512 | tf_op jit(solution)/shard_map/all_to_all | solution.py:584
  59.0 0.6 reduce_sum.9
  (1 shorter events, 0.0 us)
Async XLA Ops:
  0.6 21.7 %copy-start = (bf16[2,1024,256]{2,1,0:T(8,128)(2,1)S(1)}, bf16[2,1024,256]{2,1,0:T(8,128)(2,1)}, u32[]{:S(2)}) copy-start(bf16[2,1024,256]{2,1,0:T(8,128)(2,1)} %constant.8.clone.refs_2_) | copy-start | bytes 3145732
  0.6 21.7 %copy-start.1 = (f32[64,256]{1,0:T(8,128)S(1)}, f32[64,256]{1,0:T(8,128)}, u32[]{:S(2)}) copy-start(f32[64,256]{1,0:T(8,128)} %constant.10.clone.refs_4_) | copy-start | bytes 196612
  0.7 21.7 %copy-start.2 = (f32[64,64]{1,0:T(8,128)S(1)}, f32[64,64]{1,0:T(8,128)}, u32[]{:S(2)}) copy-start(f32[64,64]{1,0:T(8,128)} %constant.9.clone.refs_3_) | copy-start | bytes 49156
  7.0 13.5 %all-to-all-start = ((bf16[8,3,64,128]{3,2,1,0:T(8,128)(2,1)}), bf16[8,3,64,128]{3,2,1,0:T(8,128)(2,1)S(1)}, u32[]{:S(2)}, u32[]{:S(2)}) async-start(bf16[8,3,64,128]{3,2,1,0:T(8,128)(2,1)} %bitcast.4), calls=%async_computation | async-start | bytes 786432 | tf_op jit(solution)/shard_map/all_to_all | solution.py:531
  12.2 21.5 %collective-permute-start.2 = (bf16[4,3,256,128]{3,2,1,0:T(8,128)(2,1)}, bf16[4,3,256,128]{3,2,1,0:T(8,128)(2,1)S(1)}, u32[]{:S(2)}, u32[]{:S(2)}) collective-permute-start(bf16[4,3,256,128]{3,2,1,0:T(8,128)(2,1)} %get-tuple-element.12), channel_id=1, source_target_pairs={{0,4},{4,0},{8,12},{12,8},{16,20},{20,16},{24,28},{28,24},{1,5},{5... | collective-permute-start | bytes 2359304 | tf_op jit(solution)/shard_map/ppermute | solution.py:525
  12.7 21.0 %collective-permute-start.3 = (bf16[4,3,256,128]{3,2,1,0:T(8,128)(2,1)}, bf16[4,3,256,128]{3,2,1,0:T(8,128)(2,1)S(1)}, u32[]{:S(2)}, u32[]{:S(2)}) collective-permute-start(bf16[4,3,256,128]{3,2,1,0:T(8,128)(2,1)} %get-tuple-element.13), channel_id=1, source_target_pairs={{4,8},{12,16},{20,24},{8,4},{16,12},{24,20},{5,9},{13,17},{21,25},... | collective-permute-start | bytes 2359304 | tf_op jit(solution)/shard_map/ppermute | solution.py:526
  20.6 1.7 %collective-permute-start = (bf16[8,3,64,128]{3,2,1,0:T(8,128)(2,1)S(1)}, bf16[8,3,64,128]{3,2,1,0:T(8,128)(2,1)S(1)}, u32[]{:S(2)}, u32[]{:S(2)}) collective-permute-start(bf16[8,3,64,128]{3,2,1,0:T(8,128)(2,1)S(1)} %all-to-all-done.refs_0_), channel_id=1, source_target_pairs={{4,0},{0,4},{12,8},{8,12},{20,16},{16,20},{28,24},{24,28},{5,1},{1... | collective-permute-start | bytes 1179656 | tf_op jit(solution)/shard_map/ppermute | solution.py:535
  20.6 1.3 %collective-permute-start.1 = (bf16[16,128]{1,0:T(8,128)(2,1)}, bf16[16,128]{1,0:T(8,128)(2,1)S(1)}, u32[]{:S(2)}, u32[]{:S(2)}) collective-permute-start(bf16[16,128]{1,0:T(8,128)(2,1)} %get-tuple-element.11), channel_id=1, source_target_pairs={{0,0},{1,1},{2,2},{3,3},{5,4},{6,5},{7,6},{4,7},{10,8},{11,9},{8,1... | collective-permute-start | bytes 12296 | tf_op jit(solution)/shard_map/ppermute | solution.py:529
  26.5 15.9 %all-to-all-start.1 = ((bf16[8,208,128]{2,1,0:T(8,128)(2,1)}), bf16[8,208,128]{2,1,0:T(8,128)(2,1)S(1)}, u32[]{:S(2)}, u32[]{:S(2)}) async-start(bf16[8,208,128]{2,1,0:T(8,128)(2,1)} %middle.1), calls=%async_computation.1 | async-start | bytes 851968 | tf_op jit(solution)/shard_map/all_to_all | solution.py:548

commit v3 on v2

--- a/solution.py
+++ b/solution.py
@@ -102,6 +102,9 @@
 
     copy = pltpu.make_async_copy(ids_hbm, ids, ids_sems.at[0])
     copy.start()
+    zero_rims(own)
+    zero_rims(once)
+    fill_band(band)
     copy.wait()
 
     def inputs(p):
@@ -110,9 +113,11 @@
             pltpu.make_async_copy(vir.at[ids[1, p]], vir_rows.at[p], in_sems.at[1, p]),
         )
 
+    def last_output(p):
+        return pltpu.make_async_copy(share.at[p], shares.at[p], out_sems.at[0, p])
+
     def outputs(p):
         return (
-            pltpu.make_async_copy(share.at[p], shares.at[p], out_sems.at[0, p]),
             pltpu.make_async_copy(packed.at[p, upper], first.at[p], out_sems.at[1, p]),
             pltpu.make_async_copy(packed.at[p, 1 - upper], second.at[p], out_sems.at[2, p]),
             pltpu.make_async_copy(v0s.at[p], v0_out.at[p], out_sems.at[3, p]),
@@ -130,10 +135,7 @@
     ids_tile[...] = tile.astype(BF16)
     ids_copy = pltpu.make_async_copy(ids_tile, ids_out, ids_sems.at[1])
     ids_copy.start()
-    fill_band(band)
     fill_children(fold, 0.5, 0)
-    zero_rims(own)
-    zero_rims(once)
 
     def one_pair(p, carry):
         for copy in inputs(p):
@@ -156,7 +158,7 @@
                 v0s[p, layer, rows] = v0
                 if layer == 0:
                     put(once, 0, row, (W * in_left) * centre)
-                    packed[p, 0, 0, rows] = centre.astype(BF16)
+                    packed[p, 0, 0, rows] = (W * W * centre).astype(BF16)
                     packed[p, 0, 1, rows] = v0.astype(BF16)
                 if layer == 1:
                     packed[p, 0, 2, rows] = v0.astype(BF16)
@@ -164,8 +166,11 @@
                     packed[p, 1, 2, rows] = v0.astype(BF16)
                 if layer == slab - 1:
                     put(once, slab + 1, row, (W * in_right) * centre)
-                    packed[p, 1, 0, rows] = centre.astype(BF16)
+                    packed[p, 1, 0, rows] = (W * W * centre).astype(BF16)
                     packed[p, 1, 1, rows] = v0.astype(BF16)
+
+        for copy in outputs(p):
+            copy.start()
 
         def twice(layer, row):
             if layer == -2:
@@ -205,14 +210,13 @@
             share[p, part, 0] = own_high[rows]
             share[p, part, 1] = own_low[rows]
             share[p, part, 2] = edge[rows]
-        for copy in outputs(p):
-            copy.start()
+        last_output(p).start()
         return carry
 
     lax.fori_loop(0, pairs, one_pair, 0)
     ids_copy.wait()
     for p in range(pairs):
-        for copy in outputs(p):
+        for copy in (*outputs(p), last_output(p)):
             copy.wait()
 
 
@@ -275,11 +279,8 @@
     for d in range(slabs):
         put(field_a, d, 0, smooth[d] + read(field_b, d, 0, rows_y))
 
-    def add_source(ref):
-        return lambda d, total: put(ref, d, 0, W * (total + read(source, d, 0, rows_y)))
-
-    apply(field_a, add_source(field_b))
-    apply(field_b, add_source(field_a))
+    apply(field_a, lambda d, total: put(field_b, d, 0, W * total))
+    apply(field_b, lambda d, total: put(field_a, d, 0, W * total + smooth[d]))
     zeros = jnp.zeros((rows_y, lanes), F32)
     before, here = zeros, swapped(field_a, 0)
     for d in range(slabs):
@@ -296,41 +297,34 @@
 
 
 def final_kernel(
-    ids_hbm, all_occ, all_vir, v0_hbm, coarse, first, second, out, panel,
-    ids, occ_rows, vir_rows, v0, band, spread, identity, own_field, wide, start, swept, kept,
+    all_occ, all_vir, v0_hbm, first_sent, second_sent, coarse, first, second, out, panel,
+    v0, edges, band, spread, identity, wide, start, swept, kept,
     occ, vir, late_vector, late_ids, turned, sums, ids_sem, in_sems, out_sems, late_sems,
 ):
     pairs, slab, rows_y, lanes = kept.shape
     groups = late_vector.shape[0]
     parts, part_rows = coarse.shape[0] // pairs, (coarse.shape[1] - 16) // 3
     in_left, in_right, even = sides()
-
-    ids_copy = pltpu.make_async_copy(ids_hbm, ids, ids_sem)
-    ids_copy.start()
+    upper = jnp.where(even, 1, 0)
 
     def inputs(p):
-        return [pltpu.make_async_copy(v0_hbm.at[p], v0.at[p], in_sems.at[0, p])]
-
-    def own_rows(p):
-        return [
-            pltpu.make_async_copy(all_occ.at[ids[0, p]], occ_rows.at[p], in_sems.at[1, p]),
-            pltpu.make_async_copy(all_vir.at[ids[1, p]], vir_rows.at[p], in_sems.at[2, p]),
-        ]
+        return (
+            pltpu.make_async_copy(v0_hbm.at[p], v0.at[p], in_sems.at[0, p]),
+            pltpu.make_async_copy(first_sent.at[p, 0], edges.at[p, upper], in_sems.at[1, p]),
+            pltpu.make_async_copy(second_sent.at[p, 0], edges.at[p, 1 - upper], in_sems.at[2, p]),
+        )
 
     def output(p):
         return pltpu.make_async_copy(kept.at[p], out.at[p], out_sems.at[p])
 
-    for copy in inputs(0):
-        copy.start()
-    ids_copy.wait()
-    for copy in own_rows(0):
-        copy.start()
-    for p in range(1, pairs):
-        for copy in inputs(p) + own_rows(p):
+    for p in range(pairs):
+        for copy in inputs(p):
             copy.start()
     late = [pltpu.make_async_copy(all_occ, occ, late_sems.at[0]), pltpu.make_async_copy(all_vir, vir, late_sems.at[1])]
-    for copy in late:
-        copy.start()
+    for turn in range(groups):
+        late_vector[turn] = coarse[turn, 3 * part_rows :].astype(F32).astype(jnp.int32)
+    ids_copy = pltpu.make_async_copy(late_vector, late_ids, ids_sem)
+    ids_copy.start()
     fill_band(band)
     fill_children(spread, 1.0, 1)
     line = lax.broadcasted_iota(jnp.int32, identity.shape, 0)
@@ -338,11 +332,7 @@
     zero_rims(start)
     zero_rims(swept)
 
-    def one_pair(p, carry):
-        for copy in inputs(p) + own_rows(p):
-            copy.wait()
-        for layer in range(slab):
-            own_field[layer] = occ_rows[p, layer].astype(F32) * vir_rows[p, layer].astype(F32)
+    def spread_out(p, carry):
         for part in range(parts):
             table = spread[...]
             at = p * parts + part
@@ -350,8 +340,20 @@
             beyond = own + dot(coarse[at, 2 * part_rows : 3 * part_rows], table)
             for at, value in enumerate((beyond[:, :lanes], own[:, :lanes], own[:, lanes:], beyond[:, lanes:])):
                 rows = 2 * part * part_rows
-                wide[at, pl.ds(rows, part_rows, stride=2), :] = value
-                wide[at, pl.ds(rows + 1, part_rows, stride=2), :] = value
+                wide[p, at, pl.ds(rows, part_rows, stride=2), :] = value
+                wide[p, at, pl.ds(rows + 1, part_rows, stride=2), :] = value
+        return carry
+
+    lax.fori_loop(0, pairs, spread_out, 0)
+
+    def one_pair(p, carry):
+        for copy in inputs(p):
+            copy.wait()
+
+        @pl.when(p == 0)
+        def _():
+            for copy in late:
+                copy.start()
 
         def halo(edge, index, row):
             rows = slice(row, row + STEP)
@@ -361,53 +363,49 @@
         for row in range(0, rows_y, STEP):
             rows = slice(row, row + STEP)
             for layer in range(slab):
-                value = v0[p, layer, rows] + wide[1 + layer // 2, rows]
+                value = v0[p, layer, rows]
                 if layer == 0:
-                    value = value + (W * W) * halo(0, 0, row)
+                    value = value + halo(0, 0, row)
+                    v0[p, layer, rows] = value
                 if layer == slab - 1:
-                    value = value + (W * W) * halo(1, 0, row)
-                put(start, layer + 2, row, value)
-            near = halo(0, 1, row) + (W * W) * own_field[0, rows] + wide[0, rows]
+                    value = value + halo(1, 0, row)
+                    v0[p, layer, rows] = value
+                put(start, layer + 2, row, value + wide[p, 1 + layer // 2, rows])
+            near = halo(0, 1, row) + edges[p, 0, rows].astype(F32) + wide[p, 0, rows]
             put(start, 1, row, in_left * near)
-            put(start, 0, row, in_left * (halo(0, 2, row) + wide[0, rows]))
-            near = halo(1, 1, row) + (W * W) * own_field[slab - 1, rows] + wide[3, rows]
+            put(start, 0, row, in_left * (halo(0, 2, row) + wide[p, 0, rows]))
+            near = halo(1, 1, row) + edges[p, 1, rows].astype(F32) + wide[p, 3, rows]
             put(start, slab + 2, row, in_right * near)
-            put(start, slab + 3, row, in_right * (halo(1, 2, row) + wide[3, rows]))
-
-        def sweep(ref, at, row, source):
+            put(start, slab + 3, row, in_right * (halo(1, 2, row) + wide[p, 3, rows]))
+
+        def sweep(ref, at, row):
             total = stencil(ref, at, row, band[...])
-            return W * (total + read(ref, at - 1, row) + read(ref, at + 1, row) + source)
+            return W * (total + read(ref, at - 1, row) + read(ref, at + 1, row))
 
         for row in range(0, rows_y, STEP):
-            rows = slice(row, row + STEP)
-            put(swept, 0, row, in_left * sweep(start, 1, row, halo(0, 0, row)))
+            put(swept, 0, row, in_left * sweep(start, 1, row))
             for layer in range(slab):
-                put(swept, layer + 1, row, sweep(start, layer + 2, row, own_field[layer, rows]))
-            put(swept, slab + 1, row, in_right * sweep(start, slab + 2, row, halo(1, 0, row)))
+                put(swept, layer + 1, row, sweep(start, layer + 2, row))
+            put(swept, slab + 1, row, in_right * sweep(start, slab + 2, row))
         for row in range(0, rows_y, STEP):
             rows = slice(row, row + STEP)
             for layer in range(slab):
-                value = sweep(swept, layer + 1, row, own_field[layer, rows]).astype(BF16)
-                kept[p, layer, rows] = value
+                kept[p, layer, rows] = (sweep(swept, layer + 1, row) + v0[p, layer, rows]).astype(BF16)
         output(p).start()
+        half = lanes // 2
+        for layer in range(slab):
+            value = dot(identity[...], kept[p, layer], ((1,), (1,))).astype(BF16)
+            column = 2 * layer * rows_y
+            turned[p, :, column : column + rows_y] = value[:half]
+            turned[p, :, column + rows_y : column + 2 * rows_y] = value[half:]
         return carry
 
     lax.fori_loop(0, pairs, one_pair, 0)
-
+    ids_copy.wait()
     for copy in late:
         copy.wait()
-    for turn in range(groups):
-        late_vector[turn] = coarse[turn, 3 * part_rows :].astype(F32).astype(jnp.int32)
-    copy = pltpu.make_async_copy(late_vector, late_ids, ids_sem)
-    copy.start()
     half = lanes // 2
-    for q in range(pairs):
-        for layer in range(slab):
-            value = dot(identity[...], kept[q, layer], ((1,), (1,))).astype(BF16)
-            column = 2 * layer * rows_y
-            turned[q * half : (q + 1) * half, column : column + rows_y] = value[:half]
-            turned[q * half : (q + 1) * half, column + rows_y : column + 2 * rows_y] = value[half:]
-    copy.wait()
+    fields = turned[...].reshape(pairs * half, 2 * slab * rows_y)
     count = groups * pairs
     first_row = lax.axis_index("pair") * pairs
     left = lax.broadcasted_iota(jnp.int32, (rows_y, lanes), 1) < half
@@ -430,7 +428,7 @@
                 upper_row.append(jnp.where(left, one, pltpu.roll(two, half, 1)))
                 lower_row.append(jnp.where(left, pltpu.roll(one, half, 1), two))
             pieces += [jnp.concatenate(upper_row, axis=1), jnp.concatenate(lower_row, axis=1)]
-        product = dot(turned[...], jnp.concatenate(pieces, axis=0))
+        product = dot(fields, jnp.concatenate(pieces, axis=0))
         row = first_row + p
         row = jnp.where(row >= count, row - count, row) // 2
         for q in range(pairs):
@@ -550,19 +548,16 @@
     count = groups * pairs
     potentials, panel = pl.pallas_call(
         final_kernel,
-        in_specs=[hbm] * 4 + [vmem] * 3,
+        in_specs=[hbm] * 5 + [vmem] * 3,
         out_specs=[hbm, vmem],
         out_shape=[pltpu.HBM(own, BF16), jax.ShapeDtypeStruct((2, count // 2, pairs), F32)],
         scratch_shapes=[
-            pltpu.SMEM(ids.shape, jnp.int32),
-            pltpu.VMEM(own, BF16),
-            pltpu.VMEM(own, BF16),
             pltpu.VMEM(own, F32),
+            pltpu.VMEM((pairs, 2, rows_y, lanes), BF16),
             pltpu.VMEM((2 * lanes, lanes), BF16),
             pltpu.VMEM((lanes, 2 * lanes), BF16),
             pltpu.VMEM((lanes, lanes), BF16),
-            pltpu.VMEM((slab, rows_y, lanes), F32),
-            pltpu.VMEM((4, rows_y, lanes), F32),
+            pltpu.VMEM((pairs, 4, rows_y, lanes), F32),
             pltpu.VMEM((slab + 4, padded_y, lanes), F32),
             pltpu.VMEM((slab + 2, padded_y, lanes), F32),
             pltpu.VMEM(own, BF16),
@@ -570,7 +565,7 @@
             pltpu.VMEM(virtual.shape, BF16),
             pltpu.VMEM((groups,) + tile, jnp.int32),
             pltpu.SMEM((groups,) + tile, jnp.int32),
-            pltpu.VMEM((pairs * lanes // 2, 2 * slab * rows_y), BF16),
+            pltpu.VMEM((pairs, lanes // 2, 2 * slab * rows_y), BF16),
             pltpu.VMEM((count // 2, pairs, lanes), F32),
             pltpu.SemaphoreType.DMA,
             pltpu.SemaphoreType.DMA((3, pairs)),
@@ -579,7 +574,7 @@
         ],
         compiler_params=pltpu.CompilerParams(vmem_limit_bytes=24 * MIB),
         name="final",
-    )(in_hbm(ids), in_hbm(occupied), in_hbm(virtual), in_hbm(v0), returned, first_halo, second_halo)
+    )(*[in_hbm(x) for x in (occupied, virtual, v0, first, second)], returned, first_halo, second_halo)
     panel = jnp.swapaxes(panel, 0, 1).reshape(slabs, count // slabs, pairs)
     return potentials, jnp.sum(lax.all_to_all(panel, "dom", 0, 0), axis=0)
 

time: 60 us -> 57.5 us (0.958)
  Pallas kernels: 20.1 us -> 17.5 us
    pallas_call x1, Pallas kernels: 9.55 us -> 7.17 us  [shards(): pl.pallas_call(final_kernel, in_specs=[hbm] * 5 + [vmem] * 3, out_specs=[...]
where the time goes in v3:
time: 57.5 us; the launch traced here: 57 us
  Pallas kernels  17.5 us (30%)
  waiting for transfers between devices  16.2 us (28%)
  starting transfers between devices  14.9 us (26%)
  blocking collectives  7.07 us (12%)
  between operations  0.71 us (1%)
  other arithmetic  0.58 us (1%)
    all_to_all x1, waiting for transfers between devices, shards(): returned = lax.all_to_all(smoothed, 'dom', 0, 0)  8.68 us
    all_to_all x1, starting transfers between devices, shards(): returned = lax.all_to_all(smoothed, 'dom', 0, 0)  7.2 us
    pallas_call x1, Pallas kernels, shards(): pl.pallas_call(final_kernel, in_specs=[hbm] * 5 + [vmem] * 3, out_specs=[...  7.17 us
    all_to_all x1, waiting for transfers between devices, shards(): lax.all_to_all(shares.reshape(slabs, 3, part_rows, lanes), 'dom', 0, 0)  7.13 us
    all_to_all x1, blocking collectives, shards(): return (potentials, jnp.sum(lax.all_to_all(panel, 'dom', 0, 0), axis=0))  7.07 us
    pallas_call x1, Pallas kernels, shards(): pl.pallas_call(source_kernel, in_specs=[hbm, hbm, hbm], out_specs=[hbm] *...  6.16 us
    all_to_all x1, starting transfers between devices, shards(): lax.all_to_all(shares.reshape(slabs, 3, part_rows, lanes), 'dom', 0, 0)  5.18 us
    pallas_call x1, Pallas kernels, shards(): pl.pallas_call(middle_kernel, in_specs=[vmem] * (parts + 4), out_specs=vm...  4.21 us
  transfers between devices with their start and end apart: 6, of which 3 were waited for; matrix products, arithmetic and copies ran while one was open for 0% of the time, Pallas kernels for 7%

profile of v3, /device:TPU:0, one launch (start us, length us, event | category | flops | bytes accessed | tf_op | source)
XLA Modules:
  0.0 57.0 jit_solution(10363030156715319278)
XLA Ops:
  0.6 0.0 copy-start
  0.6 0.0 copy-start.1
  0.7 0.0 copy-start.2
  0.7 6.2 %source.1 = (bf16[4,2,3,64,128]{4,3,2,1,0:T(8,128)(2,1)}, bf16[4,3,256,128]{3,2,1,0:T(8,128)(2,1)}, bf16[4,3,256,128]{3,2,1,0:T(8,128)(2,1)}, f32[4,4,256,128]{3,2,1,0:T(8,128)}, bf16[16,128]{1,0:T(8,128)(2,1)}) custom-call(s32[2,4]{1,0:T(2,128)} %bitcast.5, bf16[12,4,256,128]{3,2,1,0:T(8,128)(2,1)} %all_occ.1, bf16[12,4,256,128]{3,2,1,0:T(8,128)(2,1)} %all_vir.1), custom_call_target="tpu_custom_call" | custom-call | tf_op jit(solution)/shard_map/source/pallas_call | solution.py:488
  6.8 5.2 %all-to-all-start = ((bf16[8,3,64,128]{3,2,1,0:T(8,128)(2,1)}), bf16[8,3,64,128]{3,2,1,0:T(8,128)(2,1)S(1)}, u32[]{:S(2)}, u32[]{:S(2)}) async-start(bf16[8,3,64,128]{3,2,1,0:T(8,128)(2,1)} %bitcast.4), calls=%async_computation | async-start | bytes 786432 | tf_op jit(solution)/shard_map/all_to_all | solution.py:529
  12.0 0.5 collective-permute-start.2
  12.5 0.7 %collective-permute-start.3 = (bf16[4,3,256,128]{3,2,1,0:T(8,128)(2,1)}, bf16[4,3,256,128]{3,2,1,0:T(8,128)(2,1)S(1)}, u32[]{:S(2)}, u32[]{:S(2)}) collective-permute-start(bf16[4,3,256,128]{3,2,1,0:T(8,128)(2,1)} %get-tuple-element.11.second_sent), channel_id=1, source_target_pairs={{4,8},{12,16},{20,24},{8,4},{16,12},{24,20},{5,9},{13,17},{21,25},... | collective-permute-start | bytes 2359304 | tf_op jit(solution)/shard_map/ppermute | solution.py:524
  13.2 7.1 %all-to-all-done.refs_0_ = bf16[8,3,64,128]{3,2,1,0:T(8,128)(2,1)S(1)} async-done(((bf16[8,3,64,128]{3,2,1,0:T(8,128)(2,1)}), bf16[8,3,64,128]{3,2,1,0:T(8,128)(2,1)S(1)}, u32[]{:S(2)}, u32[]{:S(2)}) %all-to-all-start) | async-done | bytes 393248 | tf_op jit(solution)/shard_map/all_to_all | solution.py:529
  20.4 0.0 collective-permute-start
  20.4 1.3 %collective-permute-start.1 = (bf16[16,128]{1,0:T(8,128)(2,1)}, bf16[16,128]{1,0:T(8,128)(2,1)S(1)}, u32[]{:S(2)}, u32[]{:S(2)}) collective-permute-start(bf16[16,128]{1,0:T(8,128)(2,1)} %get-tuple-element.13), channel_id=1, source_target_pairs={{0,0},{1,1},{2,2},{3,3},{5,4},{6,5},{7,6},{4,7},{10,8},{11,9},{8,1... | collective-permute-start | bytes 12296 | tf_op jit(solution)/shard_map/ppermute | solution.py:527
  21.7 0.0 collective-permute-done.1.refs_5_
  21.7 0.4 collective-permute-done.refs_1_
  22.1 0.0 copy-done
  22.1 0.0 copy-done.1
  22.1 0.0 copy-done.2
  22.1 4.2 %middle.1 = bf16[8,208,128]{2,1,0:T(8,128)(2,1)} custom-call(bf16[8,3,64,128]{3,2,1,0:T(8,128)(2,1)S(1)} %all-to-all-done.refs_0_, bf16[8,3,64,128]{3,2,1,0:T(8,128)(2,1)S(1)} %collective-permute-done.refs_1_, bf16[2,1024,256]{2,1,0:T(8,128)(2,1)S(1)} %copy-done, f32[64,64]{1,0:T(8,128)S(1)} %copy-done.2, f32[64,256]{1,0:T(8,128)S(1)} %copy-done.1, ...), custom_call_target="tpu_custom_call" | custom-call | tf_op jit(solution)/shard_map/middle/pallas_call | solution.py:537
  26.3 7.2 %all-to-all-start.1 = ((bf16[8,208,128]{2,1,0:T(8,128)(2,1)}), bf16[8,208,128]{2,1,0:T(8,128)(2,1)S(1)}, u32[]{:S(2)}, u32[]{:S(2)}) async-start(bf16[8,208,128]{2,1,0:T(8,128)(2,1)} %middle.1), calls=%async_computation.1 | async-start | bytes 851968 | tf_op jit(solution)/shard_map/all_to_all | solution.py:546
  33.5 0.0 collective-permute-done.2.first
  33.5 0.0 collective-permute-done.3.second
  33.5 8.7 %all-to-all-done.1.coarse = bf16[8,208,128]{2,1,0:T(8,128)(2,1)S(1)} async-done(((bf16[8,208,128]{2,1,0:T(8,128)(2,1)}), bf16[8,208,128]{2,1,0:T(8,128)(2,1)S(1)}, u32[]{:S(2)}, u32[]{:S(2)}) %all-to-all-start.1) | async-done | bytes 426016 | tf_op jit(solution)/shard_map/all_to_all | solution.py:546
  42.2 7.2 %final.1 = (bf16[4,4,256,128]{3,2,1,0:T(8,128)(2,1)}, f32[2,8,4]{2,1,0:T(8,128)S(1)}) custom-call(bf16[12,4,256,128]{3,2,1,0:T(8,128)(2,1)} %all_occ.1, bf16[12,4,256,128]{3,2,1,0:T(8,128)(2,1)} %all_vir.1, f32[4,4,256,128]{3,2,1,0:T(8,128)} %get-tuple-element.9.v0_hbm, bf16[4,3,256,128]{3,2,1,0:T(8,128)(2,1)} %get-tuple-element.10.first_sent, ...), custom_call_target="tpu_custom_call" | custom-call | tf_op jit(solution)/shard_map/final/pallas_call | solution.py:549
  49.4 7.1 %all_to_all.15 = f32[8,2,4]{2,1,0:T(2,128)S(1)} all-to-all(f32[8,2,4]{2,1,0:T(2,128)S(1)} %copy.8), channel_id=1, replica_groups=mesh['dom'=8,'pair'=4] {'dom'}, dimensions={0} | all-to-all | bytes 512 | tf_op jit(solution)/shard_map/all_to_all | solution.py:579
  56.5 0.6 %reduce_sum.9 = f32[2,4]{1,0:T(2,128)} reduce(f32[8,2,4]{2,1,0:T(2,128)S(1)} %all_to_all.15, f32[]{:T(128)} %constant.3.clone.1), dimensions={0}, to_apply=%region_0.0 | reduce | flops 56 | bytes 292 | tf_op jit(solution)/shard_map/reduce_sum | solution.py:579
  (1 shorter events, 0.0 us)
Async XLA Ops:
  0.6 21.5 %copy-start = (bf16[2,1024,256]{2,1,0:T(8,128)(2,1)S(1)}, bf16[2,1024,256]{2,1,0:T(8,128)(2,1)}, u32[]{:S(2)}) copy-start(bf16[2,1024,256]{2,1,0:T(8,128)(2,1)} %constant.8.clone.refs_2_) | copy-start | bytes 3145732
  0.6 21.4 %copy-start.1 = (f32[64,256]{1,0:T(8,128)S(1)}, f32[64,256]{1,0:T(8,128)}, u32[]{:S(2)}) copy-start(f32[64,256]{1,0:T(8,128)} %constant.10.clone.refs_4_) | copy-start | bytes 196612
  0.7 21.4 %copy-start.2 = (f32[64,64]{1,0:T(8,128)S(1)}, f32[64,64]{1,0:T(8,128)}, u32[]{:S(2)}) copy-start(f32[64,64]{1,0:T(8,128)} %constant.9.clone.refs_3_) | copy-start | bytes 49156
  6.8 13.5 %all-to-all-start = ((bf16[8,3,64,128]{3,2,1,0:T(8,128)(2,1)}), bf16[8,3,64,128]{3,2,1,0:T(8,128)(2,1)S(1)}, u32[]{:S(2)}, u32[]{:S(2)}) async-start(bf16[8,3,64,128]{3,2,1,0:T(8,128)(2,1)} %bitcast.4), calls=%async_computation | async-start | bytes 786432 | tf_op jit(solution)/shard_map/all_to_all | solution.py:529
  12.0 21.5 %collective-permute-start.2 = (bf16[4,3,256,128]{3,2,1,0:T(8,128)(2,1)}, bf16[4,3,256,128]{3,2,1,0:T(8,128)(2,1)S(1)}, u32[]{:S(2)}, u32[]{:S(2)}) collective-permute-start(bf16[4,3,256,128]{3,2,1,0:T(8,128)(2,1)} %get-tuple-element.10.first_sent), channel_id=1, source_target_pairs={{0,4},{4,0},{8,12},{12,8},{16,20},{20,16},{24,28},{28,24},{1,5},{5... | collective-permute-start | bytes 2359304 | tf_op jit(solution)/shard_map/ppermute | solution.py:523
  12.5 21.0 %collective-permute-start.3 = (bf16[4,3,256,128]{3,2,1,0:T(8,128)(2,1)}, bf16[4,3,256,128]{3,2,1,0:T(8,128)(2,1)S(1)}, u32[]{:S(2)}, u32[]{:S(2)}) collective-permute-start(bf16[4,3,256,128]{3,2,1,0:T(8,128)(2,1)} %get-tuple-element.11.second_sent), channel_id=1, source_target_pairs={{4,8},{12,16},{20,24},{8,4},{16,12},{24,20},{5,9},{13,17},{21,25},... | collective-permute-start | bytes 2359304 | tf_op jit(solution)/shard_map/ppermute | solution.py:524
  20.4 1.7 %collective-permute-start = (bf16[8,3,64,128]{3,2,1,0:T(8,128)(2,1)S(1)}, bf16[8,3,64,128]{3,2,1,0:T(8,128)(2,1)S(1)}, u32[]{:S(2)}, u32[]{:S(2)}) collective-permute-start(bf16[8,3,64,128]{3,2,1,0:T(8,128)(2,1)S(1)} %all-to-all-done.refs_0_), channel_id=1, source_target_pairs={{4,0},{0,4},{12,8},{8,12},{20,16},{16,20},{28,24},{24,28},{5,1},{1... | collective-permute-start | bytes 1179656 | tf_op jit(solution)/shard_map/ppermute | solution.py:533
  20.4 1.3 %collective-permute-start.1 = (bf16[16,128]{1,0:T(8,128)(2,1)}, bf16[16,128]{1,0:T(8,128)(2,1)S(1)}, u32[]{:S(2)}, u32[]{:S(2)}) collective-permute-start(bf16[16,128]{1,0:T(8,128)(2,1)} %get-tuple-element.13), channel_id=1, source_target_pairs={{0,0},{1,1},{2,2},{3,3},{5,4},{6,5},{7,6},{4,7},{10,8},{11,9},{8,1... | collective-permute-start | bytes 12296 | tf_op jit(solution)/shard_map/ppermute | solution.py:527
  26.3 15.9 %all-to-all-start.1 = ((bf16[8,208,128]{2,1,0:T(8,128)(2,1)}), bf16[8,208,128]{2,1,0:T(8,128)(2,1)S(1)}, u32[]{:S(2)}, u32[]{:S(2)}) async-start(bf16[8,208,128]{2,1,0:T(8,128)(2,1)} %middle.1), calls=%async_computation.1 | async-start | bytes 851968 | tf_op jit(solution)/shard_map/all_to_all | solution.py:546

commit v4 on v3

--- a/solution.py
+++ b/solution.py
@@ -93,7 +93,7 @@
 
 def source_kernel(
     ids_hbm, occ, vir, shares, first, second, v0_out, ids_out,
-    ids, occ_rows, vir_rows, band, fold, own, once, v0s, sums, packed, share, ids_tile, ids_sems, in_sems, out_sems,
+    ids, occ_rows, vir_rows, band, fold, own, once, beyond, v0s, sums, packed, share, ids_tile, ids_sems, in_sems, out_sems,
 ):
     pairs, slab, rows_y, lanes = occ_rows.shape
     parts, part_rows = share.shape[1], share.shape[3]
@@ -148,6 +148,10 @@
             for layer in range(slab):
                 centre = read(own, layer, row)
                 total = stencil(own, layer, row, band[...])
+                if layer == 0:
+                    beyond[0, rows] = (W * in_left) * total
+                if layer == slab - 1:
+                    beyond[1, rows] = (W * in_right) * total
                 if layer > 0:
                     total = total + read(own, layer - 1, row)
                 if layer < slab - 1:
@@ -177,13 +181,12 @@
                 return read(once, 0, row)
             if layer == slab + 1:
                 return read(once, slab + 1, row)
+            if layer == -1:
+                return beyond[0, row : row + STEP] + read(once, 1, row)
+            if layer == slab:
+                return beyond[1, row : row + STEP] + read(once, slab, row)
             at = layer + 1
-            total = stencil(once, at, row, band[...])
-            if at > 0:
-                total = total + read(once, at - 1, row)
-            if at < slab + 1:
-                total = total + read(once, at + 1, row)
-            return total
+            return stencil(once, at, row, band[...]) + read(once, at - 1, row) + read(once, at + 1, row)
 
         for row in range(0, rows_y, STEP):
             for coarse in range(slab // 2 + 2):
@@ -504,6 +507,7 @@
             pltpu.VMEM((2 * lanes, lanes), BF16),
             pltpu.VMEM((slab, padded_y, lanes), F32),
             pltpu.VMEM((slab + 2, padded_y, lanes), F32),
+            pltpu.VMEM((2, rows_y, lanes), F32),
             pltpu.VMEM(own, F32),
             pltpu.VMEM((slab // 2 + 2, rows_y, lanes), F32),
             pltpu.VMEM((pairs, 2, 3, rows_y, lanes), BF16),

time: 57.5 us -> 57 us (level)
  no operation moved by 1% of the time
where the time goes in v4:
time: 57 us; the launch traced here: 56.6 us
  Pallas kernels  17.1 us (30%)
  waiting for transfers between devices  16.2 us (28%)
  starting transfers between devices  14.9 us (26%)
  blocking collectives  7.07 us (12%)
  between operations  0.71 us (1%)
  other arithmetic  0.58 us (1%)
    all_to_all x1, waiting for transfers between devices, shards(): returned = lax.all_to_all(smoothed, 'dom', 0, 0)  8.68 us
    all_to_all x1, starting transfers between devices, shards(): returned = lax.all_to_all(smoothed, 'dom', 0, 0)  7.21 us
    pallas_call x1, Pallas kernels, shards(): pl.pallas_call(final_kernel, in_specs=[hbm] * 5 + [vmem] * 3, out_specs=[...  7.17 us
    all_to_all x1, waiting for transfers between devices, shards(): lax.all_to_all(shares.reshape(slabs, 3, part_rows, lanes), 'dom', 0, 0)  7.13 us
    all_to_all x1, blocking collectives, shards(): return (potentials, jnp.sum(lax.all_to_all(panel, 'dom', 0, 0), axis=0))  7.07 us
    pallas_call x1, Pallas kernels, shards(): pl.pallas_call(source_kernel, in_specs=[hbm, hbm, hbm], out_specs=[hbm] *...  5.71 us
    all_to_all x1, starting transfers between devices, shards(): lax.all_to_all(shares.reshape(slabs, 3, part_rows, lanes), 'dom', 0, 0)  5.18 us
    pallas_call x1, Pallas kernels, shards(): pl.pallas_call(middle_kernel, in_specs=[vmem] * (parts + 4), out_specs=vm...  4.2 us
  transfers between devices with their start and end apart: 6, of which 3 were waited for; matrix products, arithmetic and copies ran while one was open for 0% of the time, Pallas kernels for 7%

profile of v4, /device:TPU:0, one launch (start us, length us, event | category | flops | bytes accessed | tf_op | source)
XLA Modules:
  0.0 56.6 jit_solution(6619386748995439647)
XLA Ops:
  0.6 0.0 copy-start
  0.6 0.0 copy-start.1
  0.7 0.0 copy-start.2
  0.7 5.7 %source.1 = (bf16[4,2,3,64,128]{4,3,2,1,0:T(8,128)(2,1)}, bf16[4,3,256,128]{3,2,1,0:T(8,128)(2,1)}, bf16[4,3,256,128]{3,2,1,0:T(8,128)(2,1)}, f32[4,4,256,128]{3,2,1,0:T(8,128)}, bf16[16,128]{1,0:T(8,128)(2,1)}) custom-call(s32[2,4]{1,0:T(2,128)} %bitcast.5, bf16[12,4,256,128]{3,2,1,0:T(8,128)(2,1)} %all_occ.1, bf16[12,4,256,128]{3,2,1,0:T(8,128)(2,1)} %all_vir.1), custom_call_target="tpu_custom_call" | custom-call | tf_op jit(solution)/shard_map/source/pallas_call | solution.py:491
  6.4 5.2 %all-to-all-start = ((bf16[8,3,64,128]{3,2,1,0:T(8,128)(2,1)}), bf16[8,3,64,128]{3,2,1,0:T(8,128)(2,1)S(1)}, u32[]{:S(2)}, u32[]{:S(2)}) async-start(bf16[8,3,64,128]{3,2,1,0:T(8,128)(2,1)} %bitcast.4), calls=%async_computation | async-start | bytes 786432 | tf_op jit(solution)/shard_map/all_to_all | solution.py:533
  11.6 0.5 collective-permute-start.2
  12.1 0.7 %collective-permute-start.3 = (bf16[4,3,256,128]{3,2,1,0:T(8,128)(2,1)}, bf16[4,3,256,128]{3,2,1,0:T(8,128)(2,1)S(1)}, u32[]{:S(2)}, u32[]{:S(2)}) collective-permute-start(bf16[4,3,256,128]{3,2,1,0:T(8,128)(2,1)} %get-tuple-element.11.second_sent), channel_id=1, source_target_pairs={{4,8},{12,16},{20,24},{8,4},{16,12},{24,20},{5,9},{13,17},{21,25},... | collective-permute-start | bytes 2359304 | tf_op jit(solution)/shard_map/ppermute | solution.py:528
  12.8 7.1 %all-to-all-done.refs_0_ = bf16[8,3,64,128]{3,2,1,0:T(8,128)(2,1)S(1)} async-done(((bf16[8,3,64,128]{3,2,1,0:T(8,128)(2,1)}), bf16[8,3,64,128]{3,2,1,0:T(8,128)(2,1)S(1)}, u32[]{:S(2)}, u32[]{:S(2)}) %all-to-all-start) | async-done | bytes 393248 | tf_op jit(solution)/shard_map/all_to_all | solution.py:533
  19.9 0.0 collective-permute-start
  19.9 1.3 %collective-permute-start.1 = (bf16[16,128]{1,0:T(8,128)(2,1)}, bf16[16,128]{1,0:T(8,128)(2,1)S(1)}, u32[]{:S(2)}, u32[]{:S(2)}) collective-permute-start(bf16[16,128]{1,0:T(8,128)(2,1)} %get-tuple-element.13), channel_id=1, source_target_pairs={{0,0},{1,1},{2,2},{3,3},{5,4},{6,5},{7,6},{4,7},{10,8},{11,9},{8,1... | collective-permute-start | bytes 12296 | tf_op jit(solution)/shard_map/ppermute | solution.py:531
  21.2 0.0 collective-permute-done.1.refs_5_
  21.2 0.4 collective-permute-done.refs_1_
  21.6 0.0 copy-done
  21.6 0.0 copy-done.1
  21.6 0.0 copy-done.2
  21.6 4.2 %middle.1 = bf16[8,208,128]{2,1,0:T(8,128)(2,1)} custom-call(bf16[8,3,64,128]{3,2,1,0:T(8,128)(2,1)S(1)} %all-to-all-done.refs_0_, bf16[8,3,64,128]{3,2,1,0:T(8,128)(2,1)S(1)} %collective-permute-done.refs_1_, bf16[2,1024,256]{2,1,0:T(8,128)(2,1)S(1)} %copy-done, f32[64,64]{1,0:T(8,128)S(1)} %copy-done.2, f32[64,256]{1,0:T(8,128)S(1)} %copy-done.1, ...), custom_call_target="tpu_custom_call" | custom-call | tf_op jit(solution)/shard_map/middle/pallas_call | solution.py:541
  25.8 7.2 %all-to-all-start.1 = ((bf16[8,208,128]{2,1,0:T(8,128)(2,1)}), bf16[8,208,128]{2,1,0:T(8,128)(2,1)S(1)}, u32[]{:S(2)}, u32[]{:S(2)}) async-start(bf16[8,208,128]{2,1,0:T(8,128)(2,1)} %middle.1), calls=%async_computation.1 | async-start | bytes 851968 | tf_op jit(solution)/shard_map/all_to_all | solution.py:550
  33.1 0.0 collective-permute-done.2.first
  33.1 0.0 collective-permute-done.3.second
  33.1 8.7 %all-to-all-done.1.coarse = bf16[8,208,128]{2,1,0:T(8,128)(2,1)S(1)} async-done(((bf16[8,208,128]{2,1,0:T(8,128)(2,1)}), bf16[8,208,128]{2,1,0:T(8,128)(2,1)S(1)}, u32[]{:S(2)}, u32[]{:S(2)}) %all-to-all-start.1) | async-done | bytes 426016 | tf_op jit(solution)/shard_map/all_to_all | solution.py:550
  41.7 7.2 %final.1 = (bf16[4,4,256,128]{3,2,1,0:T(8,128)(2,1)}, f32[2,8,4]{2,1,0:T(8,128)S(1)}) custom-call(bf16[12,4,256,128]{3,2,1,0:T(8,128)(2,1)} %all_occ.1, bf16[12,4,256,128]{3,2,1,0:T(8,128)(2,1)} %all_vir.1, f32[4,4,256,128]{3,2,1,0:T(8,128)} %get-tuple-element.9.v0_hbm, bf16[4,3,256,128]{3,2,1,0:T(8,128)(2,1)} %get-tuple-element.10.first_sent, ...), custom_call_target="tpu_custom_call" | custom-call | tf_op jit(solution)/shard_map/final/pallas_call | solution.py:553
  48.9 7.1 %all_to_all.15 = f32[8,2,4]{2,1,0:T(2,128)S(1)} all-to-all(f32[8,2,4]{2,1,0:T(2,128)S(1)} %copy.8), channel_id=1, replica_groups=mesh['dom'=8,'pair'=4] {'dom'}, dimensions={0} | all-to-all | bytes 512 | tf_op jit(solution)/shard_map/all_to_all | solution.py:583
  56.0 0.6 %reduce_sum.9 = f32[2,4]{1,0:T(2,128)} reduce(f32[8,2,4]{2,1,0:T(2,128)S(1)} %all_to_all.15, f32[]{:T(128)} %constant.3.clone.1), dimensions={0}, to_apply=%region_0.0 | reduce | flops 56 | bytes 292 | tf_op jit(solution)/shard_map/reduce_sum | solution.py:583
  (1 shorter events, 0.0 us)
Async XLA Ops:
  0.6 21.0 %copy-start = (bf16[2,1024,256]{2,1,0:T(8,128)(2,1)S(1)}, bf16[2,1024,256]{2,1,0:T(8,128)(2,1)}, u32[]{:S(2)}) copy-start(bf16[2,1024,256]{2,1,0:T(8,128)(2,1)} %constant.8.clone.refs_2_) | copy-start | bytes 3145732
  0.6 21.0 %copy-start.1 = (f32[64,256]{1,0:T(8,128)S(1)}, f32[64,256]{1,0:T(8,128)}, u32[]{:S(2)}) copy-start(f32[64,256]{1,0:T(8,128)} %constant.10.clone.refs_4_) | copy-start | bytes 196612
  0.7 21.0 %copy-start.2 = (f32[64,64]{1,0:T(8,128)S(1)}, f32[64,64]{1,0:T(8,128)}, u32[]{:S(2)}) copy-start(f32[64,64]{1,0:T(8,128)} %constant.9.clone.refs_3_) | copy-start | bytes 49156
  6.4 13.5 %all-to-all-start = ((bf16[8,3,64,128]{3,2,1,0:T(8,128)(2,1)}), bf16[8,3,64,128]{3,2,1,0:T(8,128)(2,1)S(1)}, u32[]{:S(2)}, u32[]{:S(2)}) async-start(bf16[8,3,64,128]{3,2,1,0:T(8,128)(2,1)} %bitcast.4), calls=%async_computation | async-start | bytes 786432 | tf_op jit(solution)/shard_map/all_to_all | solution.py:533
  11.6 21.5 %collective-permute-start.2 = (bf16[4,3,256,128]{3,2,1,0:T(8,128)(2,1)}, bf16[4,3,256,128]{3,2,1,0:T(8,128)(2,1)S(1)}, u32[]{:S(2)}, u32[]{:S(2)}) collective-permute-start(bf16[4,3,256,128]{3,2,1,0:T(8,128)(2,1)} %get-tuple-element.10.first_sent), channel_id=1, source_target_pairs={{0,4},{4,0},{8,12},{12,8},{16,20},{20,16},{24,28},{28,24},{1,5},{5... | collective-permute-start | bytes 2359304 | tf_op jit(solution)/shard_map/ppermute | solution.py:527
  12.1 21.0 %collective-permute-start.3 = (bf16[4,3,256,128]{3,2,1,0:T(8,128)(2,1)}, bf16[4,3,256,128]{3,2,1,0:T(8,128)(2,1)S(1)}, u32[]{:S(2)}, u32[]{:S(2)}) collective-permute-start(bf16[4,3,256,128]{3,2,1,0:T(8,128)(2,1)} %get-tuple-element.11.second_sent), channel_id=1, source_target_pairs={{4,8},{12,16},{20,24},{8,4},{16,12},{24,20},{5,9},{13,17},{21,25},... | collective-permute-start | bytes 2359304 | tf_op jit(solution)/shard_map/ppermute | solution.py:528
  19.9 1.7 %collective-permute-start = (bf16[8,3,64,128]{3,2,1,0:T(8,128)(2,1)S(1)}, bf16[8,3,64,128]{3,2,1,0:T(8,128)(2,1)S(1)}, u32[]{:S(2)}, u32[]{:S(2)}) collective-permute-start(bf16[8,3,64,128]{3,2,1,0:T(8,128)(2,1)S(1)} %all-to-all-done.refs_0_), channel_id=1, source_target_pairs={{4,0},{0,4},{12,8},{8,12},{20,16},{16,20},{28,24},{24,28},{5,1},{1... | collective-permute-start | bytes 1179656 | tf_op jit(solution)/shard_map/ppermute | solution.py:537
  19.9 1.3 %collective-permute-start.1 = (bf16[16,128]{1,0:T(8,128)(2,1)}, bf16[16,128]{1,0:T(8,128)(2,1)S(1)}, u32[]{:S(2)}, u32[]{:S(2)}) collective-permute-start(bf16[16,128]{1,0:T(8,128)(2,1)} %get-tuple-element.13), channel_id=1, source_target_pairs={{0,0},{1,1},{2,2},{3,3},{5,4},{6,5},{7,6},{4,7},{10,8},{11,9},{8,1... | collective-permute-start | bytes 12296 | tf_op jit(solution)/shard_map/ppermute | solution.py:531
  25.8 15.9 %all-to-all-start.1 = ((bf16[8,208,128]{2,1,0:T(8,128)(2,1)}), bf16[8,208,128]{2,1,0:T(8,128)(2,1)S(1)}, u32[]{:S(2)}, u32[]{:S(2)}) async-start(bf16[8,208,128]{2,1,0:T(8,128)(2,1)} %middle.1), calls=%async_computation.1 | async-start | bytes 851968 | tf_op jit(solution)/shard_map/all_to_all | solution.py:550

commit v5 on v4

--- a/solution.py
+++ b/solution.py
@@ -92,15 +92,15 @@
 
 
 def source_kernel(
-    ids_hbm, occ, vir, shares, first, second, v0_out, ids_out,
-    ids, occ_rows, vir_rows, band, fold, own, once, beyond, v0s, sums, packed, share, ids_tile, ids_sems, in_sems, out_sems,
+    ids_hbm, occ, vir, shares, first, second, v0_out,
+    ids, occ_rows, vir_rows, band, fold, own, once, beyond, v0s, sums, packed, share, ids_sem, in_sems, out_sems,
 ):
     pairs, slab, rows_y, lanes = occ_rows.shape
     parts, part_rows = share.shape[1], share.shape[3]
     in_left, in_right, even = sides()
     upper = jnp.where(even, 1, 0)
 
-    copy = pltpu.make_async_copy(ids_hbm, ids, ids_sems.at[0])
+    copy = pltpu.make_async_copy(ids_hbm, ids, ids_sem)
     copy.start()
     zero_rims(own)
     zero_rims(once)
@@ -126,15 +126,6 @@
     for p in range(pairs):
         for copy in inputs(p):
             copy.start()
-    line = lax.broadcasted_iota(jnp.int32, ids_tile.shape, 0)
-    lane = lax.broadcasted_iota(jnp.int32, ids_tile.shape, 1)
-    tile = jnp.zeros(ids_tile.shape, F32)
-    for p in range(pairs):
-        for j in range(2):
-            tile = jnp.where((line == j) & (lane == p), ids[j, p].astype(F32), tile)
-    ids_tile[...] = tile.astype(BF16)
-    ids_copy = pltpu.make_async_copy(ids_tile, ids_out, ids_sems.at[1])
-    ids_copy.start()
     fill_children(fold, 0.5, 0)
 
     def one_pair(p, carry):
@@ -217,17 +208,16 @@
         return carry
 
     lax.fori_loop(0, pairs, one_pair, 0)
-    ids_copy.wait()
     for p in range(pairs):
         for copy in (*outputs(p), last_output(p)):
             copy.wait()
 
 
 def middle_kernel(*refs):
-    parts = len(refs) - 10
+    parts = len(refs) - 9
     received = refs[:parts]
-    modes, table_y, inverse, ids_tile, out = refs[parts : parts + 5]
-    source, field_a, field_b, smooth, edge = refs[parts + 5 :]
+    modes, table_y, inverse, out = refs[parts : parts + 4]
+    source, field_a, field_b, smooth, edge = refs[parts + 4 :]
     slabs, _, part_rows, lanes = received[0].shape
     rows_y = parts * part_rows
     own_part = lax.rem(lax.axis_index("dom"), parts)
@@ -295,18 +285,16 @@
         high, low = high_low(field_a[d, pl.ds(PAD + at, part_rows)])
         out[d, :part_rows] = high
         out[d, part_rows : 2 * part_rows] = low
-        out[d, 2 * part_rows : 3 * part_rows] = edge[d, pl.ds(at, part_rows)].astype(BF16)
-        out[d, 3 * part_rows :] = ids_tile[...]
+        out[d, 2 * part_rows :] = edge[d, pl.ds(at, part_rows)].astype(BF16)
 
 
 def final_kernel(
-    all_occ, all_vir, v0_hbm, first_sent, second_sent, coarse, first, second, out, panel,
+    all_ids, all_occ, all_vir, v0_hbm, first_sent, second_sent, coarse, first, second, out, panel,
     v0, edges, band, spread, identity, wide, start, swept, kept,
-    occ, vir, late_vector, late_ids, turned, sums, ids_sem, in_sems, out_sems, late_sems,
+    occ, vir, ids, turned, sums, in_sems, out_sems, late_sems,
 ):
     pairs, slab, rows_y, lanes = kept.shape
-    groups = late_vector.shape[0]
-    parts, part_rows = coarse.shape[0] // pairs, (coarse.shape[1] - 16) // 3
+    parts, part_rows = coarse.shape[0] // pairs, coarse.shape[1] // 3
     in_left, in_right, even = sides()
     upper = jnp.where(even, 1, 0)
 
@@ -323,11 +311,11 @@
     for p in range(pairs):
         for copy in inputs(p):
             copy.start()
-    late = [pltpu.make_async_copy(all_occ, occ, late_sems.at[0]), pltpu.make_async_copy(all_vir, vir, late_sems.at[1])]
-    for turn in range(groups):
-        late_vector[turn] = coarse[turn, 3 * part_rows :].astype(F32).astype(jnp.int32)
-    ids_copy = pltpu.make_async_copy(late_vector, late_ids, ids_sem)
-    ids_copy.start()
+    late = [
+        pltpu.make_async_copy(all_ids, ids, late_sems.at[0]),
+        pltpu.make_async_copy(all_occ, occ, late_sems.at[1]),
+        pltpu.make_async_copy(all_vir, vir, late_sems.at[2]),
+    ]
     fill_band(band)
     fill_children(spread, 1.0, 1)
     line = lax.broadcasted_iota(jnp.int32, identity.shape, 0)
@@ -340,7 +328,7 @@
             table = spread[...]
             at = p * parts + part
             own = dot(coarse[at, :part_rows], table) + dot(coarse[at, part_rows : 2 * part_rows], table)
-            beyond = own + dot(coarse[at, 2 * part_rows : 3 * part_rows], table)
+            beyond = own + dot(coarse[at, 2 * part_rows :], table)
             for at, value in enumerate((beyond[:, :lanes], own[:, :lanes], own[:, lanes:], beyond[:, lanes:])):
                 rows = 2 * part * part_rows
                 wide[p, at, pl.ds(rows, part_rows, stride=2), :] = value
@@ -404,12 +392,11 @@
         return carry
 
     lax.fori_loop(0, pairs, one_pair, 0)
-    ids_copy.wait()
     for copy in late:
         copy.wait()
     half = lanes // 2
     fields = turned[...].reshape(pairs * half, 2 * slab * rows_y)
-    count = groups * pairs
+    count = ids.shape[0] // 2 * pairs
     first_row = lax.axis_index("pair") * pairs
     left = lax.broadcasted_iota(jnp.int32, (rows_y, lanes), 1) < half
     diagonal = lax.broadcasted_iota(jnp.int32, (half, 2 * lanes), 0) == lax.rem(
@@ -418,7 +405,7 @@
 
     def density16(p, layer):
         turn, k = p // pairs, lax.rem(p, pairs)
-        i, a = late_ids[turn, 0, k], late_ids[turn, 1, k]
+        i, a = ids[2 * turn, k], ids[2 * turn + 1, k]
         return (occ[i, layer].astype(F32) * vir[a, layer].astype(F32)).astype(BF16)
 
     def four_rows(turn, carry):
@@ -487,17 +474,15 @@
     halo = (pairs, 3, rows_y, lanes)
     own = (pairs, slab, rows_y, lanes)
     share = (pairs, parts, 3, part_rows, lanes)
-    tile = (16, lanes)
-    shares, first, second, v0, ids_tile = pl.pallas_call(
+    shares, first, second, v0 = pl.pallas_call(
         source_kernel,
         in_specs=[hbm, hbm, hbm],
-        out_specs=[hbm] * 5,
+        out_specs=[hbm] * 4,
         out_shape=[
             pltpu.HBM(share, BF16),
             pltpu.HBM(halo, BF16),
             pltpu.HBM(halo, BF16),
             pltpu.HBM(own, F32),
-            pltpu.HBM(tile, BF16),
         ],
         scratch_shapes=[
             pltpu.SMEM(ids.shape, jnp.int32),
@@ -512,8 +497,7 @@
             pltpu.VMEM((slab // 2 + 2, rows_y, lanes), F32),
             pltpu.VMEM((pairs, 2, 3, rows_y, lanes), BF16),
             pltpu.VMEM(share, BF16),
-            pltpu.VMEM(tile, BF16),
-            pltpu.SemaphoreType.DMA((2,)),
+            pltpu.SemaphoreType.DMA,
             pltpu.SemaphoreType.DMA((2, pairs)),
             pltpu.SemaphoreType.DMA((4, pairs)),
         ],
@@ -526,10 +510,6 @@
     outside = outside + [(j, i) for i, j in outside]
     first_halo = lax.ppermute(first, "dom", inside)
     second_halo = lax.ppermute(second, "dom", outside)
-    groups = lax.axis_size("pair")
-    perm = [(d * groups + (g + d) % groups, d * groups + g) for d in range(slabs) for g in range(groups)]
-    ids_tile = lax.ppermute(ids_tile, ("dom", "pair"), perm)
-
     received = lax.all_to_all(shares.reshape(slabs, 3, part_rows, lanes), "dom", 0, 0)
     views = [received]
     for turn in range(1, parts):
@@ -540,19 +520,23 @@
     plain = pltpu.VMEM((slabs, half_y, lanes), F32)
     smoothed = pl.pallas_call(
         middle_kernel,
-        in_specs=[vmem] * (parts + 4),
+        in_specs=[vmem] * (parts + 3),
         out_specs=vmem,
-        out_shape=jax.ShapeDtypeStruct((slabs, 3 * part_rows + 16, lanes), BF16),
+        out_shape=jax.ShapeDtypeStruct((slabs, 3 * part_rows, lanes), BF16),
         scratch_shapes=[padded, padded, padded, plain, plain],
         compiler_params=pltpu.CompilerParams(vmem_limit_bytes=32 * MIB),
         name="middle",
-    )(*views, *tables, ids_tile)
+    )(*views, *tables)
+    groups = lax.axis_size("pair")
+    late_ids, smoothed = lax.optimization_barrier((ids, smoothed))
+    turns = [[((g + turn) % groups, g) for g in range(groups)] for turn in range(1, groups)]
+    all_ids = jnp.concatenate([ids] + [lax.ppermute(late_ids, "pair", perm) for perm in turns], axis=0)
     returned = lax.all_to_all(smoothed, "dom", 0, 0)
 
     count = groups * pairs
     potentials, panel = pl.pallas_call(
         final_kernel,
-        in_specs=[hbm] * 5 + [vmem] * 3,
+        in_specs=[anywhere] + [hbm] * 5 + [vmem] * 3,
         out_specs=[hbm, vmem],
         out_shape=[pltpu.HBM(own, BF16), jax.ShapeDtypeStruct((2, count // 2, pairs), F32)],
         scratch_shapes=[
@@ -567,18 +551,16 @@
             pltpu.VMEM(own, BF16),
             pltpu.VMEM(occupied.shape, BF16),
             pltpu.VMEM(virtual.shape, BF16),
-            pltpu.VMEM((groups,) + tile, jnp.int32),
-            pltpu.SMEM((groups,) + tile, jnp.int32),
+            pltpu.SMEM(all_ids.shape, jnp.int32),
             pltpu.VMEM((pairs, lanes // 2, 2 * slab * rows_y), BF16),
             pltpu.VMEM((count // 2, pairs, lanes), F32),
-            pltpu.SemaphoreType.DMA,
             pltpu.SemaphoreType.DMA((3, pairs)),
             pltpu.SemaphoreType.DMA((pairs,)),
-            pltpu.SemaphoreType.DMA((2,)),
+            pltpu.SemaphoreType.DMA((3,)),
         ],
         compiler_params=pltpu.CompilerParams(vmem_limit_bytes=24 * MIB),
         name="final",
-    )(*[in_hbm(x) for x in (occupied, virtual, v0, first, second)], returned, first_halo, second_halo)
+    )(all_ids, *[in_hbm(x) for x in (occupied, virtual, v0, first, second)], returned, first_halo, second_halo)
     panel = jnp.swapaxes(panel, 0, 1).reshape(slabs, count // slabs, pairs)
     return potentials, jnp.sum(lax.all_to_all(panel, "dom", 0, 0), axis=0)
 

time: 57 us -> 55.8 us (0.979)
  waiting for transfers between devices: 16.2 us -> 13.4 us
  blocking collectives: 7.07 us -> 7.86 us
    all_to_all x1, waiting for transfers between devices: 8.68 us -> 2.36 us  [shards(): returned = lax.all_to_all(smoothed, 'dom', 0, 0)]
    ppermute x1 -> x3, starting transfers between devices: 1.32 us -> 5.57 us  [shards(): lax.ppermute(late_ids, 'pair', perm)]
    all_to_all x1, starting transfers between devices: 7.21 us -> 3.45 us  [shards(): returned = lax.all_to_all(smoothed, 'dom', 0, 0)]
    ppermute x1 -> x3, waiting for transfers between devices: 0.01 us -> 2.22 us  [shards(): lax.ppermute(late_ids, 'pair', perm)]
    ppermute x1, waiting for transfers between devices: 0.4 us -> 1.72 us  [shards(): views.append(lax.ppermute(received, 'dom', perm))]
    all_to_all x1, blocking collectives: 7.07 us -> 7.86 us  [shards(): return (potentials, jnp.sum(lax.all_to_all(panel, 'dom', 0, 0), axis=0))]
  transfers between devices with their start and end apart: 6 -> 8, of which waited for: 3 -> 5; matrix products, arithmetic and copies ran while one was open for 0% -> 0% of each run, Pallas kernels for 7% -> 8%
where the time goes in v5:
time: 55.8 us; the launch traced here: 55.4 us
  Pallas kernels  17.4 us (31%)
  starting transfers between devices  15.4 us (28%)
  waiting for transfers between devices  13.4 us (24%)
  blocking collectives  7.86 us (14%)
  between operations  0.74 us (1%)
  other arithmetic  0.59 us (1%)
    all_to_all x1, blocking collectives, shards(): return (potentials, jnp.sum(lax.all_to_all(panel, 'dom', 0, 0), axis=0))  7.86 us
    pallas_call x1, Pallas kernels, shards(): pl.pallas_call(final_kernel, in_specs=[anywhere] + [hbm] * 5 + [vmem] * 3...  7.49 us
    all_to_all x1, waiting for transfers between devices, shards(): lax.all_to_all(shares.reshape(slabs, 3, part_rows, lanes), 'dom', 0, 0)  7.13 us
    pallas_call x1, Pallas kernels, shards(): pl.pallas_call(source_kernel, in_specs=[hbm, hbm, hbm], out_specs=[hbm] *...  5.69 us
    ppermute x3, starting transfers between devices, shards(): lax.ppermute(late_ids, 'pair', perm)  5.57 us
    all_to_all x1, starting transfers between devices, shards(): lax.all_to_all(shares.reshape(slabs, 3, part_rows, lanes), 'dom', 0, 0)  5.18 us
    pallas_call x1, Pallas kernels, shards(): pl.pallas_call(middle_kernel, in_specs=[vmem] * (parts + 3), out_specs=vm...  4.19 us
    all_to_all x1, starting transfers between devices, shards(): returned = lax.all_to_all(smoothed, 'dom', 0, 0)  3.45 us
  transfers between devices with their start and end apart: 8, of which 5 were waited for; matrix products, arithmetic and copies ran while one was open for 0% of the time, Pallas kernels for 8%

profile of v5, /device:TPU:0, one launch (start us, length us, event | category | flops | bytes accessed | tf_op | source)
XLA Modules:
  0.0 55.4 jit_solution(15468000595853734568)
XLA Ops:
  0.6 0.0 copy-start
  0.6 0.0 copy-start.1
  0.7 0.0 copy-start.2
  0.7 5.7 %source.1 = (bf16[4,2,3,64,128]{4,3,2,1,0:T(8,128)(2,1)}, bf16[4,3,256,128]{3,2,1,0:T(8,128)(2,1)}, bf16[4,3,256,128]{3,2,1,0:T(8,128)(2,1)}, f32[4,4,256,128]{3,2,1,0:T(8,128)}) custom-call(s32[2,4]{1,0:T(2,128)} %bitcast.5, bf16[12,4,256,128]{3,2,1,0:T(8,128)(2,1)} %all_occ.1, bf16[12,4,256,128]{3,2,1,0:T(8,128)(2,1)} %all_vir.1), custom_call_target="tpu_custom_call" | custom-call | tf_op jit(solution)/shard_map/source/pallas_call | solution.py:477
  6.4 0.0 copy-start.3
  6.4 5.2 %all-to-all-start = ((bf16[8,3,64,128]{3,2,1,0:T(8,128)(2,1)}), bf16[8,3,64,128]{3,2,1,0:T(8,128)(2,1)S(1)}, u32[]{:S(2)}, u32[]{:S(2)}) async-start(bf16[8,3,64,128]{3,2,1,0:T(8,128)(2,1)} %bitcast.4), calls=%async_computation | async-start | bytes 786432 | tf_op jit(solution)/shard_map/all_to_all | solution.py:513
  11.6 0.5 collective-permute-start.4
  12.1 0.7 %collective-permute-start.5 = (bf16[4,3,256,128]{3,2,1,0:T(8,128)(2,1)}, bf16[4,3,256,128]{3,2,1,0:T(8,128)(2,1)S(1)}, u32[]{:S(2)}, u32[]{:S(2)}) collective-permute-start(bf16[4,3,256,128]{3,2,1,0:T(8,128)(2,1)} %get-tuple-element.14.second_sent), channel_id=1, source_target_pairs={{4,8},{12,16},{20,24},{8,4},{16,12},{24,20},{5,9},{13,17},{21,25},... | collective-permute-start | bytes 2359304 | tf_op jit(solution)/shard_map/ppermute | solution.py:512
  12.8 7.1 %all-to-all-done.refs_0_ = bf16[8,3,64,128]{3,2,1,0:T(8,128)(2,1)S(1)} async-done(((bf16[8,3,64,128]{3,2,1,0:T(8,128)(2,1)}), bf16[8,3,64,128]{3,2,1,0:T(8,128)(2,1)S(1)}, u32[]{:S(2)}, u32[]{:S(2)}) %all-to-all-start) | async-done | bytes 393248 | tf_op jit(solution)/shard_map/all_to_all | solution.py:513
  19.9 0.0 collective-permute-start
  19.9 1.7 %collective-permute-done.refs_1_ = bf16[8,3,64,128]{3,2,1,0:T(8,128)(2,1)S(1)} collective-permute-done((bf16[8,3,64,128]{3,2,1,0:T(8,128)(2,1)S(1)}, bf16[8,3,64,128]{3,2,1,0:T(8,128)(2,1)S(1)}, u32[]{:S(2)}, u32[]{:S(2)}) %collective-permute-start) | collective-permute-done | bytes 393248 | tf_op jit(solution)/shard_map/ppermute | solution.py:517
  21.6 0.0 copy-done
  21.6 0.0 copy-done.1
  21.6 0.0 copy-done.2
  21.6 4.2 %middle.1 = bf16[8,192,128]{2,1,0:T(8,128)(2,1)} custom-call(bf16[8,3,64,128]{3,2,1,0:T(8,128)(2,1)S(1)} %all-to-all-done.refs_0_, bf16[8,3,64,128]{3,2,1,0:T(8,128)(2,1)S(1)} %collective-permute-done.refs_1_, bf16[2,1024,256]{2,1,0:T(8,128)(2,1)S(1)} %copy-done, f32[64,64]{1,0:T(8,128)S(1)} %copy-done.2, f32[64,256]{1,0:T(8,128)S(1)} %copy-done.1), custom_call_target="tpu_custom_call" | custom-call | tf_op jit(solution)/shard_map/middle/pallas_call | solution.py:521
  25.8 3.5 %all-to-all-start.1 = ((bf16[8,192,128]{2,1,0:T(8,128)(2,1)}), bf16[8,192,128]{2,1,0:T(8,128)(2,1)S(1)}, u32[]{:S(2)}, u32[]{:S(2)}) async-start(bf16[8,192,128]{2,1,0:T(8,128)(2,1)} %middle.1), calls=%async_computation.1 | async-start | bytes 786432 | tf_op jit(solution)/shard_map/all_to_all | solution.py:534
  29.3 0.0 copy-done.3
  29.3 1.6 %collective-permute-start.3 = (s32[2,4]{1,0:T(2,128)S(1)}, s32[2,4]{1,0:T(2,128)S(1)}, u32[]{:S(2)}, u32[]{:S(2)}) collective-permute-start(s32[2,4]{1,0:T(2,128)S(1)} %bitcast.6), channel_id=1, source_target_pairs={{3,0},{0,1},{1,2},{2,3},{7,4},{4,5},{5,6},{6,7},{11,8},{8,9},{9,10... | collective-permute-start | bytes 104 | tf_op jit(solution)/shard_map/ppermute | solution.py:533
  30.9 2.6 %collective-permute-start.2 = (s32[2,4]{1,0:T(2,128)S(1)}, s32[2,4]{1,0:T(2,128)S(1)}, u32[]{:S(2)}, u32[]{:S(2)}) collective-permute-start(s32[2,4]{1,0:T(2,128)S(1)} %bitcast.7), channel_id=1, source_target_pairs={{2,0},{3,1},{0,2},{1,3},{6,4},{7,5},{4,6},{5,7},{10,8},{11,9},{8,1... | collective-permute-start | bytes 104 | tf_op jit(solution)/shard_map/ppermute | solution.py:533
  33.5 1.3 %collective-permute-start.1 = (s32[2,4]{1,0:T(2,128)S(1)}, s32[2,4]{1,0:T(2,128)S(1)}, u32[]{:S(2)}, u32[]{:S(2)}) collective-permute-start(s32[2,4]{1,0:T(2,128)S(1)} %bitcast.8), channel_id=1, source_target_pairs={{1,0},{2,1},{3,2},{0,3},{5,4},{6,5},{7,6},{4,7},{9,8},{10,9},{11,1... | collective-permute-start | bytes 104 | tf_op jit(solution)/shard_map/ppermute | solution.py:533
  34.9 0.0 collective-permute-done.3
  34.9 0.5 collective-permute-done.2
  35.4 1.7 %collective-permute-done.1 = s32[2,4]{1,0:T(2,128)S(1)} collective-permute-done((s32[2,4]{1,0:T(2,128)S(1)}, s32[2,4]{1,0:T(2,128)S(1)}, u32[]{:S(2)}, u32[]{:S(2)}) %collective-permute-start.1) | collective-permute-done | bytes 64 | tf_op jit(solution)/shard_map/ppermute | solution.py:533
  37.1 0.0 collective-permute-done.4.first
  37.1 0.0 collective-permute-done.5.second
  37.1 2.4 %all-to-all-done.1.coarse = bf16[8,192,128]{2,1,0:T(8,128)(2,1)S(1)} async-done(((bf16[8,192,128]{2,1,0:T(8,128)(2,1)}), bf16[8,192,128]{2,1,0:T(8,128)(2,1)S(1)}, u32[]{:S(2)}, u32[]{:S(2)}) %all-to-all-start.1) | async-done | bytes 393248 | tf_op jit(solution)/shard_map/all_to_all | solution.py:534
  39.5 7.5 %final.1 = (bf16[4,4,256,128]{3,2,1,0:T(8,128)(2,1)}, f32[2,8,4]{2,1,0:T(8,128)S(1)}) custom-call(s32[8,4]{1,0:T(8,128)S(1)} %pad_add_fusion.all_ids, bf16[12,4,256,128]{3,2,1,0:T(8,128)(2,1)} %all_occ.1, bf16[12,4,256,128]{3,2,1,0:T(8,128)(2,1)} %all_vir.1, f32[4,4,256,128]{3,2,1,0:T(8,128)} %get-tuple-element.12.v0_hbm, ...), custom_call_target="tpu_custom_call" | custom-call | tf_op jit(solution)/shard_map/final/pallas_call | solution.py:537
  47.0 7.9 %all_to_all.15 = f32[8,2,4]{2,1,0:T(2,128)S(1)} all-to-all(f32[8,2,4]{2,1,0:T(2,128)S(1)} %copy.8), channel_id=1, replica_groups=mesh['dom'=8,'pair'=4] {'dom'}, dimensions={0} | all-to-all | bytes 512 | tf_op jit(solution)/shard_map/all_to_all | solution.py:565
  54.9 0.6 %reduce_sum.9 = f32[2,4]{1,0:T(2,128)} reduce(f32[8,2,4]{2,1,0:T(2,128)S(1)} %all_to_all.15, f32[]{:T(128)} %constant.3.clone.1), dimensions={0}, to_apply=%region_0.0 | reduce | flops 56 | bytes 292 | tf_op jit(solution)/shard_map/reduce_sum | solution.py:565
  (2 shorter events, 0.0 us)
Async XLA Ops:
  0.6 21.0 %copy-start = (bf16[2,1024,256]{2,1,0:T(8,128)(2,1)S(1)}, bf16[2,1024,256]{2,1,0:T(8,128)(2,1)}, u32[]{:S(2)}) copy-start(bf16[2,1024,256]{2,1,0:T(8,128)(2,1)} %constant.8.clone.refs_2_) | copy-start | bytes 3145732
  0.6 21.0 %copy-start.1 = (f32[64,256]{1,0:T(8,128)S(1)}, f32[64,256]{1,0:T(8,128)}, u32[]{:S(2)}) copy-start(f32[64,256]{1,0:T(8,128)} %constant.10.clone.refs_4_) | copy-start | bytes 196612
  0.7 21.0 %copy-start.2 = (f32[64,64]{1,0:T(8,128)S(1)}, f32[64,64]{1,0:T(8,128)}, u32[]{:S(2)}) copy-start(f32[64,64]{1,0:T(8,128)} %constant.9.clone.refs_3_) | copy-start | bytes 49156
  6.4 22.9 %copy-start.3 = (s32[4,2]{0,1:T(2,128)S(1)}, s32[4,2]{0,1:T(2,128)}, u32[]{:S(2)}) copy-start(s32[4,2]{0,1:T(2,128)} %param.8) | copy-start | bytes 100
  6.4 13.5 %all-to-all-start = ((bf16[8,3,64,128]{3,2,1,0:T(8,128)(2,1)}), bf16[8,3,64,128]{3,2,1,0:T(8,128)(2,1)S(1)}, u32[]{:S(2)}, u32[]{:S(2)}) async-start(bf16[8,3,64,128]{3,2,1,0:T(8,128)(2,1)} %bitcast.4), calls=%async_computation | async-start | bytes 786432 | tf_op jit(solution)/shard_map/all_to_all | solution.py:513
  11.6 25.5 %collective-permute-start.4 = (bf16[4,3,256,128]{3,2,1,0:T(8,128)(2,1)}, bf16[4,3,256,128]{3,2,1,0:T(8,128)(2,1)S(1)}, u32[]{:S(2)}, u32[]{:S(2)}) collective-permute-start(bf16[4,3,256,128]{3,2,1,0:T(8,128)(2,1)} %get-tuple-element.13.first_sent), channel_id=1, source_target_pairs={{0,4},{4,0},{8,12},{12,8},{16,20},{20,16},{24,28},{28,24},{1,5},{5... | collective-permute-start | bytes 2359304 | tf_op jit(solution)/shard_map/ppermute | solution.py:511
  12.1 25.0 %collective-permute-start.5 = (bf16[4,3,256,128]{3,2,1,0:T(8,128)(2,1)}, bf16[4,3,256,128]{3,2,1,0:T(8,128)(2,1)S(1)}, u32[]{:S(2)}, u32[]{:S(2)}) collective-permute-start(bf16[4,3,256,128]{3,2,1,0:T(8,128)(2,1)} %get-tuple-element.14.second_sent), channel_id=1, source_target_pairs={{4,8},{12,16},{20,24},{8,4},{16,12},{24,20},{5,9},{13,17},{21,25},... | collective-permute-start | bytes 2359304 | tf_op jit(solution)/shard_map/ppermute | solution.py:512
  19.9 1.7 %collective-permute-start = (bf16[8,3,64,128]{3,2,1,0:T(8,128)(2,1)S(1)}, bf16[8,3,64,128]{3,2,1,0:T(8,128)(2,1)S(1)}, u32[]{:S(2)}, u32[]{:S(2)}) collective-permute-start(bf16[8,3,64,128]{3,2,1,0:T(8,128)(2,1)S(1)} %all-to-all-done.refs_0_), channel_id=1, source_target_pairs={{4,0},{0,4},{12,8},{8,12},{20,16},{16,20},{28,24},{24,28},{5,1},{1... | collective-permute-start | bytes 1179656 | tf_op jit(solution)/shard_map/ppermute | solution.py:517
  25.8 13.7 %all-to-all-start.1 = ((bf16[8,192,128]{2,1,0:T(8,128)(2,1)}), bf16[8,192,128]{2,1,0:T(8,128)(2,1)S(1)}, u32[]{:S(2)}, u32[]{:S(2)}) async-start(bf16[8,192,128]{2,1,0:T(8,128)(2,1)} %middle.1), calls=%async_computation.1 | async-start | bytes 786432 | tf_op jit(solution)/shard_map/all_to_all | solution.py:534
  29.3 5.6 %collective-permute-start.3 = (s32[2,4]{1,0:T(2,128)S(1)}, s32[2,4]{1,0:T(2,128)S(1)}, u32[]{:S(2)}, u32[]{:S(2)}) collective-permute-start(s32[2,4]{1,0:T(2,128)S(1)} %bitcast.6), channel_id=1, source_target_pairs={{3,0},{0,1},{1,2},{2,3},{7,4},{4,5},{5,6},{6,7},{11,8},{8,9},{9,10... | collective-permute-start | bytes 104 | tf_op jit(solution)/shard_map/ppermute | solution.py:533
  30.9 4.5 %collective-permute-start.2 = (s32[2,4]{1,0:T(2,128)S(1)}, s32[2,4]{1,0:T(2,128)S(1)}, u32[]{:S(2)}, u32[]{:S(2)}) collective-permute-start(s32[2,4]{1,0:T(2,128)S(1)} %bitcast.7), channel_id=1, source_target_pairs={{2,0},{3,1},{0,2},{1,3},{6,4},{7,5},{4,6},{5,7},{10,8},{11,9},{8,1... | collective-permute-start | bytes 104 | tf_op jit(solution)/shard_map/ppermute | solution.py:533
  33.5 3.6 %collective-permute-start.1 = (s32[2,4]{1,0:T(2,128)S(1)}, s32[2,4]{1,0:T(2,128)S(1)}, u32[]{:S(2)}, u32[]{:S(2)}) collective-permute-start(s32[2,4]{1,0:T(2,128)S(1)} %bitcast.8), channel_id=1, source_target_pairs={{1,0},{2,1},{3,2},{0,3},{5,4},{6,5},{7,6},{4,7},{9,8},{10,9},{11,1... | collective-permute-start | bytes 104 | tf_op jit(solution)/shard_map/ppermute | solution.py:533

commit v6 on v5

--- a/solution.py
+++ b/solution.py
@@ -391,7 +391,7 @@
             turned[p, :, column + rows_y : column + 2 * rows_y] = value[half:]
         return carry
 
-    lax.fori_loop(0, pairs, one_pair, 0)
+    lax.fori_loop(0, pairs, one_pair, 0, unroll=2)
     for copy in late:
         copy.wait()
     half = lanes // 2
@@ -428,7 +428,7 @@
             sums[row + 1, q : q + 1] = block[:, lanes:]
         return carry
 
-    lax.fori_loop(0, count // 4, four_rows, 0)
+    lax.fori_loop(0, count // 4, four_rows, 0, unroll=4)
     scale = 1.0 / float(slab * rows_y * lanes * lax.axis_size("dom"))
     total = scale * sums[...]
     left = lax.broadcasted_iota(jnp.int32, total.shape, 2) < half

time: 55.8 us -> 54.7 us (0.980)
  Pallas kernels: 17.4 us -> 16.2 us
    pallas_call x1, Pallas kernels: 7.49 us -> 6.32 us  [shards(): pl.pallas_call(final_kernel, in_specs=[anywhere] + [hbm] * 5 + [vmem] * 3...]
where the time goes in v6:
time: 54.7 us; the launch traced here: 54.3 us
  Pallas kernels  16.2 us (30%)
  starting transfers between devices  15.4 us (28%)
  waiting for transfers between devices  13.4 us (24%)
  blocking collectives  7.87 us (14%)
  between operations  0.74 us (1%)
  other arithmetic  0.59 us (1%)
    all_to_all x1, blocking collectives, shards(): return (potentials, jnp.sum(lax.all_to_all(panel, 'dom', 0, 0), axis=0))  7.87 us
    all_to_all x1, waiting for transfers between devices, shards(): lax.all_to_all(shares.reshape(slabs, 3, part_rows, lanes), 'dom', 0, 0)  7.13 us
    pallas_call x1, Pallas kernels, shards(): pl.pallas_call(final_kernel, in_specs=[anywhere] + [hbm] * 5 + [vmem] * 3...  6.32 us
    pallas_call x1, Pallas kernels, shards(): pl.pallas_call(source_kernel, in_specs=[hbm, hbm, hbm], out_specs=[hbm] *...  5.69 us
    ppermute x3, starting transfers between devices, shards(): lax.ppermute(late_ids, 'pair', perm)  5.57 us
    all_to_all x1, starting transfers between devices, shards(): lax.all_to_all(shares.reshape(slabs, 3, part_rows, lanes), 'dom', 0, 0)  5.18 us
    pallas_call x1, Pallas kernels, shards(): pl.pallas_call(middle_kernel, in_specs=[vmem] * (parts + 3), out_specs=vm...  4.19 us
    all_to_all x1, starting transfers between devices, shards(): returned = lax.all_to_all(smoothed, 'dom', 0, 0)  3.45 us
  transfers between devices with their start and end apart: 8, of which 5 were waited for; matrix products, arithmetic and copies ran while one was open for 0% of the time, Pallas kernels for 8%

profile of v6, /device:TPU:0, one launch (start us, length us, event | category | flops | bytes accessed | tf_op | source)
XLA Modules:
  0.0 54.3 jit_solution(18060193340215099891)
XLA Ops:
  0.6 0.0 copy-start
  0.6 0.0 copy-start.1
  0.7 0.0 copy-start.2
  0.7 5.7 %source.1 = (bf16[4,2,3,64,128]{4,3,2,1,0:T(8,128)(2,1)}, bf16[4,3,256,128]{3,2,1,0:T(8,128)(2,1)}, bf16[4,3,256,128]{3,2,1,0:T(8,128)(2,1)}, f32[4,4,256,128]{3,2,1,0:T(8,128)}) custom-call(s32[2,4]{1,0:T(2,128)} %bitcast.5, bf16[12,4,256,128]{3,2,1,0:T(8,128)(2,1)} %all_occ.1, bf16[12,4,256,128]{3,2,1,0:T(8,128)(2,1)} %all_vir.1), custom_call_target="tpu_custom_call" | custom-call | tf_op jit(solution)/shard_map/source/pallas_call | solution.py:477
  6.4 0.0 copy-start.3
  6.4 5.2 %all-to-all-start = ((bf16[8,3,64,128]{3,2,1,0:T(8,128)(2,1)}), bf16[8,3,64,128]{3,2,1,0:T(8,128)(2,1)S(1)}, u32[]{:S(2)}, u32[]{:S(2)}) async-start(bf16[8,3,64,128]{3,2,1,0:T(8,128)(2,1)} %bitcast.4), calls=%async_computation | async-start | bytes 786432 | tf_op jit(solution)/shard_map/all_to_all | solution.py:513
  11.6 0.5 collective-permute-start.4
  12.1 0.7 %collective-permute-start.5 = (bf16[4,3,256,128]{3,2,1,0:T(8,128)(2,1)}, bf16[4,3,256,128]{3,2,1,0:T(8,128)(2,1)S(1)}, u32[]{:S(2)}, u32[]{:S(2)}) collective-permute-start(bf16[4,3,256,128]{3,2,1,0:T(8,128)(2,1)} %get-tuple-element.14.second_sent), channel_id=1, source_target_pairs={{4,8},{12,16},{20,24},{8,4},{16,12},{24,20},{5,9},{13,17},{21,25},... | collective-permute-start | bytes 2359304 | tf_op jit(solution)/shard_map/ppermute | solution.py:512
  12.8 7.1 %all-to-all-done.refs_0_ = bf16[8,3,64,128]{3,2,1,0:T(8,128)(2,1)S(1)} async-done(((bf16[8,3,64,128]{3,2,1,0:T(8,128)(2,1)}), bf16[8,3,64,128]{3,2,1,0:T(8,128)(2,1)S(1)}, u32[]{:S(2)}, u32[]{:S(2)}) %all-to-all-start) | async-done | bytes 393248 | tf_op jit(solution)/shard_map/all_to_all | solution.py:513
  19.9 0.0 collective-permute-start
  19.9 1.7 %collective-permute-done.refs_1_ = bf16[8,3,64,128]{3,2,1,0:T(8,128)(2,1)S(1)} collective-permute-done((bf16[8,3,64,128]{3,2,1,0:T(8,128)(2,1)S(1)}, bf16[8,3,64,128]{3,2,1,0:T(8,128)(2,1)S(1)}, u32[]{:S(2)}, u32[]{:S(2)}) %collective-permute-start) | collective-permute-done | bytes 393248 | tf_op jit(solution)/shard_map/ppermute | solution.py:517
  21.6 0.0 copy-done
  21.6 0.0 copy-done.1
  21.6 0.0 copy-done.2
  21.6 4.2 %middle.1 = bf16[8,192,128]{2,1,0:T(8,128)(2,1)} custom-call(bf16[8,3,64,128]{3,2,1,0:T(8,128)(2,1)S(1)} %all-to-all-done.refs_0_, bf16[8,3,64,128]{3,2,1,0:T(8,128)(2,1)S(1)} %collective-permute-done.refs_1_, bf16[2,1024,256]{2,1,0:T(8,128)(2,1)S(1)} %copy-done, f32[64,64]{1,0:T(8,128)S(1)} %copy-done.2, f32[64,256]{1,0:T(8,128)S(1)} %copy-done.1), custom_call_target="tpu_custom_call" | custom-call | tf_op jit(solution)/shard_map/middle/pallas_call | solution.py:521
  25.8 3.5 %all-to-all-start.1 = ((bf16[8,192,128]{2,1,0:T(8,128)(2,1)}), bf16[8,192,128]{2,1,0:T(8,128)(2,1)S(1)}, u32[]{:S(2)}, u32[]{:S(2)}) async-start(bf16[8,192,128]{2,1,0:T(8,128)(2,1)} %middle.1), calls=%async_computation.1 | async-start | bytes 786432 | tf_op jit(solution)/shard_map/all_to_all | solution.py:534
  29.3 0.0 copy-done.3
  29.3 1.6 %collective-permute-start.3 = (s32[2,4]{1,0:T(2,128)S(1)}, s32[2,4]{1,0:T(2,128)S(1)}, u32[]{:S(2)}, u32[]{:S(2)}) collective-permute-start(s32[2,4]{1,0:T(2,128)S(1)} %bitcast.6), channel_id=1, source_target_pairs={{3,0},{0,1},{1,2},{2,3},{7,4},{4,5},{5,6},{6,7},{11,8},{8,9},{9,10... | collective-permute-start | bytes 104 | tf_op jit(solution)/shard_map/ppermute | solution.py:533
  30.9 2.6 %collective-permute-start.2 = (s32[2,4]{1,0:T(2,128)S(1)}, s32[2,4]{1,0:T(2,128)S(1)}, u32[]{:S(2)}, u32[]{:S(2)}) collective-permute-start(s32[2,4]{1,0:T(2,128)S(1)} %bitcast.7), channel_id=1, source_target_pairs={{2,0},{3,1},{0,2},{1,3},{6,4},{7,5},{4,6},{5,7},{10,8},{11,9},{8,1... | collective-permute-start | bytes 104 | tf_op jit(solution)/shard_map/ppermute | solution.py:533
  33.5 1.3 %collective-permute-start.1 = (s32[2,4]{1,0:T(2,128)S(1)}, s32[2,4]{1,0:T(2,128)S(1)}, u32[]{:S(2)}, u32[]{:S(2)}) collective-permute-start(s32[2,4]{1,0:T(2,128)S(1)} %bitcast.8), channel_id=1, source_target_pairs={{1,0},{2,1},{3,2},{0,3},{5,4},{6,5},{7,6},{4,7},{9,8},{10,9},{11,1... | collective-permute-start | bytes 104 | tf_op jit(solution)/shard_map/ppermute | solution.py:533
  34.9 0.0 collective-permute-done.3
  34.9 0.5 collective-permute-done.2
  35.4 1.7 %collective-permute-done.1 = s32[2,4]{1,0:T(2,128)S(1)} collective-permute-done((s32[2,4]{1,0:T(2,128)S(1)}, s32[2,4]{1,0:T(2,128)S(1)}, u32[]{:S(2)}, u32[]{:S(2)}) %collective-permute-start.1) | collective-permute-done | bytes 64 | tf_op jit(solution)/shard_map/ppermute | solution.py:533
  37.1 0.0 collective-permute-done.4.first
  37.1 0.0 collective-permute-done.5.second
  37.1 2.4 %all-to-all-done.1.coarse = bf16[8,192,128]{2,1,0:T(8,128)(2,1)S(1)} async-done(((bf16[8,192,128]{2,1,0:T(8,128)(2,1)}), bf16[8,192,128]{2,1,0:T(8,128)(2,1)S(1)}, u32[]{:S(2)}, u32[]{:S(2)}) %all-to-all-start.1) | async-done | bytes 393248 | tf_op jit(solution)/shard_map/all_to_all | solution.py:534
  39.5 6.3 %final.1 = (bf16[4,4,256,128]{3,2,1,0:T(8,128)(2,1)}, f32[2,8,4]{2,1,0:T(8,128)S(1)}) custom-call(s32[8,4]{1,0:T(8,128)S(1)} %pad_add_fusion.all_ids, bf16[12,4,256,128]{3,2,1,0:T(8,128)(2,1)} %all_occ.1, bf16[12,4,256,128]{3,2,1,0:T(8,128)(2,1)} %all_vir.1, f32[4,4,256,128]{3,2,1,0:T(8,128)} %get-tuple-element.12.v0_hbm, ...), custom_call_target="tpu_custom_call" | custom-call | tf_op jit(solution)/shard_map/final/pallas_call | solution.py:537
  45.8 7.9 %all_to_all.15 = f32[8,2,4]{2,1,0:T(2,128)S(1)} all-to-all(f32[8,2,4]{2,1,0:T(2,128)S(1)} %copy.8), channel_id=1, replica_groups=mesh['dom'=8,'pair'=4] {'dom'}, dimensions={0} | all-to-all | bytes 512 | tf_op jit(solution)/shard_map/all_to_all | solution.py:565
  53.7 0.6 %reduce_sum.9 = f32[2,4]{1,0:T(2,128)} reduce(f32[8,2,4]{2,1,0:T(2,128)S(1)} %all_to_all.15, f32[]{:T(128)} %constant.3.clone.1), dimensions={0}, to_apply=%region_0.0 | reduce | flops 56 | bytes 292 | tf_op jit(solution)/shard_map/reduce_sum | solution.py:565
  (2 shorter events, 0.0 us)
Async XLA Ops:
  0.6 21.0 %copy-start = (bf16[2,1024,256]{2,1,0:T(8,128)(2,1)S(1)}, bf16[2,1024,256]{2,1,0:T(8,128)(2,1)}, u32[]{:S(2)}) copy-start(bf16[2,1024,256]{2,1,0:T(8,128)(2,1)} %constant.8.clone.refs_2_) | copy-start | bytes 3145732
  0.6 21.0 %copy-start.1 = (f32[64,256]{1,0:T(8,128)S(1)}, f32[64,256]{1,0:T(8,128)}, u32[]{:S(2)}) copy-start(f32[64,256]{1,0:T(8,128)} %constant.10.clone.refs_4_) | copy-start | bytes 196612
  0.7 21.0 %copy-start.2 = (f32[64,64]{1,0:T(8,128)S(1)}, f32[64,64]{1,0:T(8,128)}, u32[]{:S(2)}) copy-start(f32[64,64]{1,0:T(8,128)} %constant.9.clone.refs_3_) | copy-start | bytes 49156
  6.4 22.9 %copy-start.3 = (s32[4,2]{0,1:T(2,128)S(1)}, s32[4,2]{0,1:T(2,128)}, u32[]{:S(2)}) copy-start(s32[4,2]{0,1:T(2,128)} %param.8) | copy-start | bytes 100
  6.4 13.5 %all-to-all-start = ((bf16[8,3,64,128]{3,2,1,0:T(8,128)(2,1)}), bf16[8,3,64,128]{3,2,1,0:T(8,128)(2,1)S(1)}, u32[]{:S(2)}, u32[]{:S(2)}) async-start(bf16[8,3,64,128]{3,2,1,0:T(8,128)(2,1)} %bitcast.4), calls=%async_computation | async-start | bytes 786432 | tf_op jit(solution)/shard_map/all_to_all | solution.py:513
  11.6 25.5 %collective-permute-start.4 = (bf16[4,3,256,128]{3,2,1,0:T(8,128)(2,1)}, bf16[4,3,256,128]{3,2,1,0:T(8,128)(2,1)S(1)}, u32[]{:S(2)}, u32[]{:S(2)}) collective-permute-start(bf16[4,3,256,128]{3,2,1,0:T(8,128)(2,1)} %get-tuple-element.13.first_sent), channel_id=1, source_target_pairs={{0,4},{4,0},{8,12},{12,8},{16,20},{20,16},{24,28},{28,24},{1,5},{5... | collective-permute-start | bytes 2359304 | tf_op jit(solution)/shard_map/ppermute | solution.py:511
  12.1 25.0 %collective-permute-start.5 = (bf16[4,3,256,128]{3,2,1,0:T(8,128)(2,1)}, bf16[4,3,256,128]{3,2,1,0:T(8,128)(2,1)S(1)}, u32[]{:S(2)}, u32[]{:S(2)}) collective-permute-start(bf16[4,3,256,128]{3,2,1,0:T(8,128)(2,1)} %get-tuple-element.14.second_sent), channel_id=1, source_target_pairs={{4,8},{12,16},{20,24},{8,4},{16,12},{24,20},{5,9},{13,17},{21,25},... | collective-permute-start | bytes 2359304 | tf_op jit(solution)/shard_map/ppermute | solution.py:512
  19.9 1.7 %collective-permute-start = (bf16[8,3,64,128]{3,2,1,0:T(8,128)(2,1)S(1)}, bf16[8,3,64,128]{3,2,1,0:T(8,128)(2,1)S(1)}, u32[]{:S(2)}, u32[]{:S(2)}) collective-permute-start(bf16[8,3,64,128]{3,2,1,0:T(8,128)(2,1)S(1)} %all-to-all-done.refs_0_), channel_id=1, source_target_pairs={{4,0},{0,4},{12,8},{8,12},{20,16},{16,20},{28,24},{24,28},{5,1},{1... | collective-permute-start | bytes 1179656 | tf_op jit(solution)/shard_map/ppermute | solution.py:517
  25.8 13.7 %all-to-all-start.1 = ((bf16[8,192,128]{2,1,0:T(8,128)(2,1)}), bf16[8,192,128]{2,1,0:T(8,128)(2,1)S(1)}, u32[]{:S(2)}, u32[]{:S(2)}) async-start(bf16[8,192,128]{2,1,0:T(8,128)(2,1)} %middle.1), calls=%async_computation.1 | async-start | bytes 786432 | tf_op jit(solution)/shard_map/all_to_all | solution.py:534
  29.3 5.6 %collective-permute-start.3 = (s32[2,4]{1,0:T(2,128)S(1)}, s32[2,4]{1,0:T(2,128)S(1)}, u32[]{:S(2)}, u32[]{:S(2)}) collective-permute-start(s32[2,4]{1,0:T(2,128)S(1)} %bitcast.6), channel_id=1, source_target_pairs={{3,0},{0,1},{1,2},{2,3},{7,4},{4,5},{5,6},{6,7},{11,8},{8,9},{9,10... | collective-permute-start | bytes 104 | tf_op jit(solution)/shard_map/ppermute | solution.py:533
  30.9 4.5 %collective-permute-start.2 = (s32[2,4]{1,0:T(2,128)S(1)}, s32[2,4]{1,0:T(2,128)S(1)}, u32[]{:S(2)}, u32[]{:S(2)}) collective-permute-start(s32[2,4]{1,0:T(2,128)S(1)} %bitcast.7), channel_id=1, source_target_pairs={{2,0},{3,1},{0,2},{1,3},{6,4},{7,5},{4,6},{5,7},{10,8},{11,9},{8,1... | collective-permute-start | bytes 104 | tf_op jit(solution)/shard_map/ppermute | solution.py:533
  33.5 3.6 %collective-permute-start.1 = (s32[2,4]{1,0:T(2,128)S(1)}, s32[2,4]{1,0:T(2,128)S(1)}, u32[]{:S(2)}, u32[]{:S(2)}) collective-permute-start(s32[2,4]{1,0:T(2,128)S(1)} %bitcast.8), channel_id=1, source_target_pairs={{1,0},{2,1},{3,2},{0,3},{5,4},{6,5},{7,6},{4,7},{9,8},{10,9},{11,1... | collective-permute-start | bytes 104 | tf_op jit(solution)/shard_map/ppermute | solution.py:533

commit v7 on v6

--- a/solution.py
+++ b/solution.py
@@ -494,7 +494,7 @@
             pltpu.VMEM((slab + 2, padded_y, lanes), F32),
             pltpu.VMEM((2, rows_y, lanes), F32),
             pltpu.VMEM(own, F32),
-            pltpu.VMEM((slab // 2 + 2, rows_y, lanes), F32),
+            pltpu.VMEM((slab // 2 + 2, rows_y + PAD, lanes), F32),
             pltpu.VMEM((pairs, 2, 3, rows_y, lanes), BF16),
             pltpu.VMEM(share, BF16),
             pltpu.SemaphoreType.DMA,
@@ -545,7 +545,7 @@
             pltpu.VMEM((2 * lanes, lanes), BF16),
             pltpu.VMEM((lanes, 2 * lanes), BF16),
             pltpu.VMEM((lanes, lanes), BF16),
-            pltpu.VMEM((pairs, 4, rows_y, lanes), F32),
+            pltpu.VMEM((pairs, 4, rows_y + PAD, lanes), F32),
             pltpu.VMEM((slab + 4, padded_y, lanes), F32),
             pltpu.VMEM((slab + 2, padded_y, lanes), F32),
             pltpu.VMEM(own, BF16),

time: 54.7 us -> 54.7 us (level)
  no operation moved by 1% of the time
where the time goes in v7:
time: 54.7 us; the launch traced here: 54.3 us
  Pallas kernels  16.2 us (30%)
  starting transfers between devices  15.4 us (28%)
  waiting for transfers between devices  13.4 us (24%)
  blocking collectives  7.86 us (14%)
  between operations  0.74 us (1%)
  other arithmetic  0.59 us (1%)
    all_to_all x1, blocking collectives, shards(): return (potentials, jnp.sum(lax.all_to_all(panel, 'dom', 0, 0), axis=0))  7.86 us
    all_to_all x1, waiting for transfers between devices, shards(): lax.all_to_all(shares.reshape(slabs, 3, part_rows, lanes), 'dom', 0, 0)  7.13 us
    pallas_call x1, Pallas kernels, shards(): pl.pallas_call(final_kernel, in_specs=[anywhere] + [hbm] * 5 + [vmem] * 3...  6.32 us
    pallas_call x1, Pallas kernels, shards(): pl.pallas_call(source_kernel, in_specs=[hbm, hbm, hbm], out_specs=[hbm] *...  5.7 us
    ppermute x3, starting transfers between devices, shards(): lax.ppermute(late_ids, 'pair', perm)  5.58 us
    all_to_all x1, starting transfers between devices, shards(): lax.all_to_all(shares.reshape(slabs, 3, part_rows, lanes), 'dom', 0, 0)  5.17 us
    pallas_call x1, Pallas kernels, shards(): pl.pallas_call(middle_kernel, in_specs=[vmem] * (parts + 3), out_specs=vm...  4.19 us
    all_to_all x1, starting transfers between devices, shards(): returned = lax.all_to_all(smoothed, 'dom', 0, 0)  3.45 us
  transfers between devices with their start and end apart: 8, of which 5 were waited for; matrix products, arithmetic and copies ran while one was open for 0% of the time, Pallas kernels for 8%

profile of v7, /device:TPU:0, one launch (start us, length us, event | category | flops | bytes accessed | tf_op | source)
XLA Modules:
  0.0 54.3 jit_solution(16233490859618980784)
XLA Ops:
  0.6 0.0 copy-start
  0.6 0.0 copy-start.1
  0.7 0.0 copy-start.2
  0.7 5.7 %source.1 = (bf16[4,2,3,64,128]{4,3,2,1,0:T(8,128)(2,1)}, bf16[4,3,256,128]{3,2,1,0:T(8,128)(2,1)}, bf16[4,3,256,128]{3,2,1,0:T(8,128)(2,1)}, f32[4,4,256,128]{3,2,1,0:T(8,128)}) custom-call(s32[2,4]{1,0:T(2,128)} %bitcast.5, bf16[12,4,256,128]{3,2,1,0:T(8,128)(2,1)} %all_occ.1, bf16[12,4,256,128]{3,2,1,0:T(8,128)(2,1)} %all_vir.1), custom_call_target="tpu_custom_call" | custom-call | tf_op jit(solution)/shard_map/source/pallas_call | solution.py:477
  6.4 0.0 copy-start.3
  6.4 5.2 %all-to-all-start = ((bf16[8,3,64,128]{3,2,1,0:T(8,128)(2,1)}), bf16[8,3,64,128]{3,2,1,0:T(8,128)(2,1)S(1)}, u32[]{:S(2)}, u32[]{:S(2)}) async-start(bf16[8,3,64,128]{3,2,1,0:T(8,128)(2,1)} %bitcast.4), calls=%async_computation | async-start | bytes 786432 | tf_op jit(solution)/shard_map/all_to_all | solution.py:513
  11.6 0.5 collective-permute-start.4
  12.1 0.7 %collective-permute-start.5 = (bf16[4,3,256,128]{3,2,1,0:T(8,128)(2,1)}, bf16[4,3,256,128]{3,2,1,0:T(8,128)(2,1)S(1)}, u32[]{:S(2)}, u32[]{:S(2)}) collective-permute-start(bf16[4,3,256,128]{3,2,1,0:T(8,128)(2,1)} %get-tuple-element.14.second_sent), channel_id=1, source_target_pairs={{4,8},{12,16},{20,24},{8,4},{16,12},{24,20},{5,9},{13,17},{21,25},... | collective-permute-start | bytes 2359304 | tf_op jit(solution)/shard_map/ppermute | solution.py:512
  12.8 7.1 %all-to-all-done.refs_0_ = bf16[8,3,64,128]{3,2,1,0:T(8,128)(2,1)S(1)} async-done(((bf16[8,3,64,128]{3,2,1,0:T(8,128)(2,1)}), bf16[8,3,64,128]{3,2,1,0:T(8,128)(2,1)S(1)}, u32[]{:S(2)}, u32[]{:S(2)}) %all-to-all-start) | async-done | bytes 393248 | tf_op jit(solution)/shard_map/all_to_all | solution.py:513
  19.9 0.0 collective-permute-start
  19.9 1.7 %collective-permute-done.refs_1_ = bf16[8,3,64,128]{3,2,1,0:T(8,128)(2,1)S(1)} collective-permute-done((bf16[8,3,64,128]{3,2,1,0:T(8,128)(2,1)S(1)}, bf16[8,3,64,128]{3,2,1,0:T(8,128)(2,1)S(1)}, u32[]{:S(2)}, u32[]{:S(2)}) %collective-permute-start) | collective-permute-done | bytes 393248 | tf_op jit(solution)/shard_map/ppermute | solution.py:517
  21.6 0.0 copy-done
  21.6 0.0 copy-done.1
  21.6 0.0 copy-done.2
  21.6 4.2 %middle.1 = bf16[8,192,128]{2,1,0:T(8,128)(2,1)} custom-call(bf16[8,3,64,128]{3,2,1,0:T(8,128)(2,1)S(1)} %all-to-all-done.refs_0_, bf16[8,3,64,128]{3,2,1,0:T(8,128)(2,1)S(1)} %collective-permute-done.refs_1_, bf16[2,1024,256]{2,1,0:T(8,128)(2,1)S(1)} %copy-done, f32[64,64]{1,0:T(8,128)S(1)} %copy-done.2, f32[64,256]{1,0:T(8,128)S(1)} %copy-done.1), custom_call_target="tpu_custom_call" | custom-call | tf_op jit(solution)/shard_map/middle/pallas_call | solution.py:521
  25.8 3.5 %all-to-all-start.1 = ((bf16[8,192,128]{2,1,0:T(8,128)(2,1)}), bf16[8,192,128]{2,1,0:T(8,128)(2,1)S(1)}, u32[]{:S(2)}, u32[]{:S(2)}) async-start(bf16[8,192,128]{2,1,0:T(8,128)(2,1)} %middle.1), calls=%async_computation.1 | async-start | bytes 786432 | tf_op jit(solution)/shard_map/all_to_all | solution.py:534
  29.3 0.0 copy-done.3
  29.3 1.6 %collective-permute-start.3 = (s32[2,4]{1,0:T(2,128)S(1)}, s32[2,4]{1,0:T(2,128)S(1)}, u32[]{:S(2)}, u32[]{:S(2)}) collective-permute-start(s32[2,4]{1,0:T(2,128)S(1)} %bitcast.6), channel_id=1, source_target_pairs={{3,0},{0,1},{1,2},{2,3},{7,4},{4,5},{5,6},{6,7},{11,8},{8,9},{9,10... | collective-permute-start | bytes 104 | tf_op jit(solution)/shard_map/ppermute | solution.py:533
  30.9 2.6 %collective-permute-start.2 = (s32[2,4]{1,0:T(2,128)S(1)}, s32[2,4]{1,0:T(2,128)S(1)}, u32[]{:S(2)}, u32[]{:S(2)}) collective-permute-start(s32[2,4]{1,0:T(2,128)S(1)} %bitcast.7), channel_id=1, source_target_pairs={{2,0},{3,1},{0,2},{1,3},{6,4},{7,5},{4,6},{5,7},{10,8},{11,9},{8,1... | collective-permute-start | bytes 104 | tf_op jit(solution)/shard_map/ppermute | solution.py:533
  33.5 1.3 %collective-permute-start.1 = (s32[2,4]{1,0:T(2,128)S(1)}, s32[2,4]{1,0:T(2,128)S(1)}, u32[]{:S(2)}, u32[]{:S(2)}) collective-permute-start(s32[2,4]{1,0:T(2,128)S(1)} %bitcast.8), channel_id=1, source_target_pairs={{1,0},{2,1},{3,2},{0,3},{5,4},{6,5},{7,6},{4,7},{9,8},{10,9},{11,1... | collective-permute-start | bytes 104 | tf_op jit(solution)/shard_map/ppermute | solution.py:533
  34.9 0.0 collective-permute-done.3
  34.9 0.5 collective-permute-done.2
  35.4 1.7 %collective-permute-done.1 = s32[2,4]{1,0:T(2,128)S(1)} collective-permute-done((s32[2,4]{1,0:T(2,128)S(1)}, s32[2,4]{1,0:T(2,128)S(1)}, u32[]{:S(2)}, u32[]{:S(2)}) %collective-permute-start.1) | collective-permute-done | bytes 64 | tf_op jit(solution)/shard_map/ppermute | solution.py:533
  37.1 0.0 collective-permute-done.4.first
  37.1 0.0 collective-permute-done.5.second
  37.1 2.3 %all-to-all-done.1.coarse = bf16[8,192,128]{2,1,0:T(8,128)(2,1)S(1)} async-done(((bf16[8,192,128]{2,1,0:T(8,128)(2,1)}), bf16[8,192,128]{2,1,0:T(8,128)(2,1)S(1)}, u32[]{:S(2)}, u32[]{:S(2)}) %all-to-all-start.1) | async-done | bytes 393248 | tf_op jit(solution)/shard_map/all_to_all | solution.py:534
  39.5 6.3 %final.1 = (bf16[4,4,256,128]{3,2,1,0:T(8,128)(2,1)}, f32[2,8,4]{2,1,0:T(8,128)S(1)}) custom-call(s32[8,4]{1,0:T(8,128)S(1)} %pad_add_fusion.all_ids, bf16[12,4,256,128]{3,2,1,0:T(8,128)(2,1)} %all_occ.1, bf16[12,4,256,128]{3,2,1,0:T(8,128)(2,1)} %all_vir.1, f32[4,4,256,128]{3,2,1,0:T(8,128)} %get-tuple-element.12.v0_hbm, ...), custom_call_target="tpu_custom_call" | custom-call | tf_op jit(solution)/shard_map/final/pallas_call | solution.py:537
  45.8 7.9 %all_to_all.15 = f32[8,2,4]{2,1,0:T(2,128)S(1)} all-to-all(f32[8,2,4]{2,1,0:T(2,128)S(1)} %copy.8), channel_id=1, replica_groups=mesh['dom'=8,'pair'=4] {'dom'}, dimensions={0} | all-to-all | bytes 512 | tf_op jit(solution)/shard_map/all_to_all | solution.py:565
  53.7 0.6 %reduce_sum.9 = f32[2,4]{1,0:T(2,128)} reduce(f32[8,2,4]{2,1,0:T(2,128)S(1)} %all_to_all.15, f32[]{:T(128)} %constant.3.clone.1), dimensions={0}, to_apply=%region_0.0 | reduce | flops 56 | bytes 292 | tf_op jit(solution)/shard_map/reduce_sum | solution.py:565
  (2 shorter events, 0.0 us)
Async XLA Ops:
  0.6 21.0 %copy-start = (bf16[2,1024,256]{2,1,0:T(8,128)(2,1)S(1)}, bf16[2,1024,256]{2,1,0:T(8,128)(2,1)}, u32[]{:S(2)}) copy-start(bf16[2,1024,256]{2,1,0:T(8,128)(2,1)} %constant.8.clone.refs_2_) | copy-start | bytes 3145732
  0.6 21.0 %copy-start.1 = (f32[64,256]{1,0:T(8,128)S(1)}, f32[64,256]{1,0:T(8,128)}, u32[]{:S(2)}) copy-start(f32[64,256]{1,0:T(8,128)} %constant.10.clone.refs_4_) | copy-start | bytes 196612
  0.7 21.0 %copy-start.2 = (f32[64,64]{1,0:T(8,128)S(1)}, f32[64,64]{1,0:T(8,128)}, u32[]{:S(2)}) copy-start(f32[64,64]{1,0:T(8,128)} %constant.9.clone.refs_3_) | copy-start | bytes 49156
  6.4 22.9 %copy-start.3 = (s32[4,2]{0,1:T(2,128)S(1)}, s32[4,2]{0,1:T(2,128)}, u32[]{:S(2)}) copy-start(s32[4,2]{0,1:T(2,128)} %param.8) | copy-start | bytes 100
  6.4 13.5 %all-to-all-start = ((bf16[8,3,64,128]{3,2,1,0:T(8,128)(2,1)}), bf16[8,3,64,128]{3,2,1,0:T(8,128)(2,1)S(1)}, u32[]{:S(2)}, u32[]{:S(2)}) async-start(bf16[8,3,64,128]{3,2,1,0:T(8,128)(2,1)} %bitcast.4), calls=%async_computation | async-start | bytes 786432 | tf_op jit(solution)/shard_map/all_to_all | solution.py:513
  11.6 25.6 %collective-permute-start.4 = (bf16[4,3,256,128]{3,2,1,0:T(8,128)(2,1)}, bf16[4,3,256,128]{3,2,1,0:T(8,128)(2,1)S(1)}, u32[]{:S(2)}, u32[]{:S(2)}) collective-permute-start(bf16[4,3,256,128]{3,2,1,0:T(8,128)(2,1)} %get-tuple-element.13.first_sent), channel_id=1, source_target_pairs={{0,4},{4,0},{8,12},{12,8},{16,20},{20,16},{24,28},{28,24},{1,5},{5... | collective-permute-start | bytes 2359304 | tf_op jit(solution)/shard_map/ppermute | solution.py:511
  12.1 25.1 %collective-permute-start.5 = (bf16[4,3,256,128]{3,2,1,0:T(8,128)(2,1)}, bf16[4,3,256,128]{3,2,1,0:T(8,128)(2,1)S(1)}, u32[]{:S(2)}, u32[]{:S(2)}) collective-permute-start(bf16[4,3,256,128]{3,2,1,0:T(8,128)(2,1)} %get-tuple-element.14.second_sent), channel_id=1, source_target_pairs={{4,8},{12,16},{20,24},{8,4},{16,12},{24,20},{5,9},{13,17},{21,25},... | collective-permute-start | bytes 2359304 | tf_op jit(solution)/shard_map/ppermute | solution.py:512
  19.9 1.7 %collective-permute-start = (bf16[8,3,64,128]{3,2,1,0:T(8,128)(2,1)S(1)}, bf16[8,3,64,128]{3,2,1,0:T(8,128)(2,1)S(1)}, u32[]{:S(2)}, u32[]{:S(2)}) collective-permute-start(bf16[8,3,64,128]{3,2,1,0:T(8,128)(2,1)S(1)} %all-to-all-done.refs_0_), channel_id=1, source_target_pairs={{4,0},{0,4},{12,8},{8,12},{20,16},{16,20},{28,24},{24,28},{5,1},{1... | collective-permute-start | bytes 1179656 | tf_op jit(solution)/shard_map/ppermute | solution.py:517
  25.8 13.7 %all-to-all-start.1 = ((bf16[8,192,128]{2,1,0:T(8,128)(2,1)}), bf16[8,192,128]{2,1,0:T(8,128)(2,1)S(1)}, u32[]{:S(2)}, u32[]{:S(2)}) async-start(bf16[8,192,128]{2,1,0:T(8,128)(2,1)} %middle.1), calls=%async_computation.1 | async-start | bytes 786432 | tf_op jit(solution)/shard_map/all_to_all | solution.py:534
  29.3 5.6 %collective-permute-start.3 = (s32[2,4]{1,0:T(2,128)S(1)}, s32[2,4]{1,0:T(2,128)S(1)}, u32[]{:S(2)}, u32[]{:S(2)}) collective-permute-start(s32[2,4]{1,0:T(2,128)S(1)} %bitcast.6), channel_id=1, source_target_pairs={{3,0},{0,1},{1,2},{2,3},{7,4},{4,5},{5,6},{6,7},{11,8},{8,9},{9,10... | collective-permute-start | bytes 104 | tf_op jit(solution)/shard_map/ppermute | solution.py:533
  30.9 4.5 %collective-permute-start.2 = (s32[2,4]{1,0:T(2,128)S(1)}, s32[2,4]{1,0:T(2,128)S(1)}, u32[]{:S(2)}, u32[]{:S(2)}) collective-permute-start(s32[2,4]{1,0:T(2,128)S(1)} %bitcast.7), channel_id=1, source_target_pairs={{2,0},{3,1},{0,2},{1,3},{6,4},{7,5},{4,6},{5,7},{10,8},{11,9},{8,1... | collective-permute-start | bytes 104 | tf_op jit(solution)/shard_map/ppermute | solution.py:533
  33.5 3.6 %collective-permute-start.1 = (s32[2,4]{1,0:T(2,128)S(1)}, s32[2,4]{1,0:T(2,128)S(1)}, u32[]{:S(2)}, u32[]{:S(2)}) collective-permute-start(s32[2,4]{1,0:T(2,128)S(1)} %bitcast.8), channel_id=1, source_target_pairs={{1,0},{2,1},{3,2},{0,3},{5,4},{6,5},{7,6},{4,7},{9,8},{10,9},{11,1... | collective-permute-start | bytes 104 | tf_op jit(solution)/shard_map/ppermute | solution.py:533

commit v8 on v7

--- a/solution.py
+++ b/solution.py
@@ -207,7 +207,7 @@
         last_output(p).start()
         return carry
 
-    lax.fori_loop(0, pairs, one_pair, 0)
+    lax.fori_loop(0, pairs, one_pair, 0, unroll=2)
     for p in range(pairs):
         for copy in (*outputs(p), last_output(p)):
             copy.wait()

time: 54.7 us -> 54.6 us (level)
  no operation moved by 1% of the time
where the time goes in v8:
time: 54.6 us; the launch traced here: 54.2 us
  Pallas kernels  16.1 us (29%)
  starting transfers between devices  15.4 us (28%)
  waiting for transfers between devices  13.4 us (25%)
  blocking collectives  7.87 us (14%)
  between operations  0.74 us (1%)
  other arithmetic  0.59 us (1%)
    all_to_all x1, blocking collectives, shards(): return (potentials, jnp.sum(lax.all_to_all(panel, 'dom', 0, 0), axis=0))  7.87 us
    all_to_all x1, waiting for transfers between devices, shards(): lax.all_to_all(shares.reshape(slabs, 3, part_rows, lanes), 'dom', 0, 0)  7.13 us
    pallas_call x1, Pallas kernels, shards(): pl.pallas_call(final_kernel, in_specs=[anywhere] + [hbm] * 5 + [vmem] * 3...  6.32 us
    pallas_call x1, Pallas kernels, shards(): pl.pallas_call(source_kernel, in_specs=[hbm, hbm, hbm], out_specs=[hbm] *...  5.58 us
    ppermute x3, starting transfers between devices, shards(): lax.ppermute(late_ids, 'pair', perm)  5.56 us
    all_to_all x1, starting transfers between devices, shards(): lax.all_to_all(shares.reshape(slabs, 3, part_rows, lanes), 'dom', 0, 0)  5.19 us
    pallas_call x1, Pallas kernels, shards(): pl.pallas_call(middle_kernel, in_specs=[vmem] * (parts + 3), out_specs=vm...  4.2 us
    all_to_all x1, starting transfers between devices, shards(): returned = lax.all_to_all(smoothed, 'dom', 0, 0)  3.45 us
  transfers between devices with their start and end apart: 8, of which 5 were waited for; matrix products, arithmetic and copies ran while one was open for 0% of the time, Pallas kernels for 8%

profile of v8, /device:TPU:0, one launch (start us, length us, event | category | flops | bytes accessed | tf_op | source)
XLA Modules:
  0.0 54.2 jit_solution(7827102229143981939)
XLA Ops:
  0.6 0.0 copy-start
  0.6 0.0 copy-start.1
  0.7 0.0 copy-start.2
  0.7 5.6 %source.1 = (bf16[4,2,3,64,128]{4,3,2,1,0:T(8,128)(2,1)}, bf16[4,3,256,128]{3,2,1,0:T(8,128)(2,1)}, bf16[4,3,256,128]{3,2,1,0:T(8,128)(2,1)}, f32[4,4,256,128]{3,2,1,0:T(8,128)}) custom-call(s32[2,4]{1,0:T(2,128)} %bitcast.5, bf16[12,4,256,128]{3,2,1,0:T(8,128)(2,1)} %all_occ.1, bf16[12,4,256,128]{3,2,1,0:T(8,128)(2,1)} %all_vir.1), custom_call_target="tpu_custom_call" | custom-call | tf_op jit(solution)/shard_map/source/pallas_call | solution.py:477
  6.3 0.0 copy-start.3
  6.3 5.2 %all-to-all-start = ((bf16[8,3,64,128]{3,2,1,0:T(8,128)(2,1)}), bf16[8,3,64,128]{3,2,1,0:T(8,128)(2,1)S(1)}, u32[]{:S(2)}, u32[]{:S(2)}) async-start(bf16[8,3,64,128]{3,2,1,0:T(8,128)(2,1)} %bitcast.4), calls=%async_computation | async-start | bytes 786432 | tf_op jit(solution)/shard_map/all_to_all | solution.py:513
  11.5 0.5 collective-permute-start.4
  12.0 0.7 %collective-permute-start.5 = (bf16[4,3,256,128]{3,2,1,0:T(8,128)(2,1)}, bf16[4,3,256,128]{3,2,1,0:T(8,128)(2,1)S(1)}, u32[]{:S(2)}, u32[]{:S(2)}) collective-permute-start(bf16[4,3,256,128]{3,2,1,0:T(8,128)(2,1)} %get-tuple-element.14.second_sent), channel_id=1, source_target_pairs={{4,8},{12,16},{20,24},{8,4},{16,12},{24,20},{5,9},{13,17},{21,25},... | collective-permute-start | bytes 2359304 | tf_op jit(solution)/shard_map/ppermute | solution.py:512
  12.7 7.1 %all-to-all-done.refs_0_ = bf16[8,3,64,128]{3,2,1,0:T(8,128)(2,1)S(1)} async-done(((bf16[8,3,64,128]{3,2,1,0:T(8,128)(2,1)}), bf16[8,3,64,128]{3,2,1,0:T(8,128)(2,1)S(1)}, u32[]{:S(2)}, u32[]{:S(2)}) %all-to-all-start) | async-done | bytes 393248 | tf_op jit(solution)/shard_map/all_to_all | solution.py:513
  19.8 0.0 collective-permute-start
  19.8 1.7 %collective-permute-done.refs_1_ = bf16[8,3,64,128]{3,2,1,0:T(8,128)(2,1)S(1)} collective-permute-done((bf16[8,3,64,128]{3,2,1,0:T(8,128)(2,1)S(1)}, bf16[8,3,64,128]{3,2,1,0:T(8,128)(2,1)S(1)}, u32[]{:S(2)}, u32[]{:S(2)}) %collective-permute-start) | collective-permute-done | bytes 393248 | tf_op jit(solution)/shard_map/ppermute | solution.py:517
  21.5 0.0 copy-done
  21.5 0.0 copy-done.1
  21.5 0.0 copy-done.2
  21.5 4.2 %middle.1 = bf16[8,192,128]{2,1,0:T(8,128)(2,1)} custom-call(bf16[8,3,64,128]{3,2,1,0:T(8,128)(2,1)S(1)} %all-to-all-done.refs_0_, bf16[8,3,64,128]{3,2,1,0:T(8,128)(2,1)S(1)} %collective-permute-done.refs_1_, bf16[2,1024,256]{2,1,0:T(8,128)(2,1)S(1)} %copy-done, f32[64,64]{1,0:T(8,128)S(1)} %copy-done.2, f32[64,256]{1,0:T(8,128)S(1)} %copy-done.1), custom_call_target="tpu_custom_call" | custom-call | tf_op jit(solution)/shard_map/middle/pallas_call | solution.py:521
  25.7 3.5 %all-to-all-start.1 = ((bf16[8,192,128]{2,1,0:T(8,128)(2,1)}), bf16[8,192,128]{2,1,0:T(8,128)(2,1)S(1)}, u32[]{:S(2)}, u32[]{:S(2)}) async-start(bf16[8,192,128]{2,1,0:T(8,128)(2,1)} %middle.1), calls=%async_computation.1 | async-start | bytes 786432 | tf_op jit(solution)/shard_map/all_to_all | solution.py:534
  29.2 0.0 copy-done.3
  29.2 1.6 %collective-permute-start.3 = (s32[2,4]{1,0:T(2,128)S(1)}, s32[2,4]{1,0:T(2,128)S(1)}, u32[]{:S(2)}, u32[]{:S(2)}) collective-permute-start(s32[2,4]{1,0:T(2,128)S(1)} %bitcast.6), channel_id=1, source_target_pairs={{3,0},{0,1},{1,2},{2,3},{7,4},{4,5},{5,6},{6,7},{11,8},{8,9},{9,10... | collective-permute-start | bytes 104 | tf_op jit(solution)/shard_map/ppermute | solution.py:533
  30.8 2.6 %collective-permute-start.2 = (s32[2,4]{1,0:T(2,128)S(1)}, s32[2,4]{1,0:T(2,128)S(1)}, u32[]{:S(2)}, u32[]{:S(2)}) collective-permute-start(s32[2,4]{1,0:T(2,128)S(1)} %bitcast.7), channel_id=1, source_target_pairs={{2,0},{3,1},{0,2},{1,3},{6,4},{7,5},{4,6},{5,7},{10,8},{11,9},{8,1... | collective-permute-start | bytes 104 | tf_op jit(solution)/shard_map/ppermute | solution.py:533
  33.4 1.3 %collective-permute-start.1 = (s32[2,4]{1,0:T(2,128)S(1)}, s32[2,4]{1,0:T(2,128)S(1)}, u32[]{:S(2)}, u32[]{:S(2)}) collective-permute-start(s32[2,4]{1,0:T(2,128)S(1)} %bitcast.8), channel_id=1, source_target_pairs={{1,0},{2,1},{3,2},{0,3},{5,4},{6,5},{7,6},{4,7},{9,8},{10,9},{11,1... | collective-permute-start | bytes 104 | tf_op jit(solution)/shard_map/ppermute | solution.py:533
  34.8 0.0 collective-permute-done.3
  34.8 0.5 collective-permute-done.2
  35.3 1.7 %collective-permute-done.1 = s32[2,4]{1,0:T(2,128)S(1)} collective-permute-done((s32[2,4]{1,0:T(2,128)S(1)}, s32[2,4]{1,0:T(2,128)S(1)}, u32[]{:S(2)}, u32[]{:S(2)}) %collective-permute-start.1) | collective-permute-done | bytes 64 | tf_op jit(solution)/shard_map/ppermute | solution.py:533
  37.0 0.0 collective-permute-done.4.first
  37.0 0.0 collective-permute-done.5.second
  37.0 2.4 %all-to-all-done.1.coarse = bf16[8,192,128]{2,1,0:T(8,128)(2,1)S(1)} async-done(((bf16[8,192,128]{2,1,0:T(8,128)(2,1)}), bf16[8,192,128]{2,1,0:T(8,128)(2,1)S(1)}, u32[]{:S(2)}, u32[]{:S(2)}) %all-to-all-start.1) | async-done | bytes 393248 | tf_op jit(solution)/shard_map/all_to_all | solution.py:534
  39.4 6.3 %final.1 = (bf16[4,4,256,128]{3,2,1,0:T(8,128)(2,1)}, f32[2,8,4]{2,1,0:T(8,128)S(1)}) custom-call(s32[8,4]{1,0:T(8,128)S(1)} %pad_add_fusion.all_ids, bf16[12,4,256,128]{3,2,1,0:T(8,128)(2,1)} %all_occ.1, bf16[12,4,256,128]{3,2,1,0:T(8,128)(2,1)} %all_vir.1, f32[4,4,256,128]{3,2,1,0:T(8,128)} %get-tuple-element.12.v0_hbm, ...), custom_call_target="tpu_custom_call" | custom-call | tf_op jit(solution)/shard_map/final/pallas_call | solution.py:537
  45.7 7.9 %all_to_all.15 = f32[8,2,4]{2,1,0:T(2,128)S(1)} all-to-all(f32[8,2,4]{2,1,0:T(2,128)S(1)} %copy.8), channel_id=1, replica_groups=mesh['dom'=8,'pair'=4] {'dom'}, dimensions={0} | all-to-all | bytes 512 | tf_op jit(solution)/shard_map/all_to_all | solution.py:565
  53.6 0.6 %reduce_sum.9 = f32[2,4]{1,0:T(2,128)} reduce(f32[8,2,4]{2,1,0:T(2,128)S(1)} %all_to_all.15, f32[]{:T(128)} %constant.3.clone.1), dimensions={0}, to_apply=%region_0.0 | reduce | flops 56 | bytes 292 | tf_op jit(solution)/shard_map/reduce_sum | solution.py:565
  (2 shorter events, 0.0 us)
Async XLA Ops:
  0.6 20.9 %copy-start = (bf16[2,1024,256]{2,1,0:T(8,128)(2,1)S(1)}, bf16[2,1024,256]{2,1,0:T(8,128)(2,1)}, u32[]{:S(2)}) copy-start(bf16[2,1024,256]{2,1,0:T(8,128)(2,1)} %constant.8.clone.refs_2_) | copy-start | bytes 3145732
  0.6 20.9 %copy-start.1 = (f32[64,256]{1,0:T(8,128)S(1)}, f32[64,256]{1,0:T(8,128)}, u32[]{:S(2)}) copy-start(f32[64,256]{1,0:T(8,128)} %constant.10.clone.refs_4_) | copy-start | bytes 196612
  0.7 20.9 %copy-start.2 = (f32[64,64]{1,0:T(8,128)S(1)}, f32[64,64]{1,0:T(8,128)}, u32[]{:S(2)}) copy-start(f32[64,64]{1,0:T(8,128)} %constant.9.clone.refs_3_) | copy-start | bytes 49156
  6.3 22.9 %copy-start.3 = (s32[4,2]{0,1:T(2,128)S(1)}, s32[4,2]{0,1:T(2,128)}, u32[]{:S(2)}) copy-start(s32[4,2]{0,1:T(2,128)} %param.8) | copy-start | bytes 100
  6.3 13.5 %all-to-all-start = ((bf16[8,3,64,128]{3,2,1,0:T(8,128)(2,1)}), bf16[8,3,64,128]{3,2,1,0:T(8,128)(2,1)S(1)}, u32[]{:S(2)}, u32[]{:S(2)}) async-start(bf16[8,3,64,128]{3,2,1,0:T(8,128)(2,1)} %bitcast.4), calls=%async_computation | async-start | bytes 786432 | tf_op jit(solution)/shard_map/all_to_all | solution.py:513
  11.5 25.5 %collective-permute-start.4 = (bf16[4,3,256,128]{3,2,1,0:T(8,128)(2,1)}, bf16[4,3,256,128]{3,2,1,0:T(8,128)(2,1)S(1)}, u32[]{:S(2)}, u32[]{:S(2)}) collective-permute-start(bf16[4,3,256,128]{3,2,1,0:T(8,128)(2,1)} %get-tuple-element.13.first_sent), channel_id=1, source_target_pairs={{0,4},{4,0},{8,12},{12,8},{16,20},{20,16},{24,28},{28,24},{1,5},{5... | collective-permute-start | bytes 2359304 | tf_op jit(solution)/shard_map/ppermute | solution.py:511
  12.0 25.0 %collective-permute-start.5 = (bf16[4,3,256,128]{3,2,1,0:T(8,128)(2,1)}, bf16[4,3,256,128]{3,2,1,0:T(8,128)(2,1)S(1)}, u32[]{:S(2)}, u32[]{:S(2)}) collective-permute-start(bf16[4,3,256,128]{3,2,1,0:T(8,128)(2,1)} %get-tuple-element.14.second_sent), channel_id=1, source_target_pairs={{4,8},{12,16},{20,24},{8,4},{16,12},{24,20},{5,9},{13,17},{21,25},... | collective-permute-start | bytes 2359304 | tf_op jit(solution)/shard_map/ppermute | solution.py:512
  19.8 1.7 %collective-permute-start = (bf16[8,3,64,128]{3,2,1,0:T(8,128)(2,1)S(1)}, bf16[8,3,64,128]{3,2,1,0:T(8,128)(2,1)S(1)}, u32[]{:S(2)}, u32[]{:S(2)}) collective-permute-start(bf16[8,3,64,128]{3,2,1,0:T(8,128)(2,1)S(1)} %all-to-all-done.refs_0_), channel_id=1, source_target_pairs={{4,0},{0,4},{12,8},{8,12},{20,16},{16,20},{28,24},{24,28},{5,1},{1... | collective-permute-start | bytes 1179656 | tf_op jit(solution)/shard_map/ppermute | solution.py:517
  25.7 13.7 %all-to-all-start.1 = ((bf16[8,192,128]{2,1,0:T(8,128)(2,1)}), bf16[8,192,128]{2,1,0:T(8,128)(2,1)S(1)}, u32[]{:S(2)}, u32[]{:S(2)}) async-start(bf16[8,192,128]{2,1,0:T(8,128)(2,1)} %middle.1), calls=%async_computation.1 | async-start | bytes 786432 | tf_op jit(solution)/shard_map/all_to_all | solution.py:534
  29.2 5.6 %collective-permute-start.3 = (s32[2,4]{1,0:T(2,128)S(1)}, s32[2,4]{1,0:T(2,128)S(1)}, u32[]{:S(2)}, u32[]{:S(2)}) collective-permute-start(s32[2,4]{1,0:T(2,128)S(1)} %bitcast.6), channel_id=1, source_target_pairs={{3,0},{0,1},{1,2},{2,3},{7,4},{4,5},{5,6},{6,7},{11,8},{8,9},{9,10... | collective-permute-start | bytes 104 | tf_op jit(solution)/shard_map/ppermute | solution.py:533
  30.8 4.5 %collective-permute-start.2 = (s32[2,4]{1,0:T(2,128)S(1)}, s32[2,4]{1,0:T(2,128)S(1)}, u32[]{:S(2)}, u32[]{:S(2)}) collective-permute-start(s32[2,4]{1,0:T(2,128)S(1)} %bitcast.7), channel_id=1, source_target_pairs={{2,0},{3,1},{0,2},{1,3},{6,4},{7,5},{4,6},{5,7},{10,8},{11,9},{8,1... | collective-permute-start | bytes 104 | tf_op jit(solution)/shard_map/ppermute | solution.py:533
  33.4 3.6 %collective-permute-start.1 = (s32[2,4]{1,0:T(2,128)S(1)}, s32[2,4]{1,0:T(2,128)S(1)}, u32[]{:S(2)}, u32[]{:S(2)}) collective-permute-start(s32[2,4]{1,0:T(2,128)S(1)} %bitcast.8), channel_id=1, source_target_pairs={{1,0},{2,1},{3,2},{0,3},{5,4},{6,5},{7,6},{4,7},{9,8},{10,9},{11,1... | collective-permute-start | bytes 104 | tf_op jit(solution)/shard_map/ppermute | solution.py:533
